TPU v7x, 128 devices: a whole 4x4x4 slice. The times are simulated.
128 devices in a mesh: sx: 8 (over z, core), sy: 16 (over y, x).
Axes of the slice: x: 4, y: 4, z: 4, core: 2. Of those that a mesh axis runs over, the one named last changes fastest.
Arguments:
- features: bfloat16 [4096, 4096], P(('sx', 'sy')), may hold values from -8 to 8
- occupancy: int32 [4096, 64], P(('sx', 'sy')), may hold values 0 or 1
- adjacency: int32 [4096, 27], P(('sx', 'sy')), may hold values from -1 to 4095, as said below
- conv_one: bfloat16 [27, 64, 64], replicated, may hold values from -0.15625 to 0.15625
- conv_two: bfloat16 [27, 64, 64], replicated, may hold values from -0.15625 to 0.15625
- scale_one: float32 [64], replicated, may hold values from 0.5 to 1.5
- shift_one: float32 [64], replicated, may hold values from -2.5 to 2.5
- scale_two: float32 [64], replicated, may hold values from 0.5 to 1.5
- shift_two: float32 [64], replicated, may hold values from -2.5 to 2.5
- w_query: bfloat16 [64, 64], replicated, may hold values from -8 to 8
- w_key: bfloat16 [64, 64], replicated, may hold values from -0.75 to 0.75
- w_value: bfloat16 [64, 64], replicated, may hold values from -0.75 to 0.75
- w_out: bfloat16 [64, 64], replicated, may hold values from -0.75 to 0.75
Outputs:
- refined: bfloat16 [4096, 4096], P(('sx', 'sy'))
Inputs may be any that keep to these rules, and one draw needn't show every extreme that they name: `adjacency`: brick ids are (i * 16 + j) * 32 + local index for the device at sx index i and sy index j. The scene is a grid of brick cells; that device owns the cells with x in [i * 4, (i+1) * 4), y in [j * 4, (j+1) * 4) and z in [0, 4), and holds exactly 32 occupied ones in ascending cell order (x, y, z). Entry (ox+1)*9 + (oy+1)*3 + (oz+1) is the id of the occupied cell at that offset, -1 if it is empty or outside the grid; entry 13 is the brick itself.
All inputs are finite; a program needn't handle non-finite values. No bound on the sum of `occupancy` on one device may be relied on, other than what follows from the above.
Results may differ from a plain program's by a relative error of at most 0.011.
Values may be sent and summed in bfloat16 or wider, within the bound.
No kernel may reach another device: no remote copies, remote signals or barrier semaphores. Data moves between devices by JAX's collectives and lax.ppermute only.
A program may use at most 128 MiB of HBM per device.

v0:
```python
import math

import jax
import jax.numpy as jnp
from jax import lax
from jax.experimental import pallas as pl
from jax.experimental.pallas import tpu as pltpu
from jax.sharding import PartitionSpec as P

HEADS = 2
C = 64
COL = 4 * C
BRICKS = 32
EPSILON = 1e-05
FAR = -(1 << 20)
VMEM_LIMIT = 48 * 1024 * 1024
f32, bf16 = jnp.float32, jnp.bfloat16


def call(kernel, out_shape, args, scratch=(), flops=0, bytes_accessed=0):
    vmem = pl.BlockSpec(memory_space=pltpu.VMEM)
    return pl.pallas_call(
        kernel,
        out_shape=out_shape,
        in_specs=[vmem] * len(args),
        out_specs=jax.tree.map(lambda _: vmem, out_shape),
        scratch_shapes=list(scratch),
        compiler_params=pltpu.CompilerParams(vmem_limit_bytes=VMEM_LIMIT),
        cost_estimate=pl.CostEstimate(
            flops=flops, bytes_accessed=bytes_accessed, transcendentals=0
        ),
    )(*args)


def shape(*dims, dtype=bf16):
    return jax.ShapeDtypeStruct(dims, dtype)


def column(x, y):
    return slice((x * 4 + y) * COL, (x * 4 + y + 1) * COL)


def face_x(ref, x):
    return ref[:, x * 4 * COL : (x + 1) * 4 * COL]


def face_y(ref, y):
    return jnp.concatenate([ref[:, column(x, y)] for x in range(4)], axis=1)


def pick(flag, a, b):
    return jnp.where(flag, a, b)


def parities():
    even_x = lax.rem(lax.axis_index("sx"), 2) == 0
    even_y = lax.rem(lax.axis_index("sy"), 2) == 0
    return even_x, even_y


def pair_exchange(value, axis, phase):
    count = lax.axis_size(axis)
    if phase == 0:
        pairs = [(s, s ^ 1) for s in range(count)]
    else:
        pairs = [(s, ((s + 1) ^ 1) - 1) for s in range(1, count - 1)]
    return lax.ppermute(value, axis, pairs)


def send_faces(field, xs0, xs1, ys0, ys1):
    even_x, even_y = parities()
    low, high = face_x(field, 0), face_x(field, 3)
    xs0[...] = pick(even_x, high, low)
    xs1[...] = pick(even_x, low, high)
    low, high = face_y(field, 0), face_y(field, 3)
    ys0[...] = pick(even_y, high, low)
    ys1[...] = pick(even_y, low, high)


def prepare_kernel(
    feat, occ, w_q, w_k, w_v, masked, cover, queries, kv, xs0, xs1, ys0, ys1
):
    occupied = occ[...].astype(f32).astype(bf16)
    row = lax.broadcasted_iota(jnp.int32, (64, COL), 0)
    voxel = lax.shift_right_logical(lax.broadcasted_iota(jnp.int32, (64, COL), 1), 6)
    total = jnp.zeros((BRICKS, 128), f32)
    for k in range(16):
        spread = (row == voxel + 4 * k).astype(f32).astype(bf16)
        cov = jnp.dot(occupied, spread, preferred_element_type=f32).astype(bf16)
        part = feat[:, k * COL : (k + 1) * COL] * cov
        cover[:, k * COL : (k + 1) * COL] = cov
        masked[:, k * COL : (k + 1) * COL] = part
        wide = part.astype(f32)
        total = total + wide[:, :128] + wide[:, 128:]
    summed = total[:, :C] + total[:, C:]
    tokens = (summed / 8.0).astype(bf16)
    q = jnp.dot(tokens, w_q[...], preferred_element_type=f32)
    k = jnp.dot(tokens, w_k[...], preferred_element_type=f32)
    v = jnp.dot(tokens, w_v[...], preferred_element_type=f32)
    wide_q = jnp.concatenate([q, jnp.zeros_like(q)], axis=1)
    lane = lax.broadcasted_iota(jnp.int32, (BRICKS, 128), 1)
    per_head = [
        jnp.where(lax.shift_right_logical(lane, 5) == h, wide_q, 0.0) for h in range(HEADS)
    ]
    queries[...] = jnp.concatenate(per_head, axis=0).astype(bf16)
    both = jnp.concatenate([k, v], axis=1).astype(bf16)
    kv[...] = jnp.broadcast_to(both[None], kv.shape)
    send_faces(masked, xs0, xs1, ys0, ys1)


def band_kernel(weight, band):
    zero = jnp.zeros((C, C), bf16)
    for t in range(9):
        for r, z_in in enumerate((0, 1, 2, 3, 4, -1)):
            blocks = []
            for z_out in range(4):
                tap = z_in - z_out + 1
                blocks.append(weight[t * 3 + tap] if 0 <= tap < 3 else zero)
            band[t, r * C : (r + 1) * C, :] = jnp.concatenate(blocks, axis=1)


def corner_kernel(ys0, ys1, r0, r1, s0, s1):
    _, even_y = parities()
    for own, out, first in ((ys0, s0, even_y), (ys1, s1, jnp.logical_not(even_y))):
        out[:, : 4 * COL] = own[...]
        for k, ref in enumerate((r0, r1)):
            out[:, (4 + k) * COL : (5 + k) * COL] = pick(first, ref[:, 3 * COL :], ref[:, :COL])


def gather_neighbours(field, halo_x, halo_y, adj_ref, padded):
    even_x, even_y = parities()
    r0, r1 = halo_x
    t0, t1 = halo_y
    ids = jnp.where(adj_ref[...] < 0, FAR, adj_ref[...])
    base = (lax.axis_index("sx") * lax.axis_size("sy") + lax.axis_index("sy")) * BRICKS
    step = {-1: -lax.axis_size("sy") * BRICKS, 0: 0, 1: lax.axis_size("sy") * BRICKS}

    def from_x(ox, y):
        lanes = slice(y * COL, (y + 1) * COL)
        a, b = (r1, r0) if ox < 0 else (r0, r1)
        return pick(even_x, a[:, lanes], b[:, lanes])

    def from_y(oy, x):
        lanes = slice(x * COL, (x + 1) * COL)
        a, b = (t1, t0) if oy < 0 else (t0, t1)
        return pick(even_y, a[:, lanes], b[:, lanes])

    def from_corner(ox, oy):
        p, q = slice(4 * COL, 5 * COL), slice(5 * COL, 6 * COL)
        a, b = (t1, t0) if oy < 0 else (t0, t1)
        u, v = (q, p) if ox < 0 else (p, q)
        return pick(
            even_y, pick(even_x, a[:, u], a[:, v]), pick(even_x, b[:, u], b[:, v])
        )

    lane_low = lax.broadcasted_iota(jnp.int32, (BRICKS, 128), 1) < C
    for ox in (-1, 0, 1):
        for oy in (-1, 0, 1):
            sources = [(0, 0)]
            if ox:
                sources.append((ox, 0))
            if oy:
                sources.append((0, oy))
            if ox and oy:
                sources.append((ox, oy))
            lane = lax.broadcasted_iota(jnp.int32, (BRICKS, 32 * len(sources)), 1)
            candidate = base + jnp.bitwise_and(lane, 31)
            for k, (dx, dy) in enumerate(sources):
                if k:
                    slot = lax.shift_right_logical(lane, 5) == k
                    candidate = candidate + jnp.where(slot, step[dx] + dy * BRICKS, 0)
            select = []
            centre = ox == 0 and oy == 0
            for oz in (1, -1) if centre else (1, -1, 0):
                o = (ox + 1) * 9 + (oy + 1) * 3 + (oz + 1)
                select.append((ids[:, o : o + 1] == candidate).astype(f32).astype(bf16))
            select = jnp.concatenate(select, axis=0)
            x_in = {-1: (3,), 0: range(4), 1: (0,)}[ox]
            y_in = {-1: (3,), 0: range(4), 1: (0,)}[oy]
            for x in x_in:
                for y in y_in:
                    parts = [field[:, column(x, y)]]
                    if ox:
                        parts.append(from_x(ox, y))
                    if oy:
                        parts.append(from_y(oy, x))
                    if ox and oy:
                        parts.append(from_corner(ox, oy))
                    table = parts[0] if len(parts) == 1 else jnp.concatenate(parts, axis=0)
                    got = jnp.dot(select, table, preferred_element_type=f32).astype(bf16)
                    above, below = got[:BRICKS, :128], got[BRICKS : 2 * BRICKS, 128:]
                    core = parts[0] if centre else got[2 * BRICKS :]
                    px = {-1: 0, 0: 1 + x, 1: 5}[ox]
                    py = {-1: 0, 0: 1 + y, 1: 5}[oy]
                    padded[px, py, :, :COL] = core
                    padded[px, py, :, COL:] = jnp.where(lane_low, above, below)


def convolve(padded, band, acc):
    for t in range(9):
        i, j = t // 3, t % 3
        window = padded[i : i + 4, j : j + 4].reshape(16 * BRICKS, 6 * C)
        part = jnp.dot(window, band[t], preferred_element_type=f32)
        if t == 0:
            acc[...] = part
        else:
            acc[...] += part


def four(ref):
    return jnp.concatenate([ref[...]] * 4, axis=1)


def attention(queries, kv_ref, w_out):
    kv = kv_ref[...].reshape(-1, 2 * C)
    logits = lax.dot_general(
        queries[...], kv, (((1,), (1,)), ((), ())), preferred_element_type=f32
    ) * (1.0 / math.sqrt(C // HEADS))
    top = jnp.max(logits, axis=1, keepdims=True)
    weight = jnp.exp(logits - top)
    total = jnp.sum(weight, axis=1, keepdims=True)
    coarse = weight.astype(bf16)
    fine = (weight - coarse.astype(f32)).astype(bf16)
    mixed = jnp.dot(coarse, kv, preferred_element_type=f32)
    mixed = mixed + jnp.dot(fine, kv, preferred_element_type=f32)
    mixed = mixed / total
    lane = lax.broadcasted_iota(jnp.int32, (BRICKS, 2 * C), 1)
    context = jnp.where(lane < C + C // 2, mixed[:BRICKS], mixed[BRICKS:])
    context = jnp.where(lane < C, 0.0, context)
    mean = jnp.sum(context * context, axis=1, keepdims=True) / C
    attended = (context / jnp.sqrt(mean + EPSILON)).astype(bf16)
    return jnp.dot(attended[:, C:], four(w_out), preferred_element_type=f32)


def first_kernel(
    masked, r0, r1, t0, t1, adj, band, scale, shift, cover, queries, kv, w_out,
    hidden, xs0, xs1, ys0, ys1, padded, acc,
):
    gather_neighbours(masked, (r0, r1), (t0, t1), adj, padded)
    convolve(padded, band, acc)
    term = attention(queries, kv, w_out)
    gain, offset = four(scale), four(shift)
    for k in range(16):
        lanes = slice(k * COL, (k + 1) * COL)
        first = jnp.maximum(acc[k * BRICKS : (k + 1) * BRICKS] * gain + offset, 0.0)
        hidden[:, lanes] = ((first + term) * cover[:, lanes].astype(f32)).astype(bf16)
    send_faces(hidden, xs0, xs1, ys0, ys1)


def second_kernel(
    hidden, r0, r1, t0, t1, adj, band, scale, shift, cover, masked, refined, padded, acc
):
    gather_neighbours(hidden, (r0, r1), (t0, t1), adj, padded)
    convolve(padded, band, acc)
    gain, offset = four(scale), four(shift)
    for k in range(16):
        lanes = slice(k * COL, (k + 1) * COL)
        value = acc[k * BRICKS : (k + 1) * BRICKS] * gain + offset
        value = jnp.maximum(value + masked[:, lanes].astype(f32), 0.0)
        refined[:, lanes] = (value * cover[:, lanes].astype(f32)).astype(bf16)


def exchange_x(xs0, xs1):
    return pair_exchange(xs0, "sx", 0), pair_exchange(xs1, "sx", 1)


def exchange_y(ys0, ys1, r0, r1):
    s0, s1 = call(
        corner_kernel, [shape(BRICKS, 6 * COL)] * 2, (ys0, ys1, r0, r1)
    )
    return pair_exchange(s0, "sy", 0), pair_exchange(s1, "sy", 1)


def local(
    features, occupancy, adjacency, conv_one, conv_two, scale_one, shift_one,
    scale_two, shift_two, w_query, w_key, w_value, w_out,
):
    n_sy = lax.axis_size("sy")
    whole, face = shape(BRICKS, 64 * C), shape(BRICKS, 4 * COL)
    band_shape = shape(9, 6 * C, COL)
    scratch = (
        pltpu.VMEM((6, 6, BRICKS, 6 * C), bf16),
        pltpu.VMEM((16 * BRICKS, COL), f32),
    )
    conv_cost = dict(flops=2 * 512 * 3456 * 256, bytes_accessed=4 << 20)
    masked, cover, queries, kv, xs0, xs1, ys0, ys1 = call(
        prepare_kernel,
        [whole, whole, shape(HEADS * BRICKS, 2 * C), shape(n_sy, BRICKS, 2 * C)] + [face] * 4,
        (features, occupancy, w_query, w_key, w_value),
        bytes_accessed=2 << 20,
    )
    r0, r1 = exchange_x(xs0, xs1)
    kv = lax.all_to_all(kv, "sy", 0, 0)
    t0, t1 = exchange_y(ys0, ys1, r0, r1)
    band_one = call(band_kernel, band_shape, (conv_one,), bytes_accessed=3 << 20)
    band_two = call(band_kernel, band_shape, (conv_two,), bytes_accessed=3 << 20)
    rows = [v.reshape(1, C) for v in (scale_one, shift_one, scale_two, shift_two)]
    hidden, xs0, xs1, ys0, ys1 = call(
        first_kernel,
        [whole] + [face] * 4,
        (masked, r0, r1, t0, t1, adjacency, band_one, rows[0], rows[1], cover, queries, kv, w_out),
        scratch,
        **conv_cost,
    )
    r0, r1 = exchange_x(xs0, xs1)
    t0, t1 = exchange_y(ys0, ys1, r0, r1)
    return call(
        second_kernel,
        whole,
        (hidden, r0, r1, t0, t1, adjacency, band_two, rows[2], rows[3], cover, masked),
        scratch,
        **conv_cost,
    )


def solution(mesh):
    split = P(("sx", "sy"), None)
    return jax.shard_map(
        local,
        mesh=mesh,
        in_specs=(split,) * 3 + (P(),) * 10,
        out_specs=split,
        check_vma=False,
    )
```

profile of v0, /device:TPU:40, one launch (start us, length us, event | category | flops | bytes accessed | tf_op | source)
XLA Modules:
  0.0 45.9 jit_solution(5146230692034325153)
XLA Ops:
  0.0 0.0 copy-start.2
  0.0 0.9 %copy-done.2 = bf16[32,4096]{1,0:T(8,128)(2,1)S(1)} copy-done((bf16[32,4096]{1,0:T(8,128)(2,1)S(1)}, bf16[32,4096]{1,0:T(8,128)(2,1)}, u32[]{:S(2)}) %copy-start.2) | copy-done | bytes 262168
  1.0 0.0 copy-start.3
  1.0 0.7 %copy-done.3 = s32[32,64]{1,0:T(8,128)S(1)} copy-done((s32[32,64]{1,0:T(8,128)S(1)}, s32[32,64]{1,0:T(8,128)}, u32[]{:S(2)}) %copy-start.3) | copy-done | bytes 8216
  1.7 0.0 copy-start.4
  1.7 0.7 %copy-done.4 = bf16[64,64]{1,0:T(8,128)(2,1)S(1)} copy-done((bf16[64,64]{1,0:T(8,128)(2,1)S(1)}, bf16[64,64]{1,0:T(8,128)(2,1)}, u32[]{:S(2)}) %copy-start.4) | copy-done | bytes 8216
  2.4 0.0 copy-start.5
  2.4 0.7 %copy-done.5 = bf16[64,64]{1,0:T(8,128)(2,1)S(1)} copy-done((bf16[64,64]{1,0:T(8,128)(2,1)S(1)}, bf16[64,64]{1,0:T(8,128)(2,1)}, u32[]{:S(2)}) %copy-start.5) | copy-done | bytes 8216
  3.1 0.0 copy-start.6
  3.1 0.7 %copy-done.6 = bf16[64,64]{1,0:T(8,128)(2,1)S(1)} copy-done((bf16[64,64]{1,0:T(8,128)(2,1)S(1)}, bf16[64,64]{1,0:T(8,128)(2,1)}, u32[]{:S(2)}) %copy-start.6) | copy-done | bytes 8216
  3.8 0.0 copy-start.7
  3.8 0.0 copy-start.8
  3.8 0.0 copy-start.9
  3.8 1.2 %shard_map.127 = (bf16[32,4096]{1,0:T(8,128)(2,1)S(1)}, bf16[32,4096]{1,0:T(8,128)(2,1)S(1)}, bf16[64,128]{1,0:T(8,128)(2,1)S(1)}, bf16[16,32,128]{2,1,0:T(8,128...) custom-call(bf16[32,4096]{1,0:T(8,128)(2,1)S(1)} %copy-done.2, ...), custom_call_target="tpu_custom_call" | custom-call | bytes 2097152 | tf_op jit(solution)/shard_map/pallas_call | solution.py:22
  5.0 0.0 collective-permute-start
  5.0 2.1 %collective-permute-start.1 = (bf16[32,1024]{1,0:T(8,128)(2,1)S(1)}, bf16[32,1024]{1,0:T(8,128)(2,1)S(1)}, u32[]{:S(2)}, u32[]{:S(2)}) collective-permute-start(bf16[32,1024]{1,0:T(8,128)(2,1)S(1)} %get-tuple-element.24), channel_id=1, source_target_pairs={{16,32},{32,16},{48,64},{64,48},{80,96},{96,80},{17,33},{33,17},{4... | collective-permute-start | bytes 196616 | tf_op jit(solution)/shard_map/ppermute | solution.py:67
  7.1 7.4 %all-to-all-start = ((bf16[16,32,128]{2,1,0:T(8,128)(2,1)}), bf16[16,32,128]{2,1,0:T(8,128)(2,1)S(1)}, u32[]{:S(2)}, u32[]{:S(2)}) async-start(bf16[16,32,128]{2,1,0:T(8,128)(2,1)} %get-tuple-element.31), calls=%async_computation | async-start | bytes 262144 | tf_op jit(solution)/shard_map/all_to_all | solution.py:293
  14.5 0.0 collective-permute-done.r0
  14.5 0.0 collective-permute-done.1.r1
  14.6 1.5 %collective-permute-start.2 = (bf16[32,1536]{1,0:T(8,128)(2,1)S(1)}, bf16[32,1536]{1,0:T(8,128)(2,1)S(1)}, u32[]{:S(2)}, u32[]{:S(2)}) collective-permute-start(bf16[32,1536]{1,0:T(8,128)(2,1)S(1)} %get-tuple-element.27), channel_id=1, source_target_pairs={{0,1},{1,0},{2,3},{3,2},{4,5},{5,4},{6,7},{7,6},{8,9},{9,8},{10,11... | collective-permute-start | bytes 294920 | tf_op jit(solution)/shard_map/ppermute | solution.py:67
  16.1 4.0 %collective-permute-start.3 = (bf16[32,1536]{1,0:T(8,128)(2,1)S(1)}, bf16[32,1536]{1,0:T(8,128)(2,1)S(1)}, u32[]{:S(2)}, u32[]{:S(2)}) collective-permute-start(bf16[32,1536]{1,0:T(8,128)(2,1)S(1)} %get-tuple-element.28), channel_id=1, source_target_pairs={{1,2},{2,1},{3,4},{4,3},{5,6},{6,5},{7,8},{8,7},{9,10},{10,9},{11,... | collective-permute-start | bytes 294920 | tf_op jit(solution)/shard_map/ppermute | solution.py:67
  20.1 0.0 copy-start
  20.1 1.0 %copy-done = bf16[27,64,64]{2,1,0:T(8,128)(2,1)S(1)} copy-done((bf16[27,64,64]{2,1,0:T(8,128)(2,1)S(1)}, bf16[27,64,64]{2,1,0:T(8,128)(2,1)}, u32[]{:S(2)}) %copy-start) | copy-done | bytes 221208
  21.1 0.3 shard_map.129.band
  21.4 0.0 all-to-all-done.kv
  21.4 0.0 collective-permute-done.2.t0
  21.4 4.3 %collective-permute-done.3.t1 = bf16[32,1536]{1,0:T(8,128)(2,1)S(1)} collective-permute-done((bf16[32,1536]{1,0:T(8,128)(2,1)S(1)}, bf16[32,1536]{1,0:T(8,128)(2,1)S(1)}, u32[]{:S(2)}, u32[]{:S(2)}) %collective-permute-start.3) | collective-permute-done | bytes 98336 | tf_op jit(solution)/shard_map/ppermute | solution.py:67
  25.8 0.0 copy-done.7
  25.8 0.0 copy-done.8
  25.8 0.0 copy-done.9
  25.8 0.0 copy-done.10
  25.8 0.0 copy-start.1
  25.8 2.4 %shard_map.130 = (bf16[32,4096]{1,0:T(8,128)(2,1)S(1)}, bf16[32,1024]{1,0:T(8,128)(2,1)S(1)}, bf16[32,1024]{1,0:T(8,128)(2,1)S(1)}, bf16[32,1024]{1,0:T(8,128)(2,1)S(1)}, bf16[32,1024]{1,0:T(8,128)(2,1)S(1)}) custom-call(bf16[32,4096]{1,0:T(8,128)(2,1)S(1)} %get-tuple-element.22.masked, bf16[32,1024]{1,0:T(8,128)(2,1)S(1)} %collective-permute-done.r0, ...), custom_call_target="tpu_custom_call" | custom-call | flops 905969664 | bytes 4194304 | tf_op jit(solution)/shard_map/pallas_call | solution.py:22
  28.3 0.0 copy-start.11
  28.3 0.0 copy-start.12
  28.3 0.2 collective-permute-start.4
  28.5 1.9 %collective-permute-start.5 = (bf16[32,1024]{1,0:T(8,128)(2,1)S(1)}, bf16[32,1024]{1,0:T(8,128)(2,1)S(1)}, u32[]{:S(2)}, u32[]{:S(2)}) collective-permute-start(bf16[32,1024]{1,0:T(8,128)(2,1)S(1)} %get-tuple-element.34), channel_id=1, source_target_pairs={{16,32},{32,16},{48,64},{64,48},{80,96},{96,80},{17,33},{33,17},{4... | collective-permute-start | bytes 196616 | tf_op jit(solution)/shard_map/ppermute | solution.py:67
  30.4 0.0 collective-permute-done.4.r0
  30.4 3.6 %collective-permute-done.5.r1 = bf16[32,1024]{1,0:T(8,128)(2,1)S(1)} collective-permute-done((bf16[32,1024]{1,0:T(8,128)(2,1)S(1)}, bf16[32,1024]{1,0:T(8,128)(2,1)S(1)}, u32[]{:S(2)}, u32[]{:S(2)}) %collective-permute-start.5) | collective-permute-done | bytes 65568 | tf_op jit(solution)/shard_map/ppermute | solution.py:67
  34.1 0.1 collective-permute-start.6
  34.2 4.0 %collective-permute-start.7 = (bf16[32,1536]{1,0:T(8,128)(2,1)S(1)}, bf16[32,1536]{1,0:T(8,128)(2,1)S(1)}, u32[]{:S(2)}, u32[]{:S(2)}) collective-permute-start(bf16[32,1536]{1,0:T(8,128)(2,1)S(1)} %get-tuple-element.38), channel_id=1, source_target_pairs={{1,2},{2,1},{3,4},{4,3},{5,6},{6,5},{7,8},{8,7},{9,10},{10,9},{11,... | collective-permute-start | bytes 294920 | tf_op jit(solution)/shard_map/ppermute | solution.py:67
  38.1 0.0 copy-done.1
  38.1 0.3 shard_map.132.band
  38.5 0.8 %collective-permute-done.6.t0 = bf16[32,1536]{1,0:T(8,128)(2,1)S(1)} collective-permute-done((bf16[32,1536]{1,0:T(8,128)(2,1)S(1)}, bf16[32,1536]{1,0:T(8,128)(2,1)S(1)}, u32[]{:S(2)}, u32[]{:S(2)}) %collective-permute-start.6) | collective-permute-done | bytes 98336 | tf_op jit(solution)/shard_map/ppermute | solution.py:67
  39.3 4.0 %collective-permute-done.7.t1 = bf16[32,1536]{1,0:T(8,128)(2,1)S(1)} collective-permute-done((bf16[32,1536]{1,0:T(8,128)(2,1)S(1)}, bf16[32,1536]{1,0:T(8,128)(2,1)S(1)}, u32[]{:S(2)}, u32[]{:S(2)}) %collective-permute-start.7) | collective-permute-done | bytes 98336 | tf_op jit(solution)/shard_map/ppermute | solution.py:67
  43.3 0.0 copy-done.11
  43.3 0.0 copy-done.12
  43.3 2.6 %shard_map.133 = bf16[32,4096]{1,0:T(8,128)(2,1)} custom-call(bf16[32,4096]{1,0:T(8,128)(2,1)S(1)} %get-tuple-element.32.hidden, bf16[32,1024]{1,0:T(8,128)(2,1)S(1)} %collective-permute-done.4.r0, bf16[32,1024]{1,0:T(8,128)(2,1)S(1)} %collective-permute-done.5.r1, bf16[32,1536]{1,0:T(8,128)(2,1)S(1)} %collective-permute-done.6.t0, ...), custom_call_target="tpu_custom_call" | custom-call | flops 905969664 | bytes 4194304 | tf_op jit(solution)/shard_map/pallas_call | solution.py:22
  (3 shorter events, 0.0 us)
Async XLA Ops:
  0.0 0.9 %copy-start.2 = (bf16[32,4096]{1,0:T(8,128)(2,1)S(1)}, bf16[32,4096]{1,0:T(8,128)(2,1)}, u32[]{:S(2)}) copy-start(bf16[32,4096]{1,0:T(8,128)(2,1)} %feat.1) | copy-start | bytes 786436
  1.0 0.7 %copy-start.3 = (s32[32,64]{1,0:T(8,128)S(1)}, s32[32,64]{1,0:T(8,128)}, u32[]{:S(2)}) copy-start(s32[32,64]{1,0:T(8,128)} %occ.1) | copy-start | bytes 24580
  1.7 0.7 %copy-start.4 = (bf16[64,64]{1,0:T(8,128)(2,1)S(1)}, bf16[64,64]{1,0:T(8,128)(2,1)}, u32[]{:S(2)}) copy-start(bf16[64,64]{1,0:T(8,128)(2,1)} %w_q.1) | copy-start | bytes 24580
  2.4 0.7 %copy-start.5 = (bf16[64,64]{1,0:T(8,128)(2,1)S(1)}, bf16[64,64]{1,0:T(8,128)(2,1)}, u32[]{:S(2)}) copy-start(bf16[64,64]{1,0:T(8,128)(2,1)} %w_k.1) | copy-start | bytes 24580
  3.1 0.7 %copy-start.6 = (bf16[64,64]{1,0:T(8,128)(2,1)S(1)}, bf16[64,64]{1,0:T(8,128)(2,1)}, u32[]{:S(2)}) copy-start(bf16[64,64]{1,0:T(8,128)(2,1)} %w_v.1) | copy-start | bytes 24580
  3.8 22.0 %copy-start.7 = (bf16[64,64]{1,0:T(8,128)(2,1)S(1)}, bf16[64,64]{1,0:T(8,128)(2,1)}, u32[]{:S(2)}) copy-start(bf16[64,64]{1,0:T(8,128)(2,1)} %w_out.1) | copy-start | bytes 24580
  3.8 22.0 %copy-start.8 = (s32[32,27]{1,0:T(8,128)S(1)}, s32[32,27]{1,0:T(8,128)}, u32[]{:S(2)}) copy-start(s32[32,27]{1,0:T(8,128)} %adj.3) | copy-start | bytes 10372
  3.8 22.0 %copy-start.9 = (f32[64]{0:T(128)S(1)}, f32[64]{0:T(128)}, u32[]{:S(2)}) copy-start(f32[64]{0:T(128)} %param.18) | copy-start | bytes 772
  3.8 22.0 %copy-start.10 = (f32[64]{0:T(128)S(1)}, f32[64]{0:T(128)}, u32[]{:S(2)}) copy-start(f32[64]{0:T(128)} %param.19) | copy-start | bytes 772
  5.0 9.5 %collective-permute-start = (bf16[32,1024]{1,0:T(8,128)(2,1)S(1)}, bf16[32,1024]{1,0:T(8,128)(2,1)S(1)}, u32[]{:S(2)}, u32[]{:S(2)}) collective-permute-start(bf16[32,1024]{1,0:T(8,128)(2,1)S(1)} %get-tuple-element.23), channel_id=1, source_target_pairs={{0,16},{16,0},{32,48},{48,32},{64,80},{80,64},{96,112},{112,96},{1... | collective-permute-start | bytes 196616 | tf_op jit(solution)/shard_map/ppermute | solution.py:67
  5.0 9.5 %collective-permute-start.1 = (bf16[32,1024]{1,0:T(8,128)(2,1)S(1)}, bf16[32,1024]{1,0:T(8,128)(2,1)S(1)}, u32[]{:S(2)}, u32[]{:S(2)}) collective-permute-start(bf16[32,1024]{1,0:T(8,128)(2,1)S(1)} %get-tuple-element.24), channel_id=1, source_target_pairs={{16,32},{32,16},{48,64},{64,48},{80,96},{96,80},{17,33},{33,17},{4... | collective-permute-start | bytes 196616 | tf_op jit(solution)/shard_map/ppermute | solution.py:67
  7.1 14.3 %all-to-all-start = ((bf16[16,32,128]{2,1,0:T(8,128)(2,1)}), bf16[16,32,128]{2,1,0:T(8,128)(2,1)S(1)}, u32[]{:S(2)}, u32[]{:S(2)}) async-start(bf16[16,32,128]{2,1,0:T(8,128)(2,1)} %get-tuple-element.31), calls=%async_computation | async-start | bytes 262144 | tf_op jit(solution)/shard_map/all_to_all | solution.py:293
  14.6 6.8 %collective-permute-start.2 = (bf16[32,1536]{1,0:T(8,128)(2,1)S(1)}, bf16[32,1536]{1,0:T(8,128)(2,1)S(1)}, u32[]{:S(2)}, u32[]{:S(2)}) collective-permute-start(bf16[32,1536]{1,0:T(8,128)(2,1)S(1)} %get-tuple-element.27), channel_id=1, source_target_pairs={{0,1},{1,0},{2,3},{3,2},{4,5},{5,4},{6,7},{7,6},{8,9},{9,8},{10,11... | collective-permute-start | bytes 294920 | tf_op jit(solution)/shard_map/ppermute | solution.py:67
  16.1 9.7 %collective-permute-start.3 = (bf16[32,1536]{1,0:T(8,128)(2,1)S(1)}, bf16[32,1536]{1,0:T(8,128)(2,1)S(1)}, u32[]{:S(2)}, u32[]{:S(2)}) collective-permute-start(bf16[32,1536]{1,0:T(8,128)(2,1)S(1)} %get-tuple-element.28), channel_id=1, source_target_pairs={{1,2},{2,1},{3,4},{4,3},{5,6},{6,5},{7,8},{8,7},{9,10},{10,9},{11,... | collective-permute-start | bytes 294920 | tf_op jit(solution)/shard_map/ppermute | solution.py:67
  20.1 1.0 %copy-start = (bf16[27,64,64]{2,1,0:T(8,128)(2,1)S(1)}, bf16[27,64,64]{2,1,0:T(8,128)(2,1)}, u32[]{:S(2)}) copy-start(bf16[27,64,64]{2,1,0:T(8,128)(2,1)} %weight.2) | copy-start | bytes 663556
  25.8 12.3 %copy-start.1 = (bf16[27,64,64]{2,1,0:T(8,128)(2,1)S(1)}, bf16[27,64,64]{2,1,0:T(8,128)(2,1)}, u32[]{:S(2)}) copy-start(bf16[27,64,64]{2,1,0:T(8,128)(2,1)} %weight.3) | copy-start | bytes 663556
  28.3 15.0 %copy-start.11 = (f32[64]{0:T(128)S(1)}, f32[64]{0:T(128)}, u32[]{:S(2)}) copy-start(f32[64]{0:T(128)} %param.20) | copy-start | bytes 772
  28.3 15.0 %copy-start.12 = (f32[64]{0:T(128)S(1)}, f32[64]{0:T(128)}, u32[]{:S(2)}) copy-start(f32[64]{0:T(128)} %param.21) | copy-start | bytes 772
  28.3 2.1 %collective-permute-start.4 = (bf16[32,1024]{1,0:T(8,128)(2,1)S(1)}, bf16[32,1024]{1,0:T(8,128)(2,1)S(1)}, u32[]{:S(2)}, u32[]{:S(2)}) collective-permute-start(bf16[32,1024]{1,0:T(8,128)(2,1)S(1)} %get-tuple-element.33), channel_id=1, source_target_pairs={{0,16},{16,0},{32,48},{48,32},{64,80},{80,64},{96,112},{112,96},{1... | collective-permute-start | bytes 196616 | tf_op jit(solution)/shard_map/ppermute | solution.py:67
  28.5 5.6 %collective-permute-start.5 = (bf16[32,1024]{1,0:T(8,128)(2,1)S(1)}, bf16[32,1024]{1,0:T(8,128)(2,1)S(1)}, u32[]{:S(2)}, u32[]{:S(2)}) collective-permute-start(bf16[32,1024]{1,0:T(8,128)(2,1)S(1)} %get-tuple-element.34), channel_id=1, source_target_pairs={{16,32},{32,16},{48,64},{64,48},{80,96},{96,80},{17,33},{33,17},{4... | collective-permute-start | bytes 196616 | tf_op jit(solution)/shard_map/ppermute | solution.py:67
  34.1 5.2 %collective-permute-start.6 = (bf16[32,1536]{1,0:T(8,128)(2,1)S(1)}, bf16[32,1536]{1,0:T(8,128)(2,1)S(1)}, u32[]{:S(2)}, u32[]{:S(2)}) collective-permute-start(bf16[32,1536]{1,0:T(8,128)(2,1)S(1)} %get-tuple-element.37), channel_id=1, source_target_pairs={{0,1},{1,0},{2,3},{3,2},{4,5},{5,4},{6,7},{7,6},{8,9},{9,8},{10,11... | collective-permute-start | bytes 294920 | tf_op jit(solution)/shard_map/ppermute | solution.py:67
  34.2 9.1 %collective-permute-start.7 = (bf16[32,1536]{1,0:T(8,128)(2,1)S(1)}, bf16[32,1536]{1,0:T(8,128)(2,1)S(1)}, u32[]{:S(2)}, u32[]{:S(2)}) collective-permute-start(bf16[32,1536]{1,0:T(8,128)(2,1)S(1)} %get-tuple-element.38), channel_id=1, source_target_pairs={{1,2},{2,1},{3,4},{4,3},{5,6},{6,5},{7,8},{8,7},{9,10},{10,9},{11,... | collective-permute-start | bytes 294920 | tf_op jit(solution)/shard_map/ppermute | solution.py:67
where the time goes:
time: 46.5 us; the launch traced here: 45.9 us
  starting transfers between devices  21.2 us (46%)
  waiting for transfers between devices  12.8 us (28%)
  Pallas kernels  6.81 us (15%)
  local copies, waits for them, and re-layouts  4.86 us (10%)
    ppermute x8, starting transfers between devices, pair_exchange(): return lax.ppermute(value, axis, pairs)  13.8 us
    ppermute x8, waiting for transfers between devices, pair_exchange(): return lax.ppermute(value, axis, pairs)  12.8 us
    all_to_all x1, starting transfers between devices, local(): kv = lax.all_to_all(kv, 'sy', 0, 0)  7.41 us
    pallas_call x7, Pallas kernels, call(): pl.pallas_call(kernel, out_shape=out_shape, in_specs=[vmem] * len(args),...  6.81 us
    unnamed x26, local copies, waits for them, and re-layouts  4.86 us
  transfers between devices with their start and end apart: 9, of which 4 were waited for; matrix products, arithmetic and copies ran while one was open for 0% of the time, Pallas kernels for 1%

commit v1 on v0

v1 whole, which is shorter than its diff:
```python
import math

import jax
import jax.numpy as jnp
from jax import lax
from jax.experimental import pallas as pl
from jax.experimental.pallas import tpu as pltpu
from jax.sharding import PartitionSpec as P

HEADS = 2
C = 64
COL = 4 * C
BRICKS = 32
EPSILON = 1e-05
FAR = -(1 << 20)
VMEM_LIMIT = 16 * 1024 * 1024
f32, bf16 = jnp.float32, jnp.bfloat16


def call(kernel, out_shape, args, scratch=(), flops=0, bytes_accessed=0):
    vmem = pl.BlockSpec(memory_space=pltpu.VMEM)
    return pl.pallas_call(
        kernel,
        out_shape=out_shape,
        in_specs=[vmem] * len(args),
        out_specs=jax.tree.map(lambda _: vmem, out_shape),
        scratch_shapes=list(scratch),
        compiler_params=pltpu.CompilerParams(vmem_limit_bytes=VMEM_LIMIT),
        cost_estimate=pl.CostEstimate(
            flops=flops, bytes_accessed=bytes_accessed, transcendentals=0
        ),
    )(*args)


def shape(*dims, dtype=bf16):
    return jax.ShapeDtypeStruct(dims, dtype)


def column(x, y):
    return slice((x * 4 + y) * COL, (x * 4 + y + 1) * COL)


def face_x(ref, x):
    return ref[:, x * 4 * COL : (x + 1) * 4 * COL]


def pick(flag, a, b):
    return jnp.where(flag, a, b)


def parities():
    even_x = lax.rem(lax.axis_index("sx"), 2) == 0
    even_y = lax.rem(lax.axis_index("sy"), 2) == 0
    return even_x, even_y


def pair_exchange(value, axis, phase):
    count = lax.axis_size(axis)
    if phase == 0:
        pairs = [(s, s ^ 1) for s in range(count)]
    else:
        pairs = [(s, (((s + 1) ^ 1) - 1) % count) for s in range(count)]
    return lax.ppermute(value, axis, pairs)


def device_base():
    return (lax.axis_index("sx") * lax.axis_size("sy") + lax.axis_index("sy")) * BRICKS


def id_step(dx, dy):
    return (dx * lax.axis_size("sy") + dy) * BRICKS


def one_hot(ids, offsets, bases):
    lane = lax.broadcasted_iota(jnp.int32, (BRICKS, 32 * len(bases)), 1)
    candidate = jnp.bitwise_and(lane, 31) + bases[0]
    for k in range(1, len(bases)):
        slot = lax.shift_right_logical(lane, 5) == k
        candidate = candidate + jnp.where(slot, bases[k] - bases[0], 0)
    rows = [
        (ids[:, o : o + 1] == candidate).astype(f32).astype(bf16)
        for o in ((ox + 1) * 9 + (oy + 1) * 3 + (oz + 1) for ox, oy, oz in offsets)
    ]
    return jnp.concatenate(rows, axis=0)


def put_column(select, parts, core, store):
    table = parts[0] if len(parts) == 1 else jnp.concatenate(parts, axis=0)
    got = jnp.dot(select, table, preferred_element_type=f32).astype(bf16)
    lane_low = lax.broadcasted_iota(jnp.int32, (BRICKS, 128), 1) < C
    ends = jnp.where(lane_low, got[:BRICKS, :128], got[BRICKS : 2 * BRICKS, 128:])
    store(got[2 * BRICKS :] if core is None else core, ends)


NEAR, BEHIND, META, Y_LANES = 0, 4 * COL, 8 * COL, 9 * COL


def prepare_kernel(feat, marks, masked, cover, tokens_all, meta, ids, s0, s1):
    occupied = marks[:, :C].astype(f32).astype(bf16)
    row = lax.broadcasted_iota(jnp.int32, (64, COL), 0)
    voxel = lax.shift_right_logical(lax.broadcasted_iota(jnp.int32, (64, COL), 1), 6)
    total = jnp.zeros((BRICKS, 128), f32)
    for k in range(16):
        lanes = slice(k * COL, (k + 1) * COL)
        spread = (row == voxel + 4 * k).astype(f32).astype(bf16)
        cov = jnp.dot(occupied, spread, preferred_element_type=f32).astype(bf16)
        part = feat[:, lanes] * cov
        cover[:, lanes] = cov
        masked[:, lanes] = part
        wide = part.astype(f32)
        total = total + wide[:, :128] + wide[:, 128:]
    summed = total[:, :C] + total[:, C:]
    tokens = (summed / 8.0).astype(bf16)
    half = BRICKS // 2
    packed = jnp.concatenate([tokens[:half], tokens[half:]], axis=1)
    tokens_all[...] = jnp.broadcast_to(packed[None], tokens_all.shape)
    number = marks[:, C : C + 27]
    ids[...] = jnp.where(number < 0, FAR, number)
    number = number + 1
    high = lax.shift_right_logical(number, 6).astype(f32).astype(bf16)
    low = jnp.bitwise_and(number, 63).astype(f32).astype(bf16)
    gap = jnp.zeros((BRICKS, C - 27), bf16)
    about = jnp.concatenate([high, gap, low, gap, occupied, tokens], axis=1)
    meta[...] = about
    _, even_y = parities()

    def write(out, near, behind):
        for place, y in ((NEAR, near), (BEHIND, behind)):
            for x in range(4):
                out[:, place + x * COL : place + (x + 1) * COL] = masked[:, column(x, y)]
        out[:, META:] = about

    @pl.when(even_y)
    def _():
        write(s0, 3, 2)
        write(s1, 0, 1)

    @pl.when(jnp.logical_not(even_y))
    def _():
        write(s0, 0, 1)
        write(s1, 3, 2)


def band_kernel(weight, band):
    zero = jnp.zeros((C, C), bf16)
    for t in range(9):
        for r, z_in in enumerate((0, 1, 2, 3, 4, -1)):
            blocks = []
            for z_out in range(4):
                tap = z_in - z_out + 1
                blocks.append(weight[t * 3 + tap] if 0 <= tap < 3 else zero)
            band[t, r * C : (r + 1) * C, :] = jnp.concatenate(blocks, axis=1)


def message_kernel(masked, t0, t1, x0, x1):
    even_x, even_y = parities()

    def write(out, x):
        out[:, : 4 * COL] = face_x(masked, x)
        place = 4 * COL
        for a, b in ((t1, t0), (t0, t1)):
            for plane in (NEAR, BEHIND):
                lanes = slice(plane + x * COL, plane + (x + 1) * COL)
                out[:, place : place + COL] = pick(even_y, a[:, lanes], b[:, lanes])
                place += COL

    @pl.when(even_x)
    def _():
        write(x0, 3)
        write(x1, 0)

    @pl.when(jnp.logical_not(even_x))
    def _():
        write(x0, 0)
        write(x1, 3)


def place_x(ox, x, whole):
    return {-1: 0, 0: 1 + x, 1: 5}[ox] if whole else {-1: 0, 0: x, 1: 1}[ox]


def gather_own(field, from_x, from_y, from_corner, ids, padded, x_offsets):
    whole = len(x_offsets) == 3
    base = device_base()
    for ox in x_offsets:
        for oy in (-1, 0, 1):
            sources = [(0, 0)]
            if ox:
                sources.append((ox, 0))
            if oy:
                sources.append((0, oy))
            if ox and oy:
                sources.append((ox, oy))
            centre = ox == 0 and oy == 0
            offsets = [(ox, oy, oz) for oz in ((1, -1) if centre else (1, -1, 0))]
            select = one_hot(ids, offsets, [base + id_step(dx, dy) for dx, dy in sources])
            for x in {-1: (3,), 0: range(4), 1: (0,)}[ox]:
                for y in {-1: (3,), 0: range(4), 1: (0,)}[oy]:
                    parts = [field[:, column(x, y)]]
                    if ox:
                        parts.append(from_x(ox, y))
                    if oy:
                        parts.append(from_y(oy, x))
                    if ox and oy:
                        parts.append(from_corner(ox, oy))
                    px = place_x(ox, x, whole)
                    py = {-1: 0, 0: 1 + y, 1: 5}[oy]

                    def store(core, ends, px=px, py=py):
                        padded[px, py, :, :COL] = core
                        padded[px, py, :, COL:] = ends

                    put_column(select, parts, parts[0] if centre else None, store)


def gather_side(field, from_x, from_message, side, ids, padded, x_offsets):
    here, there = device_base(), device_base() + id_step(0, side)
    mine = {-1: 0, 1: 3}[side]
    rows = slice(0, BRICKS) if side < 0 else slice(BRICKS, 2 * BRICKS)
    for ox in x_offsets:
        x_range = {-1: (3,), 0: range(4), 1: (0,)}[ox]
        outer = [here] if ox == 0 else [here, here + id_step(ox, 0)]
        inner = [there] if ox == 0 else [there, there + id_step(ox, 0)]
        offsets = [(ox, 0, oz) for oz in ((1, -1) if ox == 0 else (1, -1, 0))]
        select_inner = one_hot(ids, offsets, inner)
        select_outer = one_hot(ids, [(ox, -side, oz) for oz in (1, -1, 0)], outer)
        for x in x_range:
            px = place_x(ox, x, len(x_offsets) == 3)
            for place, py in ((BEHIND, 1 + side), (NEAR, 1), (None, 1 - side)):

                def store(core, ends, px=px, py=py):
                    padded[py, px, rows, :COL] = core
                    padded[py, px, rows, COL:] = ends

                if place is None:
                    parts = [field[:, column(x, mine)]]
                    if ox:
                        parts.append(from_x(ox, mine))
                    put_column(select_outer, parts, None, store)
                    continue
                parts = [from_message(side, place + x * COL)]
                if ox:
                    parts.append(from_x(ox, corner_place(side, place)))
                put_column(select_inner, parts, parts[0] if ox == 0 else None, store)


def corner_place(side, plane):
    return 4 + (0 if side < 0 else 2) + (0 if plane == NEAR else 1)


def window(padded, padded_side, i, j, x_range):
    rows = len(x_range)
    first = x_range[0] + i
    own = padded[first : first + rows, j : j + 4].reshape(rows * 4 * BRICKS, 6 * C)
    if padded_side is None:
        return own
    side = padded_side[j, first : first + rows].reshape(rows * 2 * BRICKS, 6 * C)
    return jnp.concatenate([own, side], axis=0)


def own_rows(x_range):
    return slice(x_range[0] * 4 * BRICKS, (x_range[0] + len(x_range)) * 4 * BRICKS)


def convolve(padded, band, acc, padded_side):
    for t in range(9):
        lhs = window(padded, padded_side, t // 3, t % 3, range(4))
        part = jnp.dot(lhs, band[t], preferred_element_type=f32)
        if t == 0:
            acc[...] = part
        else:
            acc[...] += part


def convolve_inner(padded, band, acc):
    for t in (3, 4, 5, 0, 1, 2, 6, 7, 8):
        i, j = t // 3, t % 3
        x_range = {0: range(1, 4), 1: range(4), 2: range(3)}[i]
        part = jnp.dot(
            window(padded, None, i - 1, j, x_range), band[t], preferred_element_type=f32
        )
        if t == 3:
            acc[...] = part
        else:
            acc[own_rows(x_range)] += part


def convolve_edges(padded, band, acc):
    for i, place, x in ((0, 0, 0), (2, 1, 3)):
        total = acc[own_rows(range(x, x + 1))]
        for j in range(3):
            lhs = window(padded, None, place, j, range(1))
            total = total + jnp.dot(lhs, band[i * 3 + j], preferred_element_type=f32)
        acc[own_rows(range(x, x + 1))] = total


def four(ref):
    return jnp.concatenate([ref[...]] * 4, axis=1)


def project(tokens, weight):
    return jnp.dot(tokens, weight, preferred_element_type=f32).astype(bf16)


def attention(tokens, packed, weights):
    group = jnp.concatenate([packed[:, :C], packed[:, C:]], axis=0)
    kv = project(group, weights[:, : 2 * C])
    queries = project(tokens, weights[:, 2 * C : 3 * C])
    rows = queries.shape[0]
    wide = jnp.concatenate([queries, jnp.zeros_like(queries)], axis=1).astype(f32)
    lane = lax.broadcasted_iota(jnp.int32, (rows, 2 * C), 1)
    per_head = [jnp.where(lax.shift_right_logical(lane, 5) == h, wide, 0.0) for h in range(HEADS)]
    wide = jnp.concatenate(per_head, axis=0).astype(bf16)
    logits = lax.dot_general(
        wide, kv, (((1,), (1,)), ((), ())), preferred_element_type=f32
    ) * (1.0 / math.sqrt(C // HEADS))
    top = jnp.max(logits, axis=1, keepdims=True)
    weight = jnp.exp(logits - top)
    total = jnp.sum(weight, axis=1, keepdims=True)
    coarse = weight.astype(bf16)
    fine = (weight - coarse.astype(f32)).astype(bf16)
    mixed = jnp.dot(coarse, kv, preferred_element_type=f32)
    mixed = mixed + jnp.dot(fine, kv, preferred_element_type=f32)
    mixed = mixed / total
    context = jnp.where(lane < C + C // 2, mixed[:rows], mixed[rows:])
    context = jnp.where(lane < C, 0.0, context)
    mean = jnp.sum(context * context, axis=1, keepdims=True) / C
    attended = (context / jnp.sqrt(mean + EPSILON)).astype(bf16)
    w_out = jnp.concatenate([weights[:, 3 * C :]] * 4, axis=1)
    return jnp.dot(attended[:, C:], w_out, preferred_element_type=f32)


def y_reader(t0, t1):
    _, even_y = parities()

    def from_y(oy, place, width=COL):
        lanes = slice(place, place + width)
        a, b = (t1, t0) if oy < 0 else (t0, t1)
        return pick(even_y, a[:, lanes], b[:, lanes])

    return from_y


def x_reader(r0, r1):
    even_x, _ = parities()

    def from_x(ox, k):
        lanes = slice(k * COL, (k + 1) * COL)
        a, b = (r1, r0) if ox < 0 else (r0, r1)
        return pick(even_x, a[:, lanes], b[:, lanes])

    return from_x


def side_ids(about):
    high, low = about[:, :C].astype(f32), about[:, C : 2 * C].astype(f32)
    number = (high * 64.0 + low).astype(jnp.int32) - 1
    return jnp.where(number < 0, FAR, number)


def attention_kernel(group, weights, term):
    count = group.shape[0]
    here = lax.axis_index("sy")
    tokens = []
    for step in (0, count - 1, 1):
        packed = group[lax.rem(here + step, count)]
        tokens += [packed[:, :C], packed[:, C:]]
    packed = group[...].reshape(-1, 2 * C)
    term[...] = attention(jnp.concatenate(tokens, axis=0), packed, weights)


def first_kernel(
    masked, r0, r1, t0, t1, ids, band, scale, shift, cover, term,
    hidden, low_side, high_side, xs0, xs1, padded, padded_side, acc,
):
    even_x, _ = parities()
    from_message, from_x = y_reader(t0, t1), x_reader(r0, r1)
    every = (-1, 0, 1)
    row = lax.broadcasted_iota(jnp.int32, (64, COL), 0)
    voxel = lax.shift_right_logical(lax.broadcasted_iota(jnp.int32, (64, COL), 1), 6)
    side_cover = []
    gather_own(
        masked,
        from_x,
        lambda oy, x: from_message(oy, NEAR + x * COL),
        lambda ox, oy: from_x(ox, corner_place(oy, NEAR)),
        ids[...],
        padded,
        every,
    )
    for side in (-1, 1):
        about = from_message(side, META)
        gather_side(masked, from_x, from_message, side, side_ids(about), padded_side, every)
        occupied = about[:, 2 * C : 3 * C]
        y = 3 if side < 0 else 0
        for x in range(4):
            spread = (row == voxel + (x * 16 + y * 4)).astype(f32).astype(bf16)
            side_cover.append(jnp.dot(occupied, spread, preferred_element_type=f32))
    convolve(padded, band, acc, padded_side)
    gain, offset = four(scale), four(shift)

    def finish(rows, which, cov):
        first = jnp.maximum(acc[rows : rows + BRICKS] * gain + offset, 0.0)
        added = first + term[which * BRICKS : (which + 1) * BRICKS]
        return (added * cov.astype(f32)).astype(bf16)

    for k in range(16):
        lanes = slice(k * COL, (k + 1) * COL)
        hidden[:, lanes] = finish(k * BRICKS, 0, cover[:, lanes])
    for x in range(4):
        lanes = slice(x * COL, (x + 1) * COL)
        for k, out in enumerate((low_side, high_side)):
            out[:, lanes] = finish((16 + 2 * x + k) * BRICKS, 1 + k, side_cover[4 * k + x])

    def edge(out, x):
        lanes = slice(x * COL, (x + 1) * COL)
        out[:, : 4 * COL] = face_x(hidden, x)
        out[:, 4 * COL : 5 * COL] = low_side[:, lanes]
        out[:, 5 * COL :] = high_side[:, lanes]

    @pl.when(even_x)
    def _():
        edge(xs0, 3)
        edge(xs1, 0)

    @pl.when(jnp.logical_not(even_x))
    def _():
        edge(xs0, 0)
        edge(xs1, 3)


def side_reader(low_side, high_side):
    return lambda oy, x: (low_side if oy < 0 else high_side)[:, x * COL : (x + 1) * COL]


def second_inner_kernel(hidden, low_side, high_side, ids, band, acc, padded):
    gather_own(
        hidden, None, side_reader(low_side, high_side), None, ids[...], padded, (0,)
    )
    convolve_inner(padded, band, acc)


def second_outer_kernel(
    hidden, low_side, high_side, r0, r1, ids, band, scale, shift, cover, masked, acc_in,
    refined, padded, acc,
):
    from_x = x_reader(r0, r1)
    gather_own(
        hidden,
        from_x,
        side_reader(low_side, high_side),
        lambda ox, oy: from_x(ox, 4 if oy < 0 else 5),
        ids[...],
        padded,
        (-1, 1),
    )
    acc[...] = acc_in[...]
    convolve_edges(padded, band, acc)
    gain, offset = four(scale), four(shift)
    for k in range(16):
        lanes = slice(k * COL, (k + 1) * COL)
        value = acc[k * BRICKS : (k + 1) * BRICKS] * gain + offset
        value = jnp.maximum(value + masked[:, lanes].astype(f32), 0.0)
        refined[:, lanes] = (value * cover[:, lanes].astype(f32)).astype(bf16)


def exchange(first, second, axis):
    return pair_exchange(first, axis, 0), pair_exchange(second, axis, 1)


def local(
    features, occupancy, adjacency, conv_one, conv_two, scale_one, shift_one,
    scale_two, shift_two, w_query, w_key, w_value, w_out,
):
    n_sy = lax.axis_size("sy")
    whole, face, edge = shape(BRICKS, 64 * C), shape(BRICKS, 4 * COL), shape(BRICKS, 6 * COL)
    band_shape = shape(9, 6 * C, COL)
    padded_whole = pltpu.VMEM((6, 6, BRICKS, 6 * C), bf16)
    padded_side = pltpu.VMEM((3, 6, 2 * BRICKS, 6 * C), bf16)
    padded_inner = pltpu.VMEM((4, 6, BRICKS, 6 * C), bf16)
    padded_outer = pltpu.VMEM((2, 6, BRICKS, 6 * C), bf16)
    own_acc, both_acc = pltpu.VMEM((16 * BRICKS, COL), f32), pltpu.VMEM((24 * BRICKS, COL), f32)
    conv_cost = dict(flops=2 * 768 * 3456 * 256, bytes_accessed=4 << 20)
    inner_cost = dict(flops=2 * 512 * 3456 * 256, bytes_accessed=3 << 20)
    outer_cost = dict(flops=2 * 256 * 1152 * 256, bytes_accessed=3 << 20)
    marks = jnp.concatenate([occupancy, adjacency], axis=1)
    message = shape(BRICKS, Y_LANES)
    masked, cover, tokens, meta, ids, s0, s1 = call(
        prepare_kernel,
        [
            whole, whole, shape(n_sy, BRICKS // 2, 2 * C), shape(BRICKS, 4 * C),
            shape(BRICKS, 27, dtype=jnp.int32), message, message,
        ],
        (features, marks),
        bytes_accessed=2 << 20,
    )
    band_one = call(band_kernel, band_shape, (conv_one,), bytes_accessed=3 << 20)
    rows = [v.reshape(1, C) for v in (scale_one, shift_one, scale_two, shift_two)]
    t0, t1 = exchange(s0, s1, "sy")
    group = lax.all_to_all(tokens, "sy", 0, 0)
    x_message = shape(BRICKS, 8 * COL)
    x0, x1 = call(
        message_kernel, [x_message] * 2, (masked, t0, t1), flops=1 << 35, bytes_accessed=1 << 20
    )
    r0, r1 = exchange(x0, x1, "sx")
    weights = jnp.concatenate([w_key, w_value, w_query, w_out], axis=1)
    term = call(
        attention_kernel,
        shape(3 * BRICKS, COL, dtype=f32),
        (group, weights),
        flops=1 << 35,
        bytes_accessed=1 << 20,
    )
    hidden, low_side, high_side, xs0, xs1 = call(
        first_kernel,
        [whole, face, face, edge, edge],
        (
            masked, r0, r1, t0, t1, ids, band_one, rows[0], rows[1], cover, term,
        ),
        [padded_whole, padded_side, both_acc],
        **conv_cost,
    )
    later, hidden = lax.optimization_barrier((conv_two, hidden))
    band_two = call(band_kernel, band_shape, (later,), bytes_accessed=3 << 20)
    r0, r1 = exchange(xs0, xs1, "sx")
    acc = call(
        second_inner_kernel,
        shape(16 * BRICKS, COL, dtype=f32),
        (hidden, low_side, high_side, ids, band_two),
        [padded_inner],
        **inner_cost,
    )
    return call(
        second_outer_kernel,
        whole,
        (
            hidden, low_side, high_side, r0, r1, ids, band_two, rows[2], rows[3], cover, masked,
            acc,
        ),
        [padded_outer, own_acc],
        **outer_cost,
    )


def solution(mesh):
    split = P(("sx", "sy"), None)
    return jax.shard_map(
        local,
        mesh=mesh,
        in_specs=(split,) * 3 + (P(),) * 10,
        out_specs=split,
        check_vma=False,
    )
```

time: 46.5 us -> 32.3 us (0.69)
  the two profiles are of different devices: /device:TPU:40 before, /device:TPU:0 now
where the time goes in v1:
time: 32.3 us; the launch traced here: 32 us
  starting transfers between devices  18.1 us (56%)
  Pallas kernels  8.42 us (26%)
  waiting for transfers between devices  2.33 us (7%)
  local copies, waits for them, and re-layouts  2.01 us (6%)
  other arithmetic  0.92 us (3%)
    ppermute x6, starting transfers between devices, pair_exchange(): return lax.ppermute(value, axis, pairs)  14.6 us
    pallas_call x8, Pallas kernels, call(): pl.pallas_call(kernel, out_shape=out_shape, in_specs=[vmem] * len(args),...  8.42 us
    all_to_all x1, starting transfers between devices, local(): group = lax.all_to_all(tokens, 'sy', 0, 0)  3.5 us
    unnamed x22, local copies, waits for them, and re-layouts  2.01 us
    all_to_all x1, waiting for transfers between devices, local(): group = lax.all_to_all(tokens, 'sy', 0, 0)  1.85 us
    concatenate x1, other arithmetic, local(): marks = jnp.concatenate([occupancy, adjacency], axis=1)  0.83 us
  transfers between devices with their start and end apart: 7, of which 2 were waited for; matrix products, arithmetic and copies ran while one was open for 0% of the time, Pallas kernels for 10%

profile of v1, /device:TPU:0, one launch (start us, length us, event | category | flops | bytes accessed | tf_op | source)
XLA Modules:
  0.0 32.0 jit_solution(17609589962073797599)
XLA Ops:
  0.0 0.0 copy-start.7
  0.0 0.0 copy-start.9
  0.0 0.0 copy-start.8
  0.0 0.8 %pad_add_fusion.marks = s32[32,91]{1,0:T(8,128)S(1)} fusion(s32[32,27]{1,0:T(8,128)} %param.15, s32[32,64]{1,0:T(8,128)} %param.14), kind=kLoop, calls=%fused_computation.1 | loop fusion | flops 2912 | bytes 23296 | tf_op jit(solution)/shard_map/concatenate | solution.py:486
  0.8 0.0 copy-start.2
  0.8 0.9 %copy-done.2 = bf16[32,4096]{1,0:T(8,128)(2,1)S(1)} copy-done((bf16[32,4096]{1,0:T(8,128)(2,1)S(1)}, bf16[32,4096]{1,0:T(8,128)(2,1)}, u32[]{:S(2)}) %copy-start.2) | copy-done | bytes 262168
  1.8 0.0 copy-start.10
  1.8 1.0 %shard_map.127 = (bf16[32,4096]{1,0:T(8,128)(2,1)S(1)}, bf16[32,4096]{1,0:T(8,128)(2,1)S(1)}, bf16[16,16,128]{2,1,0:T(8,128)(2,1)}, bf16[32,256]{1,0:T(8,128)(2,...) custom-call(bf16[32,4096]{1,0:T(8,128)(2,1)S(1)} %copy-done.2, ...), custom_call_target="tpu_custom_call" | custom-call | bytes 2097152 | tf_op jit(solution)/shard_map/pallas_call | solution.py:22
  2.8 1.6 %collective-permute-start = (bf16[32,2304]{1,0:T(8,128)(2,1)S(1)}, bf16[32,2304]{1,0:T(8,128)(2,1)S(1)}, u32[]{:S(2)}, u32[]{:S(2)}) collective-permute-start(bf16[32,2304]{1,0:T(8,128)(2,1)S(1)} %get-tuple-element.21), channel_id=1, source_target_pairs={{0,1},{1,0},{2,3},{3,2},{4,5},{5,4},{6,7},{7,6},{8,9},{9,8},{10,11... | collective-permute-start | bytes 442376 | tf_op jit(solution)/shard_map/ppermute | solution.py:63
  4.4 4.5 %collective-permute-start.1 = (bf16[32,2304]{1,0:T(8,128)(2,1)S(1)}, bf16[32,2304]{1,0:T(8,128)(2,1)S(1)}, u32[]{:S(2)}, u32[]{:S(2)}) collective-permute-start(bf16[32,2304]{1,0:T(8,128)(2,1)S(1)} %get-tuple-element.22), channel_id=1, source_target_pairs={{0,15},{1,2},{2,1},{3,4},{4,3},{5,6},{6,5},{7,8},{8,7},{9,10},{10,... | collective-permute-start | bytes 442376 | tf_op jit(solution)/shard_map/ppermute | solution.py:63
  8.9 3.5 %all-to-all-start = ((bf16[16,16,128]{2,1,0:T(8,128)(2,1)}), bf16[16,16,128]{2,1,0:T(8,128)(2,1)S(1)}, u32[]{:S(2)}, u32[]{:S(2)}) async-start(bf16[16,16,128]{2,1,0:T(8,128)(2,1)} %get-tuple-element.27), calls=%async_computation | async-start | bytes 131072 | tf_op jit(solution)/shard_map/all_to_all | solution.py:500
  12.4 0.0 copy-start
  12.5 1.0 %copy-done = bf16[27,64,64]{2,1,0:T(8,128)(2,1)S(1)} copy-done((bf16[27,64,64]{2,1,0:T(8,128)(2,1)S(1)}, bf16[27,64,64]{2,1,0:T(8,128)(2,1)}, u32[]{:S(2)}) %copy-start) | copy-done | bytes 221208
  13.5 0.3 shard_map.129.band
  13.8 0.0 copy-done.7
  13.8 0.0 copy-done.9
  13.8 0.0 copy-done.8
  13.8 0.0 copy-done.10
  13.8 0.1 pad_maximum_fusion.weights
  13.9 0.0 collective-permute-done.t0
  13.9 0.0 collective-permute-done.1.t1
  14.0 0.1 collective-permute-start.2
  14.1 0.0 copy-start.5
  14.1 0.0 copy-start.6
  14.1 4.1 %collective-permute-start.3 = (bf16[32,2048]{1,0:T(8,128)(2,1)S(1)}, bf16[32,2048]{1,0:T(8,128)(2,1)S(1)}, u32[]{:S(2)}, u32[]{:S(2)}) collective-permute-start(bf16[32,2048]{1,0:T(8,128)(2,1)S(1)} %get-tuple-element.24), channel_id=1, source_target_pairs={{0,112},{16,32},{32,16},{48,64},{64,48},{80,96},{96,80},{112,0},{1... | collective-permute-start | bytes 393224 | tf_op jit(solution)/shard_map/ppermute | solution.py:63
  18.2 1.8 %all-to-all-done.group = bf16[16,16,128]{2,1,0:T(8,128)(2,1)S(1)} async-done(((bf16[16,16,128]{2,1,0:T(8,128)(2,1)}), bf16[16,16,128]{2,1,0:T(8,128)(2,1)S(1)}, u32[]{:S(2)}, u32[]{:S(2)}) %all-to-all-start) | async-done | bytes 65568 | tf_op jit(solution)/shard_map/all_to_all | solution.py:500
  20.0 1.0 %shard_map.130.term = f32[96,256]{1,0:T(8,128)S(1)} custom-call(bf16[16,16,128]{2,1,0:T(8,128)(2,1)S(1)} %all-to-all-done.group, bf16[64,256]{1,0:T(8,128)(2,1)S(1)} %pad_maximum_fusion.weights), custom_call_target="tpu_custom_call" | custom-call | flops 34359738368 | bytes 1048576 | tf_op jit(solution)/shard_map/pallas_call | solution.py:22
  21.0 0.0 collective-permute-done.2.r0
  21.0 0.0 collective-permute-done.3.r1
  21.1 0.0 copy-done.5
  21.1 0.0 copy-done.6
  21.1 0.0 copy-start.1
  21.1 2.9 %shard_map.131 = (bf16[32,4096]{1,0:T(8,128)(2,1)S(1)}, bf16[32,1024]{1,0:T(8,128)(2,1)S(1)}, bf16[32,1024]{1,0:T(8,128)(2,1)S(1)}, bf16[32,1536]{1,0:T(8,128)(2,1)S(1)}, bf16[32,1536]{1,0:T(8,128)(2,1)S(1)}) custom-call(bf16[32,4096]{1,0:T(8,128)(2,1)S(1)} %get-tuple-element.20.masked, bf16[32,2048]{1,0:T(8,128)(2,1)S(1)} %collective-permute-done.2.r0, ...), custom_call_target="tpu_custom_call" | custom-call | flops 1358954496 | bytes 4194304 | tf_op jit(solution)/shard_map/pallas_call | solution.py:22
  24.0 0.1 collective-permute-start.4
  24.1 4.1 %collective-permute-start.5 = (bf16[32,1536]{1,0:T(8,128)(2,1)S(1)}, bf16[32,1536]{1,0:T(8,128)(2,1)S(1)}, u32[]{:S(2)}, u32[]{:S(2)}) collective-permute-start(bf16[32,1536]{1,0:T(8,128)(2,1)S(1)} %get-tuple-element.33), channel_id=1, source_target_pairs={{0,112},{16,32},{32,16},{48,64},{64,48},{80,96},{96,80},{112,0},{1... | collective-permute-start | bytes 294920 | tf_op jit(solution)/shard_map/ppermute | solution.py:63
  28.3 0.0 copy-done.1
  28.3 0.3 shard_map.132.band
  28.6 0.0 copy-start.3
  28.6 0.0 copy-start.4
  28.6 1.5 %shard_map.133.acc_in = f32[512,256]{1,0:T(8,128)S(1)} custom-call(bf16[32,4096]{1,0:T(8,128)(2,1)S(1)} %get-tuple-element.29.hidden, bf16[32,1024]{1,0:T(8,128)(2,1)S(1)} %get-tuple-element.30.low_side, bf16[32,1024]{1,0:T(8,128)(2,1)S(1)} %get-tuple-element.31.high_side, s32[32,27]{1,0:T(8,128)S(1)} %get-tuple-element.25.ids, ...), custom_call_target="tpu_custom_call" | custom-call | flops 905969664 | bytes 3145728 | tf_op jit(solution)/shard_map/pallas_call | solution.py:22
  30.1 0.0 collective-permute-done.4.r0
  30.1 0.5 %collective-permute-done.5.r1 = bf16[32,1536]{1,0:T(8,128)(2,1)S(1)} collective-permute-done((bf16[32,1536]{1,0:T(8,128)(2,1)S(1)}, bf16[32,1536]{1,0:T(8,128)(2,1)S(1)}, u32[]{:S(2)}, u32[]{:S(2)}) %collective-permute-start.5) | collective-permute-done | bytes 98336 | tf_op jit(solution)/shard_map/ppermute | solution.py:63
  30.6 0.0 copy-done.3
  30.6 0.0 copy-done.4
  30.6 1.4 %shard_map.134 = bf16[32,4096]{1,0:T(8,128)(2,1)} custom-call(bf16[32,4096]{1,0:T(8,128)(2,1)S(1)} %get-tuple-element.29.hidden, bf16[32,1024]{1,0:T(8,128)(2,1)S(1)} %get-tuple-element.30.low_side, bf16[32,1024]{1,0:T(8,128)(2,1)S(1)} %get-tuple-element.31.high_side, bf16[32,1536]{1,0:T(8,128)(2,1)S(1)} %collective-permute-done.4.r0, ...), custom_call_target="tpu_custom_call" | custom-call | flops 150994944 | bytes 3145728 | tf_op jit(solution)/shard_map/pallas_call | solution.py:22
  (1 shorter events, 0.0 us)
Async XLA Ops:
  0.0 13.8 %copy-start.7 = (bf16[64,64]{1,0:T(8,128)(2,1)S(1)}, bf16[64,64]{1,0:T(8,128)(2,1)}, u32[]{:S(2)}) copy-start(bf16[64,64]{1,0:T(8,128)(2,1)} %param.25) | copy-start | bytes 24580
  0.0 13.8 %copy-start.9 = (bf16[64,64]{1,0:T(8,128)(2,1)S(1)}, bf16[64,64]{1,0:T(8,128)(2,1)}, u32[]{:S(2)}) copy-start(bf16[64,64]{1,0:T(8,128)(2,1)} %param.24) | copy-start | bytes 24580
  0.0 13.8 %copy-start.8 = (bf16[64,64]{1,0:T(8,128)(2,1)S(1)}, bf16[64,64]{1,0:T(8,128)(2,1)}, u32[]{:S(2)}) copy-start(bf16[64,64]{1,0:T(8,128)(2,1)} %param.22) | copy-start | bytes 24580
  0.8 1.0 %copy-start.2 = (bf16[32,4096]{1,0:T(8,128)(2,1)S(1)}, bf16[32,4096]{1,0:T(8,128)(2,1)}, u32[]{:S(2)}) copy-start(bf16[32,4096]{1,0:T(8,128)(2,1)} %feat.1) | copy-start | bytes 786436
  1.8 12.0 %copy-start.10 = (bf16[64,64]{1,0:T(8,128)(2,1)S(1)}, bf16[64,64]{1,0:T(8,128)(2,1)}, u32[]{:S(2)}) copy-start(bf16[64,64]{1,0:T(8,128)(2,1)} %param.23) | copy-start | bytes 24580
  2.8 11.1 %collective-permute-start = (bf16[32,2304]{1,0:T(8,128)(2,1)S(1)}, bf16[32,2304]{1,0:T(8,128)(2,1)S(1)}, u32[]{:S(2)}, u32[]{:S(2)}) collective-permute-start(bf16[32,2304]{1,0:T(8,128)(2,1)S(1)} %get-tuple-element.21), channel_id=1, source_target_pairs={{0,1},{1,0},{2,3},{3,2},{4,5},{5,4},{6,7},{7,6},{8,9},{9,8},{10,11... | collective-permute-start | bytes 442376 | tf_op jit(solution)/shard_map/ppermute | solution.py:63
  4.4 9.5 %collective-permute-start.1 = (bf16[32,2304]{1,0:T(8,128)(2,1)S(1)}, bf16[32,2304]{1,0:T(8,128)(2,1)S(1)}, u32[]{:S(2)}, u32[]{:S(2)}) collective-permute-start(bf16[32,2304]{1,0:T(8,128)(2,1)S(1)} %get-tuple-element.22), channel_id=1, source_target_pairs={{0,15},{1,2},{2,1},{3,4},{4,3},{5,6},{6,5},{7,8},{8,7},{9,10},{10,... | collective-permute-start | bytes 442376 | tf_op jit(solution)/shard_map/ppermute | solution.py:63
  8.9 11.1 %all-to-all-start = ((bf16[16,16,128]{2,1,0:T(8,128)(2,1)}), bf16[16,16,128]{2,1,0:T(8,128)(2,1)S(1)}, u32[]{:S(2)}, u32[]{:S(2)}) async-start(bf16[16,16,128]{2,1,0:T(8,128)(2,1)} %get-tuple-element.27), calls=%async_computation | async-start | bytes 131072 | tf_op jit(solution)/shard_map/all_to_all | solution.py:500
  12.4 1.0 %copy-start = (bf16[27,64,64]{2,1,0:T(8,128)(2,1)S(1)}, bf16[27,64,64]{2,1,0:T(8,128)(2,1)}, u32[]{:S(2)}) copy-start(bf16[27,64,64]{2,1,0:T(8,128)(2,1)} %weight.1) | copy-start | bytes 663556
  14.0 7.1 %collective-permute-start.2 = (bf16[32,2048]{1,0:T(8,128)(2,1)S(1)}, bf16[32,2048]{1,0:T(8,128)(2,1)S(1)}, u32[]{:S(2)}, u32[]{:S(2)}) collective-permute-start(bf16[32,2048]{1,0:T(8,128)(2,1)S(1)} %get-tuple-element.23), channel_id=1, source_target_pairs={{0,16},{16,0},{32,48},{48,32},{64,80},{80,64},{96,112},{112,96},{1... | collective-permute-start | bytes 393224 | tf_op jit(solution)/shard_map/ppermute | solution.py:63
  14.1 7.0 %copy-start.5 = (f32[64]{0:T(128)S(1)}, f32[64]{0:T(128)}, u32[]{:S(2)}) copy-start(f32[64]{0:T(128)} %param.18) | copy-start | bytes 772
  14.1 7.0 %copy-start.6 = (f32[64]{0:T(128)S(1)}, f32[64]{0:T(128)}, u32[]{:S(2)}) copy-start(f32[64]{0:T(128)} %param.19) | copy-start | bytes 772
  14.1 7.0 %collective-permute-start.3 = (bf16[32,2048]{1,0:T(8,128)(2,1)S(1)}, bf16[32,2048]{1,0:T(8,128)(2,1)S(1)}, u32[]{:S(2)}, u32[]{:S(2)}) collective-permute-start(bf16[32,2048]{1,0:T(8,128)(2,1)S(1)} %get-tuple-element.24), channel_id=1, source_target_pairs={{0,112},{16,32},{32,16},{48,64},{64,48},{80,96},{96,80},{112,0},{1... | collective-permute-start | bytes 393224 | tf_op jit(solution)/shard_map/ppermute | solution.py:63
  21.1 7.2 %copy-start.1 = (bf16[27,64,64]{2,1,0:T(8,128)(2,1)S(1)}, bf16[27,64,64]{2,1,0:T(8,128)(2,1)}, u32[]{:S(2)}) copy-start(bf16[27,64,64]{2,1,0:T(8,128)(2,1)} %weight.2) | copy-start | bytes 663556
  24.0 6.1 %collective-permute-start.4 = (bf16[32,1536]{1,0:T(8,128)(2,1)S(1)}, bf16[32,1536]{1,0:T(8,128)(2,1)S(1)}, u32[]{:S(2)}, u32[]{:S(2)}) collective-permute-start(bf16[32,1536]{1,0:T(8,128)(2,1)S(1)} %get-tuple-element.32), channel_id=1, source_target_pairs={{0,16},{16,0},{32,48},{48,32},{64,80},{80,64},{96,112},{112,96},{1... | collective-permute-start | bytes 294920 | tf_op jit(solution)/shard_map/ppermute | solution.py:63
  24.1 6.4 %collective-permute-start.5 = (bf16[32,1536]{1,0:T(8,128)(2,1)S(1)}, bf16[32,1536]{1,0:T(8,128)(2,1)S(1)}, u32[]{:S(2)}, u32[]{:S(2)}) collective-permute-start(bf16[32,1536]{1,0:T(8,128)(2,1)S(1)} %get-tuple-element.33), channel_id=1, source_target_pairs={{0,112},{16,32},{32,16},{48,64},{64,48},{80,96},{96,80},{112,0},{1... | collective-permute-start | bytes 294920 | tf_op jit(solution)/shard_map/ppermute | solution.py:63
  28.6 2.0 %copy-start.3 = (f32[64]{0:T(128)S(1)}, f32[64]{0:T(128)}, u32[]{:S(2)}) copy-start(f32[64]{0:T(128)} %param.20) | copy-start | bytes 772
  28.6 2.0 %copy-start.4 = (f32[64]{0:T(128)S(1)}, f32[64]{0:T(128)}, u32[]{:S(2)}) copy-start(f32[64]{0:T(128)} %param.21) | copy-start | bytes 772

commit v2 on v1

v2 whole, which is shorter than its diff:
```python
import math

import jax
import jax.numpy as jnp
from jax import lax
from jax.experimental import pallas as pl
from jax.experimental.pallas import tpu as pltpu
from jax.sharding import PartitionSpec as P

HEADS = 2
C = 64
COL = 4 * C
BRICKS = 32
EPSILON = 1e-05
FAR = -(1 << 20)
VMEM_LIMIT = 16 * 1024 * 1024
f32, bf16 = jnp.float32, jnp.bfloat16


def call(kernel, out_shape, args, scratch=(), flops=0, bytes_accessed=0):
    vmem = pl.BlockSpec(memory_space=pltpu.VMEM)
    return pl.pallas_call(
        kernel,
        out_shape=out_shape,
        in_specs=[vmem] * len(args),
        out_specs=jax.tree.map(lambda _: vmem, out_shape),
        scratch_shapes=list(scratch),
        compiler_params=pltpu.CompilerParams(vmem_limit_bytes=VMEM_LIMIT),
        cost_estimate=pl.CostEstimate(
            flops=flops, bytes_accessed=bytes_accessed, transcendentals=0
        ),
    )(*args)


def shape(*dims, dtype=bf16):
    return jax.ShapeDtypeStruct(dims, dtype)


def column(x, y):
    return slice((x * 4 + y) * COL, (x * 4 + y + 1) * COL)


def face_x(ref, x):
    return ref[:, x * 4 * COL : (x + 1) * 4 * COL]


def pick(flag, a, b):
    return jnp.where(flag, a, b)


def parities():
    even_x = lax.rem(lax.axis_index("sx"), 2) == 0
    even_y = lax.rem(lax.axis_index("sy"), 2) == 0
    return even_x, even_y


def pair_exchange(value, axis, phase):
    n_x, n_y = lax.axis_size("sx"), lax.axis_size("sy")

    def partner(x, y):
        s, count = (x, n_x) if axis == "sx" else (y, n_y)
        if phase == 1 and s in (0, count - 1):
            return (x, y ^ 1) if axis == "sx" else (x ^ 1, y)
        s = s ^ 1 if phase == 0 else ((s + 1) ^ 1) - 1
        return (s, y) if axis == "sx" else (x, s)

    pairs = []
    for x in range(n_x):
        for y in range(n_y):
            there = partner(x, y)
            pairs.append((x * n_y + y, there[0] * n_y + there[1]))
    return lax.ppermute(value, ("sx", "sy"), pairs)


def device_base():
    return (lax.axis_index("sx") * lax.axis_size("sy") + lax.axis_index("sy")) * BRICKS


def id_step(dx, dy):
    return (dx * lax.axis_size("sy") + dy) * BRICKS


def one_hot(ids, offsets, bases):
    lane = lax.broadcasted_iota(jnp.int32, (BRICKS, 32 * len(bases)), 1)
    candidate = jnp.bitwise_and(lane, 31) + bases[0]
    for k in range(1, len(bases)):
        slot = lax.shift_right_logical(lane, 5) == k
        candidate = candidate + jnp.where(slot, bases[k] - bases[0], 0)
    rows = [
        (ids[:, o : o + 1] == candidate).astype(f32).astype(bf16)
        for o in ((ox + 1) * 9 + (oy + 1) * 3 + (oz + 1) for ox, oy, oz in offsets)
    ]
    return jnp.concatenate(rows, axis=0)


def put_column(select, parts, core, store):
    table = parts[0] if len(parts) == 1 else jnp.concatenate(parts, axis=0)
    got = jnp.dot(select, table, preferred_element_type=f32).astype(bf16)
    lane_low = lax.broadcasted_iota(jnp.int32, (BRICKS, 128), 1) < C
    ends = jnp.where(lane_low, got[:BRICKS, :128], got[BRICKS : 2 * BRICKS, 128:])
    store(got[2 * BRICKS :] if core is None else core, ends)


NEAR, BEHIND, META, Y_LANES = 0, 4 * COL, 8 * COL, 9 * COL


def prepare_kernel(feat, marks, masked, cover, tokens_all, meta, ids, s0, s1):
    occupied = marks[:, :C].astype(f32).astype(bf16)
    row = lax.broadcasted_iota(jnp.int32, (64, COL), 0)
    voxel = lax.shift_right_logical(lax.broadcasted_iota(jnp.int32, (64, COL), 1), 6)
    total = jnp.zeros((BRICKS, 128), f32)
    for k in range(16):
        lanes = slice(k * COL, (k + 1) * COL)
        spread = (row == voxel + 4 * k).astype(f32).astype(bf16)
        cov = jnp.dot(occupied, spread, preferred_element_type=f32).astype(bf16)
        part = feat[:, lanes] * cov
        cover[:, lanes] = cov
        masked[:, lanes] = part
        wide = part.astype(f32)
        total = total + wide[:, :128] + wide[:, 128:]
    summed = total[:, :C] + total[:, C:]
    tokens = (summed / 8.0).astype(bf16)
    half = BRICKS // 2
    packed = jnp.concatenate([tokens[:half], tokens[half:]], axis=1)
    tokens_all[...] = jnp.broadcast_to(packed[None], tokens_all.shape)
    number = marks[:, C : C + 27]
    ids[...] = jnp.where(number < 0, FAR, number)
    number = number + 1
    high = lax.shift_right_logical(number, 6).astype(f32).astype(bf16)
    low = jnp.bitwise_and(number, 63).astype(f32).astype(bf16)
    gap = jnp.zeros((BRICKS, C - 27), bf16)
    about = jnp.concatenate([high, gap, low, gap, occupied, tokens], axis=1)
    meta[...] = about
    _, even_y = parities()

    def write(out, near, behind):
        for place, y in ((NEAR, near), (BEHIND, behind)):
            for x in range(4):
                out[:, place + x * COL : place + (x + 1) * COL] = masked[:, column(x, y)]
        out[:, META:] = about

    @pl.when(even_y)
    def _():
        write(s0, 3, 2)
        write(s1, 0, 1)

    @pl.when(jnp.logical_not(even_y))
    def _():
        write(s0, 0, 1)
        write(s1, 3, 2)


def fill_band(weight, band):
    zero = jnp.zeros((C, C), bf16)
    for t in range(9):
        for r, z_in in enumerate((0, 1, 2, 3, 4, -1)):
            blocks = []
            for z_out in range(4):
                tap = z_in - z_out + 1
                blocks.append(weight[t * 3 + tap] if 0 <= tap < 3 else zero)
            band[t, r * C : (r + 1) * C, :] = jnp.concatenate(blocks, axis=1)


def message_kernel(masked, t0, t1, x0, x1):
    even_x, even_y = parities()

    def write(out, x):
        out[:, : 4 * COL] = face_x(masked, x)
        place = 4 * COL
        for a, b in ((t1, t0), (t0, t1)):
            for plane in (NEAR, BEHIND):
                lanes = slice(plane + x * COL, plane + (x + 1) * COL)
                out[:, place : place + COL] = pick(even_y, a[:, lanes], b[:, lanes])
                place += COL

    @pl.when(even_x)
    def _():
        write(x0, 3)
        write(x1, 0)

    @pl.when(jnp.logical_not(even_x))
    def _():
        write(x0, 0)
        write(x1, 3)


def place_x(ox, x):
    return x if ox == 0 else (0 if ox < 0 else 1)


def sources_of(ox, oy):
    sources = [(0, 0)]
    if ox:
        sources.append((ox, 0))
    if oy:
        sources.append((0, oy))
    if ox and oy:
        sources.append((ox, oy))
    return sources


def own_select(ids, ox, oy):
    base = device_base()
    offsets = [(ox, oy, oz) for oz in ((1, -1) if ox == 0 and oy == 0 else (1, -1, 0))]
    return one_hot(ids, offsets, [base + id_step(dx, dy) for dx, dy in sources_of(ox, oy)])


def side_select(ids, side, ox):
    here, there = device_base(), device_base() + id_step(0, side)
    outer = [here] if ox == 0 else [here, here + id_step(ox, 0)]
    inner = [there] if ox == 0 else [there, there + id_step(ox, 0)]
    offsets = [(ox, 0, oz) for oz in ((1, -1) if ox == 0 else (1, -1, 0))]
    return (
        one_hot(ids, offsets, inner),
        one_hot(ids, [(ox, -side, oz) for oz in (1, -1, 0)], outer),
    )


def gather_own(own, from_x, from_y, from_corner, select_of, padded, x_offsets):
    for ox in x_offsets:
        for oy in (-1, 0, 1):
            centre = ox == 0 and oy == 0
            select = select_of(ox, oy)
            for x in {-1: (3,), 0: range(4), 1: (0,)}[ox]:
                for y in {-1: (3,), 0: range(4), 1: (0,)}[oy]:
                    parts = [own(x, y)]
                    if ox:
                        parts.append(from_x(ox, y))
                    if oy:
                        parts.append(from_y(oy, x))
                    if ox and oy:
                        parts.append(from_corner(ox, oy))
                    px = place_x(ox, x)
                    py = {-1: 0, 0: 1 + y, 1: 5}[oy]

                    def store(core, ends, px=px, py=py):
                        padded[px, py, :, :COL] = core
                        padded[px, py, :, COL:] = ends

                    put_column(select, parts, parts[0] if centre else None, store)


def gather_side(own, from_x, from_message, side, select_of, padded, x_offsets):
    mine = {-1: 0, 1: 3}[side]
    rows = slice(0, BRICKS) if side < 0 else slice(BRICKS, 2 * BRICKS)
    for ox in x_offsets:
        select_inner, select_outer = select_of(side, ox)
        for x in {-1: (3,), 0: range(4), 1: (0,)}[ox]:
            px = place_x(ox, x)
            for place, py in ((BEHIND, 1 + side), (NEAR, 1), (None, 1 - side)):

                def store(core, ends, px=px, py=py):
                    padded[px, py, rows, :COL] = core
                    padded[px, py, rows, COL:] = ends

                if place is None:
                    parts = [own(x, mine)]
                    if ox:
                        parts.append(from_x(ox, mine))
                    put_column(select_outer, parts, None, store)
                    continue
                parts = [from_message(side, place + x * COL)]
                if ox:
                    parts.append(from_x(ox, corner_place(side, place)))
                put_column(select_inner, parts, parts[0] if ox == 0 else None, store)


def corner_place(side, plane):
    return 4 + (0 if side < 0 else 2) + (0 if plane == NEAR else 1)


TAP = 6 * C


def taps(padded, side, x_range, first, count):
    parts = []
    for t in range(first, first + count):
        i, j = t // 3, t % 3
        rows = [padded[x + i, j : j + 4].reshape(4 * BRICKS, TAP) for x in x_range]
        if side is not None:
            rows += [side[x + i, j] for x in x_range]
        parts.append(jnp.concatenate(rows, axis=0))
    return jnp.concatenate(parts, axis=1)


def product(lhs, band, first, count):
    rhs = band[first : first + count].reshape(count * TAP, COL)
    return jnp.dot(lhs, rhs, preferred_element_type=f32)


def convolve_inner(inner, side, band, store):
    store((1, 2), product(taps(inner, side, (0, 1), 0, 9), band, 0, 9))
    store((0,), product(taps(inner, side, (-1,), 3, 6), band, 3, 6))
    store((3,), product(taps(inner, side, (2,), 0, 6), band, 0, 6))


def convolve_edge(outer, side, band, x):
    i, place = (0, 0) if x == 0 else (2, 1)
    return product(taps(outer, side, (place - i,), 3 * i, 3), band, 0 if x == 0 else 3, 3)


def four(ref):
    return jnp.concatenate([ref[...]] * 4, axis=1)


def project(tokens, weight):
    return jnp.dot(tokens, weight, preferred_element_type=f32).astype(bf16)


def attention(tokens, packed, w_key, w_value, w_query, w_out):
    group = jnp.concatenate([packed[:, :C], packed[:, C:]], axis=0)
    kv = project(group, jnp.concatenate([w_key, w_value], axis=1))
    queries = project(tokens, w_query)
    rows = queries.shape[0]
    wide = jnp.concatenate([queries, jnp.zeros_like(queries)], axis=1).astype(f32)
    lane = lax.broadcasted_iota(jnp.int32, (rows, 2 * C), 1)
    per_head = [jnp.where(lax.shift_right_logical(lane, 5) == h, wide, 0.0) for h in range(HEADS)]
    wide = jnp.concatenate(per_head, axis=0).astype(bf16)
    logits = lax.dot_general(
        wide, kv, (((1,), (1,)), ((), ())), preferred_element_type=f32
    ) * (1.0 / math.sqrt(C // HEADS))
    top = jnp.max(logits, axis=1, keepdims=True)
    weight = jnp.exp(logits - top)
    total = jnp.sum(weight, axis=1, keepdims=True)
    coarse = weight.astype(bf16)
    fine = (weight - coarse.astype(f32)).astype(bf16)
    mixed = jnp.dot(coarse, kv, preferred_element_type=f32)
    mixed = mixed + jnp.dot(fine, kv, preferred_element_type=f32)
    mixed = mixed / total
    context = jnp.where(lane < C + C // 2, mixed[:rows], mixed[rows:])
    context = jnp.where(lane < C, 0.0, context)
    mean = jnp.sum(context * context, axis=1, keepdims=True) / C
    attended = (context / jnp.sqrt(mean + EPSILON)).astype(bf16)
    w_out = jnp.concatenate([w_out] * 4, axis=1)
    return jnp.dot(attended[:, C:], w_out, preferred_element_type=f32)


def y_reader(t0, t1):
    _, even_y = parities()

    def from_y(oy, place, width=COL):
        lanes = slice(place, place + width)
        a, b = (t1, t0) if oy < 0 else (t0, t1)
        return pick(even_y, a[:, lanes], b[:, lanes])

    return from_y


def x_reader(r0, r1):
    even_x, _ = parities()

    def from_x(ox, k):
        lanes = slice(k * COL, (k + 1) * COL)
        a, b = (r1, r0) if ox < 0 else (r0, r1)
        return pick(even_x, a[:, lanes], b[:, lanes])

    return from_x


def side_ids(about):
    high, low = about[:, :C].astype(f32), about[:, C : 2 * C].astype(f32)
    number = (high * 64.0 + low).astype(jnp.int32) - 1
    return jnp.where(number < 0, FAR, number)


def attention_kernel(group, w_key, w_value, w_query, w_out, term):
    count = group.shape[0]
    here = lax.axis_index("sy")
    tokens = []
    for step in (0, count - 1, 1):
        packed = group[lax.rem(here + step, count)]
        tokens += [packed[:, :C], packed[:, C:]]
    packed = group[...].reshape(-1, 2 * C)
    tokens = jnp.concatenate(tokens, axis=0)
    term[...] = attention(tokens, packed, w_key[...], w_value[...], w_query[...], w_out[...])


def near_kernel(
    masked, t0, t1, ids_ref, weight, acc, acc_side, band_edge, inner, side_inner, band
):
    from_message = y_reader(t0, t1)
    ids = ids_ref[...]

    def own(x, y):
        return masked[:, column(x, y)]

    def from_y(oy, x):
        return from_message(oy, NEAR + x * COL)

    fill_band(weight, band)
    gather_own(own, None, from_y, None, lambda ox, oy: own_select(ids, ox, oy), inner, (0,))
    for side in (-1, 1):
        number = side_ids(from_message(side, META))
        gather_side(
            own, None, from_message, side,
            lambda side, ox, number=number: side_select(number, side, ox), side_inner, (0,),
        )

    def store(x_range, value):
        count = len(x_range)
        for n, x in enumerate(x_range):
            acc[x] = value[n * 4 * BRICKS : (n + 1) * 4 * BRICKS]
            rows = (4 * count + 2 * n) * BRICKS
            acc_side[x] = value[rows : rows + 2 * BRICKS]

    convolve_inner(inner, side_inner, band, store)
    band_edge[:3] = band[:3]
    band_edge[3:] = band[6:]


def finish(acc, acc_side, x, gain, offset, cover, from_message, term, store, store_side):
    def one(part, which, cov):
        first = jnp.maximum(part * gain + offset, 0.0)
        return ((first + term[which * BRICKS : (which + 1) * BRICKS]) * cov).astype(bf16)

    row = lax.broadcasted_iota(jnp.int32, (64, COL), 0)
    voxel = lax.shift_right_logical(lax.broadcasted_iota(jnp.int32, (64, COL), 1), 6)
    for y in range(4):
        cov = cover[:, column(x, y)].astype(f32)
        store(x, y, one(acc[y * BRICKS : (y + 1) * BRICKS], 0, cov))
    for k, side in enumerate((-1, 1)):
        occupied = from_message(side, META)[:, 2 * C : 3 * C]
        spread = (row == voxel + (x * 16 + (3 - 3 * k) * 4)).astype(f32).astype(bf16)
        cov = jnp.dot(occupied, spread, preferred_element_type=f32)
        store_side(x, side, one(acc_side[k * BRICKS : (k + 1) * BRICKS], 1 + k, cov))


def first_edge_kernel(
    masked, r0, r1, t0, t1, ids_ref, band_edge, scale, shift, cover, term, acc, acc_side,
    xs0, xs1, outer, side_outer,
):
    even_x, _ = parities()
    from_message, from_x = y_reader(t0, t1), x_reader(r0, r1)
    ids = ids_ref[...]

    def own(x, y):
        return masked[:, column(x, y)]

    gather_own(
        own,
        from_x,
        lambda oy, x: from_message(oy, NEAR + x * COL),
        lambda ox, oy: from_x(ox, corner_place(oy, NEAR)),
        lambda ox, oy: own_select(ids, ox, oy),
        outer,
        (-1, 1),
    )
    for side in (-1, 1):
        number = side_ids(from_message(side, META))
        gather_side(
            own, from_x, from_message, side,
            lambda side, ox, number=number: side_select(number, side, ox), side_outer, (-1, 1),
        )

    def put(x, k, value):
        lanes = slice(k * COL, (k + 1) * COL)

        @pl.when(even_x == (x == 3))
        def _():
            xs0[:, lanes] = value

        @pl.when(even_x != (x == 3))
        def _():
            xs1[:, lanes] = value

    for x in (0, 3):
        more = convolve_edge(outer, side_outer, band_edge, x)
        finish(
            acc[x] + more[: 4 * BRICKS], acc_side[x] + more[4 * BRICKS :], x, four(scale),
            four(shift), cover, from_message, term,
            put, lambda x, side, value: put(x, 4 if side < 0 else 5, value),
        )


def edge_reader(xs0, xs1):
    even_x, _ = parities()

    def edge(x, k):
        lanes = slice(k * COL, (k + 1) * COL)
        a, b = (xs0, xs1) if x == 3 else (xs1, xs0)
        return pick(even_x, a[:, lanes], b[:, lanes])

    return edge


def middle_kernel(
    acc, acc_side, scale, shift, cover, t0, t1, term, xs0, xs1, ids_ref, weight,
    acc_out, band_edge, mid, mid_side, padded, band,
):
    edge = edge_reader(xs0, xs1)
    from_message = y_reader(t0, t1)
    ids = ids_ref[...]
    fill_band(weight, band)
    band_edge[:3] = band[:3]
    band_edge[3:] = band[6:]

    def put(x, y, value):
        mid[x - 1, y] = value

    def put_side(x, side, value):
        mid_side[x - 1, 0 if side < 0 else 1] = value

    for x in (1, 2):
        finish(
            acc[x], acc_side[x], x, four(scale), four(shift), cover, from_message, term,
            put, put_side,
        )

    def own(x, y):
        return mid[x - 1, y] if x in (1, 2) else edge(x, y)

    def from_y(oy, x):
        k = 0 if oy < 0 else 1
        return mid_side[x - 1, k] if x in (1, 2) else edge(x, 4 + k)

    gather_own(own, None, from_y, None, lambda ox, oy: own_select(ids, ox, oy), padded, (0,))

    def store(x_range, value):
        for n, x in enumerate(x_range):
            acc_out[x] = value[n * 4 * BRICKS : (n + 1) * 4 * BRICKS]

    convolve_inner(padded, None, band, store)


def second_kernel(
    xs0, xs1, r0, r1, ids_ref, band_edge, scale, shift, cover, masked, acc, refined, outer
):
    edge, from_x = edge_reader(xs0, xs1), x_reader(r0, r1)
    ids = ids_ref[...]
    gather_own(
        edge,
        from_x,
        lambda oy, x: edge(x, 4 if oy < 0 else 5),
        lambda ox, oy: from_x(ox, 4 if oy < 0 else 5),
        lambda ox, oy: own_select(ids, ox, oy),
        outer,
        (-1, 1),
    )
    gain, offset = four(scale), four(shift)
    for x in (1, 2, 0, 3):
        total = acc[x]
        if x in (0, 3):
            total = total + convolve_edge(outer, None, band_edge, x)
        for y in range(4):
            lanes = column(x, y)
            value = total[y * BRICKS : (y + 1) * BRICKS] * gain + offset
            value = jnp.maximum(value + masked[:, lanes].astype(f32), 0.0)
            refined[:, lanes] = (value * cover[:, lanes].astype(f32)).astype(bf16)


def exchange(first, second, axis):
    return pair_exchange(first, axis, 0), pair_exchange(second, axis, 1)


def local(
    features, occupancy, adjacency, conv_one, conv_two, scale_one, shift_one,
    scale_two, shift_two, w_query, w_key, w_value, w_out,
):
    n_sy = lax.axis_size("sy")
    whole, edge = shape(BRICKS, 64 * C), shape(BRICKS, 6 * COL)
    band_edge = shape(6, TAP, COL)
    own_acc, side_acc = shape(4, 4 * BRICKS, COL, dtype=f32), shape(4, 2 * BRICKS, COL, dtype=f32)
    band = pltpu.VMEM((9, TAP, COL), bf16)
    inner = pltpu.VMEM((4, 6, BRICKS, TAP), bf16)
    outer = pltpu.VMEM((2, 6, BRICKS, TAP), bf16)
    side_inner = pltpu.VMEM((4, 3, 2 * BRICKS, TAP), bf16)
    side_outer = pltpu.VMEM((2, 3, 2 * BRICKS, TAP), bf16)
    marks = jnp.concatenate([occupancy, adjacency], axis=1)
    message = shape(BRICKS, Y_LANES)
    masked, cover, tokens, meta, ids, s0, s1 = call(
        prepare_kernel,
        [
            whole, whole, shape(n_sy, BRICKS // 2, 2 * C), shape(BRICKS, 4 * C),
            shape(BRICKS, 27, dtype=jnp.int32), message, message,
        ],
        (features, marks),
        bytes_accessed=2 << 20,
    )
    rows = [v.reshape(1, C) for v in (scale_one, shift_one, scale_two, shift_two)]
    t0, t1 = exchange(s0, s1, "sy")
    group = lax.all_to_all(tokens, "sy", 0, 0)
    x_message = shape(BRICKS, 8 * COL)
    x0, x1 = call(
        message_kernel, [x_message] * 2, (masked, t0, t1), flops=1 << 35, bytes_accessed=1 << 20
    )
    r0, r1 = exchange(x0, x1, "sx")
    acc, acc_side, band_one = call(
        near_kernel,
        [own_acc, side_acc, band_edge],
        (masked, t0, t1, ids, conv_one),
        [inner, side_inner, band],
        flops=1 << 31,
        bytes_accessed=2 << 20,
    )
    group, acc = lax.optimization_barrier((group, acc))
    term = call(
        attention_kernel,
        shape(3 * BRICKS, COL, dtype=f32),
        (group, w_key, w_value, w_query, w_out),
        flops=1 << 26,
        bytes_accessed=1 << 20,
    )
    xs0, xs1 = call(
        first_edge_kernel,
        [edge, edge],
        (
            masked, r0, r1, t0, t1, ids, band_one, rows[0], rows[1], cover, term, acc, acc_side,
        ),
        [outer, side_outer],
        flops=2 * 384 * 3456 * 256,
        bytes_accessed=4 << 20,
    )
    r0, r1 = exchange(xs0, xs1, "sx")
    acc, band_two = call(
        middle_kernel,
        [own_acc, band_edge],
        (
            acc, acc_side, rows[0], rows[1], cover, t0, t1, term, xs0, xs1, ids, conv_two,
        ),
        [
            pltpu.VMEM((2, 4, BRICKS, COL), bf16),
            pltpu.VMEM((2, 2, BRICKS, COL), bf16),
            inner,
            band,
        ],
        flops=1 << 33,
        bytes_accessed=4 << 20,
    )
    return call(
        second_kernel,
        whole,
        (xs0, xs1, r0, r1, ids, band_two, rows[2], rows[3], cover, masked, acc),
        [outer],
        flops=2 * 256 * 1152 * 256,
        bytes_accessed=3 << 20,
    )


def solution(mesh):
    split = P(("sx", "sy"), None)
    return jax.shard_map(
        local,
        mesh=mesh,
        in_specs=(split,) * 3 + (P(),) * 10,
        out_specs=split,
        check_vma=False,
    )
```

time: 32.3 us -> 30.4 us (0.941)
  the two profiles are of different devices: /device:TPU:0 before, /device:TPU:1 now
where the time goes in v2:
time: 30.4 us; the launch traced here: 30 us
  starting transfers between devices  17 us (56%)
  Pallas kernels  8.47 us (28%)
  waiting for transfers between devices  2.65 us (9%)
  local copies, waits for them, and re-layouts  1 us (3%)
  other arithmetic  0.81 us (3%)
    ppermute x6, starting transfers between devices, pair_exchange(): return lax.ppermute(value, ('sx', 'sy'), pairs)  10.5 us
    pallas_call x7, Pallas kernels, call(): pl.pallas_call(kernel, out_shape=out_shape, in_specs=[vmem] * len(args),...  8.47 us
    all_to_all x1, starting transfers between devices, local(): group = lax.all_to_all(tokens, 'sy', 0, 0)  6.45 us
    ppermute x6, waiting for transfers between devices, pair_exchange(): return lax.ppermute(value, ('sx', 'sy'), pairs)  1.37 us
    all_to_all x1, waiting for transfers between devices, local(): group = lax.all_to_all(tokens, 'sy', 0, 0)  1.28 us
    unnamed x22, local copies, waits for them, and re-layouts  1 us
    concatenate x1, other arithmetic, local(): marks = jnp.concatenate([occupancy, adjacency], axis=1)  0.81 us
  transfers between devices with their start and end apart: 7, of which 2 were waited for; matrix products, arithmetic and copies ran while one was open for 0% of the time, Pallas kernels for 14%

profile of v2, /device:TPU:1, one launch (start us, length us, event | category | flops | bytes accessed | tf_op | source)
XLA Modules:
  0.0 30.0 jit_solution(1166890301670545303)
XLA Ops:
  0.0 0.8 %pad_add_fusion.marks = s32[32,91]{1,0:T(8,128)S(1)} fusion(s32[32,27]{1,0:T(8,128)} %param.15, s32[32,64]{1,0:T(8,128)} %param.14), kind=kLoop, calls=%fused_computation | loop fusion | flops 2912 | bytes 23296 | tf_op jit(solution)/shard_map/concatenate | solution.py:568
  0.8 0.0 copy-start
  0.8 0.9 %copy-done = bf16[32,4096]{1,0:T(8,128)(2,1)S(1)} copy-done((bf16[32,4096]{1,0:T(8,128)(2,1)S(1)}, bf16[32,4096]{1,0:T(8,128)(2,1)}, u32[]{:S(2)}) %copy-start) | copy-done | bytes 262168
  1.8 1.0 %shard_map.127 = (bf16[32,4096]{1,0:T(8,128)(2,1)S(1)}, bf16[32,4096]{1,0:T(8,128)(2,1)S(1)}, bf16[16,16,128]{2,1,0:T(8,128)(2,1)}, bf16[32,256]{1,0:T(8,128)(2,...) custom-call(bf16[32,4096]{1,0:T(8,128)(2,1)S(1)} %copy-done, ...), custom_call_target="tpu_custom_call" | custom-call | bytes 2097152 | tf_op jit(solution)/shard_map/pallas_call | solution.py:22
  2.8 2.1 %collective-permute-start = (bf16[32,2304]{1,0:T(8,128)(2,1)S(1)}, bf16[32,2304]{1,0:T(8,128)(2,1)S(1)}, u32[]{:S(2)}, u32[]{:S(2)}) collective-permute-start(bf16[32,2304]{1,0:T(8,128)(2,1)S(1)} %get-tuple-element.23), channel_id=1, source_target_pairs={{0,1},{1,0},{2,3},{3,2},{4,5},{5,4},{6,7},{7,6},{8,9},{9,8},{10,11... | collective-permute-start | bytes 442376 | tf_op jit(solution)/shard_map/ppermute | solution.py:72
  4.8 1.0 %collective-permute-start.1 = (bf16[32,2304]{1,0:T(8,128)(2,1)S(1)}, bf16[32,2304]{1,0:T(8,128)(2,1)S(1)}, u32[]{:S(2)}, u32[]{:S(2)}) collective-permute-start(bf16[32,2304]{1,0:T(8,128)(2,1)S(1)} %get-tuple-element.24), channel_id=1, source_target_pairs={{0,16},{1,2},{2,1},{3,4},{4,3},{5,6},{6,5},{7,8},{8,7},{9,10},{10,... | collective-permute-start | bytes 442376 | tf_op jit(solution)/shard_map/ppermute | solution.py:72
  5.8 6.5 %all-to-all-start = ((bf16[16,16,128]{2,1,0:T(8,128)(2,1)}), bf16[16,16,128]{2,1,0:T(8,128)(2,1)S(1)}, u32[]{:S(2)}, u32[]{:S(2)}) async-start(bf16[16,16,128]{2,1,0:T(8,128)(2,1)} %get-tuple-element.30), calls=%async_computation | async-start | bytes 131072 | tf_op jit(solution)/shard_map/all_to_all | solution.py:581
  12.2 0.0 collective-permute-done.t0
  12.2 0.0 collective-permute-done.1.t1
  12.3 0.0 copy-start.5
  12.3 1.6 %collective-permute-start.2 = (bf16[32,2048]{1,0:T(8,128)(2,1)S(1)}, bf16[32,2048]{1,0:T(8,128)(2,1)S(1)}, u32[]{:S(2)}, u32[]{:S(2)}) collective-permute-start(bf16[32,2048]{1,0:T(8,128)(2,1)S(1)} %get-tuple-element.25), channel_id=1, source_target_pairs={{0,16},{1,17},{2,18},{3,19},{4,20},{5,21},{6,22},{7,23},{8,24},{9,... | collective-permute-start | bytes 393224 | tf_op jit(solution)/shard_map/ppermute | solution.py:72
  13.9 1.6 %collective-permute-start.3 = (bf16[32,2048]{1,0:T(8,128)(2,1)S(1)}, bf16[32,2048]{1,0:T(8,128)(2,1)S(1)}, u32[]{:S(2)}, u32[]{:S(2)}) collective-permute-start(bf16[32,2048]{1,0:T(8,128)(2,1)S(1)} %get-tuple-element.26), channel_id=1, source_target_pairs={{0,1},{1,0},{2,3},{3,2},{4,5},{5,4},{6,7},{7,6},{8,9},{9,8},{10,11... | collective-permute-start | bytes 393224 | tf_op jit(solution)/shard_map/ppermute | solution.py:72
  15.5 0.0 copy-done.5
  15.5 0.0 copy-start.7
  15.5 0.0 copy-start.8
  15.5 0.0 copy-start.9
  15.5 0.0 copy-start.10
  15.5 0.0 copy-start.1
  15.6 0.0 copy-start.2
  15.6 1.9 %shard_map.129 = (f32[4,128,256]{2,1,0:T(8,128)S(1)}, f32[4,64,256]{2,1,0:T(8,128)S(1)}, bf16[6,384,256]{2,1,0:T(8,128)(2,1)S(1)}) custom-call(bf16[32,4096]{1,0:T(8,128)(2,1)S(1)} %get-tuple-element.22.masked, bf16[32,2304]{1,0:T(8,128)(2,1)S(1)} %collective-permute-done.t0, bf16[32,2304]{1,0:T(8,128)(2,1)S(1)} %collective-permute-done.1.t1, ...), custom_call_target="tpu_custom_call" | custom-call | flops 2147483648 | bytes 2097152 | tf_op jit(solution)/shard_map/pallas_call | solution.py:22
  17.5 1.3 %all-to-all-done.group = bf16[16,16,128]{2,1,0:T(8,128)(2,1)S(1)} async-done(((bf16[16,16,128]{2,1,0:T(8,128)(2,1)}), bf16[16,16,128]{2,1,0:T(8,128)(2,1)S(1)}, u32[]{:S(2)}, u32[]{:S(2)}) %all-to-all-start) | async-done | bytes 65568 | tf_op jit(solution)/shard_map/all_to_all | solution.py:581
  18.7 0.0 copy-done.7
  18.8 0.0 copy-done.8
  18.8 0.0 copy-done.9
  18.8 0.0 copy-done.10
  18.8 1.0 %shard_map.130.term = f32[96,256]{1,0:T(8,128)S(1)} custom-call(bf16[16,16,128]{2,1,0:T(8,128)(2,1)S(1)} %all-to-all-done.group, bf16[64,64]{1,0:T(8,128)(2,1)S(1)} %copy-done.7, bf16[64,64]{1,0:T(8,128)(2,1)S(1)} %copy-done.8, bf16[64,64]{1,0:T(8,128)(2,1)S(1)} %copy-done.9, bf16[64,64]{1,0:T(8,128)(2,1)S(1)} %copy-done.10), custom_call_target="tpu_custom_call" | custom-call | flops 67108864 | bytes 1048576 | tf_op jit(solution)/shard_map/pallas_call | solution.py:22
  19.8 0.0 collective-permute-done.2.r0
  19.8 0.0 collective-permute-done.3.r1
  19.8 0.0 copy-done.1
  19.8 0.0 copy-done.2
  19.9 0.0 copy-start.6
  19.9 1.8 %shard_map.131 = (bf16[32,1536]{1,0:T(8,128)(2,1)S(1)}, bf16[32,1536]{1,0:T(8,128)(2,1)S(1)}) custom-call(bf16[32,4096]{1,0:T(8,128)(2,1)S(1)} %get-tuple-element.22.masked, bf16[32,2048]{1,0:T(8,128)(2,1)S(1)} %collective-permute-done.2.r0, bf16[32,2048]{1,0:T(8,128)(2,1)S(1)} %collective-permute-done.3.r1, bf16[32,2304]{1,0:T(8,128)(2,1)S(1)} %collective-permute-done.t0, ...), custom_call_target="tpu_custom_call" | custom-call | flops 679477248 | bytes 4194304 | tf_op jit(solution)/shard_map/pallas_call | solution.py:22
  21.7 2.7 %collective-permute-start.4 = (bf16[32,1536]{1,0:T(8,128)(2,1)S(1)}, bf16[32,1536]{1,0:T(8,128)(2,1)S(1)}, u32[]{:S(2)}, u32[]{:S(2)}) collective-permute-start(bf16[32,1536]{1,0:T(8,128)(2,1)S(1)} %get-tuple-element.35.xs0), channel_id=1, source_target_pairs={{0,16},{1,17},{2,18},{3,19},{4,20},{5,21},{6,22},{7,23},{8,24},{9,... | collective-permute-start | bytes 294920 | tf_op jit(solution)/shard_map/ppermute | solution.py:72
  24.3 0.0 copy-start.3
  24.3 0.0 copy-start.4
  24.3 1.6 %collective-permute-start.5 = (bf16[32,1536]{1,0:T(8,128)(2,1)S(1)}, bf16[32,1536]{1,0:T(8,128)(2,1)S(1)}, u32[]{:S(2)}, u32[]{:S(2)}) collective-permute-start(bf16[32,1536]{1,0:T(8,128)(2,1)S(1)} %get-tuple-element.36.xs1), channel_id=1, source_target_pairs={{0,1},{1,0},{2,3},{3,2},{4,5},{5,4},{6,7},{7,6},{8,9},{9,8},{10,11... | collective-permute-start | bytes 294920 | tf_op jit(solution)/shard_map/ppermute | solution.py:72
  26.0 0.0 copy-done.6
  26.0 1.3 %shard_map.132 = (f32[4,128,256]{2,1,0:T(8,128)S(1)}, bf16[6,384,256]{2,1,0:T(8,128)(2,1)S(1)}) custom-call(f32[4,128,256]{2,1,0:T(8,128)S(1)} %get-tuple-element.33.acc, f32[4,64,256]{2,1,0:T(8,128)S(1)} %get-tuple-element.34.acc_side, f32[1,64]{1,0:T(1,128)S(1)} %bitcast.5, f32[1,64]{1,0:T(1,128)S(1)} %bitcast.7, ...), custom_call_target="tpu_custom_call" | custom-call | flops 8589934592 | bytes 4194304 | tf_op jit(solution)/shard_map/pallas_call | solution.py:22
  27.3 0.0 collective-permute-done.4.r0
  27.3 1.4 %collective-permute-done.5.r1 = bf16[32,1536]{1,0:T(8,128)(2,1)S(1)} collective-permute-done((bf16[32,1536]{1,0:T(8,128)(2,1)S(1)}, bf16[32,1536]{1,0:T(8,128)(2,1)S(1)}, u32[]{:S(2)}, u32[]{:S(2)}) %collective-permute-start.5) | collective-permute-done | bytes 98336 | tf_op jit(solution)/shard_map/ppermute | solution.py:72
  28.7 0.0 copy-done.3
  28.7 0.0 copy-done.4
  28.7 1.4 %shard_map.133 = bf16[32,4096]{1,0:T(8,128)(2,1)} custom-call(bf16[32,1536]{1,0:T(8,128)(2,1)S(1)} %get-tuple-element.35.xs0, bf16[32,1536]{1,0:T(8,128)(2,1)S(1)} %get-tuple-element.36.xs1, bf16[32,1536]{1,0:T(8,128)(2,1)S(1)} %collective-permute-done.4.r0, bf16[32,1536]{1,0:T(8,128)(2,1)S(1)} %collective-permute-done.5.r1, ...), custom_call_target="tpu_custom_call" | custom-call | flops 150994944 | bytes 3145728 | tf_op jit(solution)/shard_map/pallas_call | solution.py:22
  (1 shorter events, 0.0 us)
Async XLA Ops:
  0.8 1.0 %copy-start = (bf16[32,4096]{1,0:T(8,128)(2,1)S(1)}, bf16[32,4096]{1,0:T(8,128)(2,1)}, u32[]{:S(2)}) copy-start(bf16[32,4096]{1,0:T(8,128)(2,1)} %feat.1) | copy-start | bytes 786436
  2.8 9.5 %collective-permute-start = (bf16[32,2304]{1,0:T(8,128)(2,1)S(1)}, bf16[32,2304]{1,0:T(8,128)(2,1)S(1)}, u32[]{:S(2)}, u32[]{:S(2)}) collective-permute-start(bf16[32,2304]{1,0:T(8,128)(2,1)S(1)} %get-tuple-element.23), channel_id=1, source_target_pairs={{0,1},{1,0},{2,3},{3,2},{4,5},{5,4},{6,7},{7,6},{8,9},{9,8},{10,11... | collective-permute-start | bytes 442376 | tf_op jit(solution)/shard_map/ppermute | solution.py:72
  4.8 7.4 %collective-permute-start.1 = (bf16[32,2304]{1,0:T(8,128)(2,1)S(1)}, bf16[32,2304]{1,0:T(8,128)(2,1)S(1)}, u32[]{:S(2)}, u32[]{:S(2)}) collective-permute-start(bf16[32,2304]{1,0:T(8,128)(2,1)S(1)} %get-tuple-element.24), channel_id=1, source_target_pairs={{0,16},{1,2},{2,1},{3,4},{4,3},{5,6},{6,5},{7,8},{8,7},{9,10},{10,... | collective-permute-start | bytes 442376 | tf_op jit(solution)/shard_map/ppermute | solution.py:72
  5.8 13.0 %all-to-all-start = ((bf16[16,16,128]{2,1,0:T(8,128)(2,1)}), bf16[16,16,128]{2,1,0:T(8,128)(2,1)S(1)}, u32[]{:S(2)}, u32[]{:S(2)}) async-start(bf16[16,16,128]{2,1,0:T(8,128)(2,1)} %get-tuple-element.30), calls=%async_computation | async-start | bytes 131072 | tf_op jit(solution)/shard_map/all_to_all | solution.py:581
  12.3 3.3 %copy-start.5 = (bf16[27,64,64]{2,1,0:T(8,128)(2,1)S(1)}, bf16[27,64,64]{2,1,0:T(8,128)(2,1)}, u32[]{:S(2)}) copy-start(bf16[27,64,64]{2,1,0:T(8,128)(2,1)} %weight.2) | copy-start | bytes 663556
  12.3 7.5 %collective-permute-start.2 = (bf16[32,2048]{1,0:T(8,128)(2,1)S(1)}, bf16[32,2048]{1,0:T(8,128)(2,1)S(1)}, u32[]{:S(2)}, u32[]{:S(2)}) collective-permute-start(bf16[32,2048]{1,0:T(8,128)(2,1)S(1)} %get-tuple-element.25), channel_id=1, source_target_pairs={{0,16},{1,17},{2,18},{3,19},{4,20},{5,21},{6,22},{7,23},{8,24},{9,... | collective-permute-start | bytes 393224 | tf_op jit(solution)/shard_map/ppermute | solution.py:72
  13.9 5.9 %collective-permute-start.3 = (bf16[32,2048]{1,0:T(8,128)(2,1)S(1)}, bf16[32,2048]{1,0:T(8,128)(2,1)S(1)}, u32[]{:S(2)}, u32[]{:S(2)}) collective-permute-start(bf16[32,2048]{1,0:T(8,128)(2,1)S(1)} %get-tuple-element.26), channel_id=1, source_target_pairs={{0,1},{1,0},{2,3},{3,2},{4,5},{5,4},{6,7},{7,6},{8,9},{9,8},{10,11... | collective-permute-start | bytes 393224 | tf_op jit(solution)/shard_map/ppermute | solution.py:72
  15.5 3.2 %copy-start.7 = (bf16[64,64]{1,0:T(8,128)(2,1)S(1)}, bf16[64,64]{1,0:T(8,128)(2,1)}, u32[]{:S(2)}) copy-start(bf16[64,64]{1,0:T(8,128)(2,1)} %w_key.1) | copy-start | bytes 24580
  15.5 3.2 %copy-start.8 = (bf16[64,64]{1,0:T(8,128)(2,1)S(1)}, bf16[64,64]{1,0:T(8,128)(2,1)}, u32[]{:S(2)}) copy-start(bf16[64,64]{1,0:T(8,128)(2,1)} %w_value.1) | copy-start | bytes 24580
  15.5 3.2 %copy-start.9 = (bf16[64,64]{1,0:T(8,128)(2,1)S(1)}, bf16[64,64]{1,0:T(8,128)(2,1)}, u32[]{:S(2)}) copy-start(bf16[64,64]{1,0:T(8,128)(2,1)} %w_query.1) | copy-start | bytes 24580
  15.5 3.2 %copy-start.10 = (bf16[64,64]{1,0:T(8,128)(2,1)S(1)}, bf16[64,64]{1,0:T(8,128)(2,1)}, u32[]{:S(2)}) copy-start(bf16[64,64]{1,0:T(8,128)(2,1)} %w_out.1) | copy-start | bytes 24580
  15.5 4.3 %copy-start.1 = (f32[64]{0:T(128)S(1)}, f32[64]{0:T(128)}, u32[]{:S(2)}) copy-start(f32[64]{0:T(128)} %param.18) | copy-start | bytes 772
  15.6 4.3 %copy-start.2 = (f32[64]{0:T(128)S(1)}, f32[64]{0:T(128)}, u32[]{:S(2)}) copy-start(f32[64]{0:T(128)} %param.19) | copy-start | bytes 772
  19.9 6.1 %copy-start.6 = (bf16[27,64,64]{2,1,0:T(8,128)(2,1)S(1)}, bf16[27,64,64]{2,1,0:T(8,128)(2,1)}, u32[]{:S(2)}) copy-start(bf16[27,64,64]{2,1,0:T(8,128)(2,1)} %weight.3) | copy-start | bytes 663556
  21.7 5.6 %collective-permute-start.4 = (bf16[32,1536]{1,0:T(8,128)(2,1)S(1)}, bf16[32,1536]{1,0:T(8,128)(2,1)S(1)}, u32[]{:S(2)}, u32[]{:S(2)}) collective-permute-start(bf16[32,1536]{1,0:T(8,128)(2,1)S(1)} %get-tuple-element.35.xs0), channel_id=1, source_target_pairs={{0,16},{1,17},{2,18},{3,19},{4,20},{5,21},{6,22},{7,23},{8,24},{9,... | collective-permute-start | bytes 294920 | tf_op jit(solution)/shard_map/ppermute | solution.py:72
  24.3 4.3 %copy-start.3 = (f32[64]{0:T(128)S(1)}, f32[64]{0:T(128)}, u32[]{:S(2)}) copy-start(f32[64]{0:T(128)} %param.20) | copy-start | bytes 772
  24.3 4.3 %copy-start.4 = (f32[64]{0:T(128)S(1)}, f32[64]{0:T(128)}, u32[]{:S(2)}) copy-start(f32[64]{0:T(128)} %param.21) | copy-start | bytes 772
  24.3 4.3 %collective-permute-start.5 = (bf16[32,1536]{1,0:T(8,128)(2,1)S(1)}, bf16[32,1536]{1,0:T(8,128)(2,1)S(1)}, u32[]{:S(2)}, u32[]{:S(2)}) collective-permute-start(bf16[32,1536]{1,0:T(8,128)(2,1)S(1)} %get-tuple-element.36.xs1), channel_id=1, source_target_pairs={{0,1},{1,0},{2,3},{3,2},{4,5},{5,4},{6,7},{7,6},{8,9},{9,8},{10,11... | collective-permute-start | bytes 294920 | tf_op jit(solution)/shard_map/ppermute | solution.py:72

commit v3 on v2

--- a/solution.py
+++ b/solution.py
@@ -80,17 +80,54 @@
     return (dx * lax.axis_size("sy") + dy) * BRICKS
 
 
-def one_hot(ids, offsets, bases):
-    lane = lax.broadcasted_iota(jnp.int32, (BRICKS, 32 * len(bases)), 1)
-    candidate = jnp.bitwise_and(lane, 31) + bases[0]
-    for k in range(1, len(bases)):
-        slot = lax.shift_right_logical(lane, 5) == k
-        candidate = candidate + jnp.where(slot, bases[k] - bases[0], 0)
+def device_row(base):
+    return jnp.bitwise_and(lax.broadcasted_iota(jnp.int32, (1, BRICKS), 1), BRICKS - 1) + base
+
+
+def one_hot(ids, offsets, candidates):
+    candidate = candidates[0]
+    if len(candidates) > 1:
+        candidate = jnp.concatenate(candidates, axis=1)
+    candidate = jnp.broadcast_to(candidate, (BRICKS, candidate.shape[1]))
     rows = [
         (ids[:, o : o + 1] == candidate).astype(f32).astype(bf16)
         for o in ((ox + 1) * 9 + (oy + 1) * 3 + (oz + 1) for ox, oy, oz in offsets)
     ]
     return jnp.concatenate(rows, axis=0)
+
+
+def owner_marks(ids, base):
+    hit = jnp.logical_and(ids >= base, ids < base + BRICKS)
+    return jnp.max(hit.astype(f32), axis=1, keepdims=True)
+
+
+def compaction(marks, slots):
+    row = lax.broadcasted_iota(jnp.int32, (BRICKS, BRICKS), 0)
+    lane = lax.broadcasted_iota(jnp.int32, (BRICKS, BRICKS), 1)
+    rank = jnp.sum(jnp.where(row < lane, marks, 0.0), axis=0, keepdims=True)
+    marked = jnp.sum(jnp.where(row == lane, marks, 0.0), axis=0, keepdims=True)
+    slot = lax.broadcasted_iota(jnp.int32, (slots, BRICKS), 0).astype(f32)
+    return jnp.where(slot == rank, marked, 0.0)
+
+
+def slot_ids(ids, base, offsets, slots):
+    candidate = jnp.broadcast_to(device_row(base), (BRICKS, BRICKS))
+    hit = jnp.zeros((BRICKS, BRICKS), f32)
+    for ox, oy, oz in offsets:
+        o = (ox + 1) * 9 + (oy + 1) * 3 + (oz + 1)
+        hit = jnp.maximum(hit, (ids[:, o : o + 1] == candidate).astype(f32))
+    marked = jnp.broadcast_to(jnp.max(hit, axis=0, keepdims=True), (8, BRICKS))
+    row = lax.broadcasted_iota(jnp.int32, (BRICKS, BRICKS), 0)
+    lane = lax.broadcasted_iota(jnp.int32, (BRICKS, BRICKS), 1)
+    before = (row < lane).astype(f32).astype(bf16)
+    rank = jnp.dot(marked.astype(bf16), before, preferred_element_type=f32)
+    slot = lax.broadcasted_iota(jnp.int32, (slots, BRICKS), 0).astype(f32)
+    pack = jnp.where(slot == rank[:1], marked[:1], 0.0).astype(bf16)
+    count = lax.broadcasted_iota(jnp.int32, (8, BRICKS), 1).astype(f32) + 1.0
+    local_id = lax.dot_general(
+        count.astype(bf16), pack, (((1,), (1,)), ((), ())), preferred_element_type=f32
+    ).astype(jnp.int32)
+    return jnp.where(local_id > 0, local_id - 1 + base, 2 * FAR)
 
 
 def put_column(select, parts, core, store):
@@ -202,13 +239,14 @@
 def own_select(ids, ox, oy):
     base = device_base()
     offsets = [(ox, oy, oz) for oz in ((1, -1) if ox == 0 and oy == 0 else (1, -1, 0))]
-    return one_hot(ids, offsets, [base + id_step(dx, dy) for dx, dy in sources_of(ox, oy)])
+    return one_hot(ids, offsets, [device_row(base + id_step(dx, dy)) for dx, dy in sources_of(ox, oy)])
 
 
 def side_select(ids, side, ox):
     here, there = device_base(), device_base() + id_step(0, side)
-    outer = [here] if ox == 0 else [here, here + id_step(ox, 0)]
-    inner = [there] if ox == 0 else [there, there + id_step(ox, 0)]
+    bases = [0] if ox == 0 else [0, id_step(ox, 0)]
+    outer = [device_row(here + step) for step in bases]
+    inner = [device_row(there + step) for step in bases]
     offsets = [(ox, 0, oz) for oz in ((1, -1) if ox == 0 else (1, -1, 0))]
     return (
         one_hot(ids, offsets, inner),
@@ -363,7 +401,7 @@
     return jnp.where(number < 0, FAR, number)
 
 
-def attention_kernel(group, w_key, w_value, w_query, w_out, term):
+def global_term(group, w_key, w_value, w_query, w_out):
     count = group.shape[0]
     here = lax.axis_index("sy")
     tokens = []
@@ -372,11 +410,15 @@
         tokens += [packed[:, :C], packed[:, C:]]
     packed = group[...].reshape(-1, 2 * C)
     tokens = jnp.concatenate(tokens, axis=0)
-    term[...] = attention(tokens, packed, w_key[...], w_value[...], w_query[...], w_out[...])
+    return attention(tokens, packed, w_key[...], w_value[...], w_query[...], w_out[...])
+
+
+FACE_SLOTS, SIDE_SLOTS = 16, 8
 
 
 def near_kernel(
-    masked, t0, t1, ids_ref, weight, acc, acc_side, band_edge, inner, side_inner, band
+    masked, t0, t1, ids_ref, weight, acc, acc_side, band_edge, pack, slots, inner, side_inner,
+    band,
 ):
     from_message = y_reader(t0, t1)
     ids = ids_ref[...]
@@ -389,12 +431,22 @@
 
     fill_band(weight, band)
     gather_own(own, None, from_y, None, lambda ox, oy: own_select(ids, ox, oy), inner, (0,))
+    numbers = {}
     for side in (-1, 1):
-        number = side_ids(from_message(side, META))
+        number = numbers[side] = side_ids(from_message(side, META))
         gather_side(
             own, None, from_message, side,
             lambda side, ox, number=number: side_select(number, side, ox), side_inner, (0,),
         )
+
+    base = device_base()
+    for k, ox in enumerate((-1, 1)):
+        face = [(ox, oy, oz) for oy in (-1, 0, 1) for oz in (-1, 0, 1)]
+        parts = [slot_ids(ids, base + id_step(ox, 0), face, FACE_SLOTS)]
+        for oy in (-1, 1):
+            corner = [(ox, oy, oz) for oz in (-1, 0, 1)]
+            parts.append(slot_ids(ids, base + id_step(ox, oy), corner, SIDE_SLOTS))
+        slots[k, :, : FACE_SLOTS + 2 * SIDE_SLOTS] = jnp.concatenate(parts, axis=1)
 
     def store(x_range, value):
         count = len(x_range)
@@ -406,6 +458,15 @@
     convolve_inner(inner, side_inner, band, store)
     band_edge[:3] = band[:3]
     band_edge[3:] = band[6:]
+    for k, ox in enumerate((-1, 1)):
+        there = device_base() + id_step(ox, 0)
+        pack[2 * k, :, :BRICKS] = compaction(owner_marks(ids, there), FACE_SLOTS).astype(bf16)
+        sides = [compaction(owner_marks(numbers[side], there), SIDE_SLOTS) for side in (-1, 1)]
+        gap = jnp.zeros_like(sides[0])
+        low = jnp.concatenate([sides[0], gap], axis=1)
+        high = jnp.concatenate([gap, sides[1]], axis=1)
+        both = jnp.concatenate([low, high], axis=0)
+        pack[2 * k + 1, :, : 2 * BRICKS] = both.astype(bf16)
 
 
 def finish(acc, acc_side, x, gain, offset, cover, from_message, term, store, store_side):
@@ -426,12 +487,14 @@
 
 
 def first_edge_kernel(
-    masked, r0, r1, t0, t1, ids_ref, band_edge, scale, shift, cover, term, acc, acc_side,
-    xs0, xs1, outer, side_outer,
+    masked, r0, r1, t0, t1, ids_ref, band_edge, scale, shift, cover, acc, acc_side,
+    group, w_key, w_value, w_query, w_out, pack, edges, m0, m1, term_out, outer, side_outer,
 ):
     even_x, _ = parities()
     from_message, from_x = y_reader(t0, t1), x_reader(r0, r1)
     ids = ids_ref[...]
+    term = global_term(group, w_key, w_value, w_query, w_out)
+    term_out[...] = term
 
     def own(x, y):
         return masked[:, column(x, y)]
@@ -453,15 +516,7 @@
         )
 
     def put(x, k, value):
-        lanes = slice(k * COL, (k + 1) * COL)
-
-        @pl.when(even_x == (x == 3))
-        def _():
-            xs0[:, lanes] = value
-
-        @pl.when(even_x != (x == 3))
-        def _():
-            xs1[:, lanes] = value
+        edges[0 if x == 0 else 1, :, k * COL : (k + 1) * COL] = value
 
     for x in (0, 3):
         more = convolve_edge(outer, side_outer, band_edge, x)
@@ -470,24 +525,29 @@
             four(shift), cover, from_message, term,
             put, lambda x, side, value: put(x, 4 if side < 0 else 5, value),
         )
-
-
-def edge_reader(xs0, xs1):
-    even_x, _ = parities()
-
-    def edge(x, k):
-        lanes = slice(k * COL, (k + 1) * COL)
-        a, b = (xs0, xs1) if x == 3 else (xs1, xs0)
-        return pick(even_x, a[:, lanes], b[:, lanes])
-
-    return edge
+    messages = []
+    for n in range(2):
+        face = jnp.dot(
+            pack[2 * n, :, :BRICKS], edges[n, :, : 4 * COL], preferred_element_type=f32
+        )
+        sides = jnp.concatenate(
+            [edges[n, :, 4 * COL : 5 * COL], edges[n, :, 5 * COL :]], axis=0
+        )
+        side = jnp.dot(pack[2 * n + 1, :, : 2 * BRICKS], sides, preferred_element_type=f32)
+        messages.append(jnp.concatenate([face, side], axis=1).astype(bf16))
+    m0[...] = pick(even_x, messages[1], messages[0])
+    m1[...] = pick(even_x, messages[0], messages[1])
+
+
+def edge_reader(edges):
+    return lambda x, k: edges[0 if x == 0 else 1, :, k * COL : (k + 1) * COL]
 
 
 def middle_kernel(
-    acc, acc_side, scale, shift, cover, t0, t1, term, xs0, xs1, ids_ref, weight,
+    acc, acc_side, scale, shift, cover, t0, t1, term, edges, ids_ref, weight,
     acc_out, band_edge, mid, mid_side, padded, band,
 ):
-    edge = edge_reader(xs0, xs1)
+    edge = edge_reader(edges)
     from_message = y_reader(t0, t1)
     ids = ids_ref[...]
     fill_band(weight, band)
@@ -523,16 +583,33 @@
 
 
 def second_kernel(
-    xs0, xs1, r0, r1, ids_ref, band_edge, scale, shift, cover, masked, acc, refined, outer
+    edges, r0, r1, ids_ref, slots, band_edge, scale, shift, cover, masked, acc, refined, outer
 ):
-    edge, from_x = edge_reader(xs0, xs1), x_reader(r0, r1)
-    ids = ids_ref[...]
+    even_x, _ = parities()
+    edge, ids = edge_reader(edges), ids_ref[...]
+    base = device_base()
+
+    def received(ox, rows, k):
+        lanes = slice(k * COL, (k + 1) * COL)
+        a, b = (r1, r0) if ox < 0 else (r0, r1)
+        return pick(even_x, a[rows, lanes], b[rows, lanes])
+
+    def from_corner(ox, oy):
+        return received(ox, slice(None), 4)
+
+    def select_of(ox, oy):
+        known = slots[0 if ox < 0 else 1, :1, : FACE_SLOTS + 2 * SIDE_SLOTS]
+        candidates = [device_row(base), known[:, :FACE_SLOTS]]
+        if oy:
+            candidates += [device_row(base + id_step(0, oy)), known[:, FACE_SLOTS:]]
+        return one_hot(ids, [(ox, oy, oz) for oz in (1, -1, 0)], candidates)
+
     gather_own(
         edge,
-        from_x,
+        lambda ox, y: received(ox, slice(None), y),
         lambda oy, x: edge(x, 4 if oy < 0 else 5),
-        lambda ox, oy: from_x(ox, 4 if oy < 0 else 5),
-        lambda ox, oy: own_select(ids, ox, oy),
+        from_corner,
+        select_of,
         outer,
         (-1, 1),
     )
@@ -557,7 +634,7 @@
     scale_two, shift_two, w_query, w_key, w_value, w_out,
 ):
     n_sy = lax.axis_size("sy")
-    whole, edge = shape(BRICKS, 64 * C), shape(BRICKS, 6 * COL)
+    whole = shape(BRICKS, 64 * C)
     band_edge = shape(6, TAP, COL)
     own_acc, side_acc = shape(4, 4 * BRICKS, COL, dtype=f32), shape(4, 2 * BRICKS, COL, dtype=f32)
     band = pltpu.VMEM((9, TAP, COL), bf16)
@@ -584,38 +661,39 @@
         message_kernel, [x_message] * 2, (masked, t0, t1), flops=1 << 35, bytes_accessed=1 << 20
     )
     r0, r1 = exchange(x0, x1, "sx")
-    acc, acc_side, band_one = call(
+    acc, acc_side, band_one, pack, slots = call(
         near_kernel,
-        [own_acc, side_acc, band_edge],
+        [
+            own_acc, side_acc, band_edge, shape(4, FACE_SLOTS, 128),
+            shape(2, 8, 128, dtype=jnp.int32),
+        ],
         (masked, t0, t1, ids, conv_one),
         [inner, side_inner, band],
-        flops=1 << 31,
+        flops=1 << 33,
         bytes_accessed=2 << 20,
     )
     group, acc = lax.optimization_barrier((group, acc))
-    term = call(
-        attention_kernel,
-        shape(3 * BRICKS, COL, dtype=f32),
-        (group, w_key, w_value, w_query, w_out),
-        flops=1 << 26,
-        bytes_accessed=1 << 20,
-    )
-    xs0, xs1 = call(
+    out_message = shape(FACE_SLOTS, 5 * COL)
+    edges, m0, m1, term = call(
         first_edge_kernel,
-        [edge, edge],
+        [
+            shape(2, BRICKS, 6 * COL), out_message, out_message,
+            shape(3 * BRICKS, COL, dtype=f32),
+        ],
         (
-            masked, r0, r1, t0, t1, ids, band_one, rows[0], rows[1], cover, term, acc, acc_side,
+            masked, r0, r1, t0, t1, ids, band_one, rows[0], rows[1], cover, acc, acc_side,
+            group, w_key, w_value, w_query, w_out, pack,
         ),
         [outer, side_outer],
         flops=2 * 384 * 3456 * 256,
         bytes_accessed=4 << 20,
     )
-    r0, r1 = exchange(xs0, xs1, "sx")
+    r0, r1 = exchange(m0, m1, "sx")
     acc, band_two = call(
         middle_kernel,
         [own_acc, band_edge],
         (
-            acc, acc_side, rows[0], rows[1], cover, t0, t1, term, xs0, xs1, ids, conv_two,
+            acc, acc_side, rows[0], rows[1], cover, t0, t1, term, edges, ids, conv_two,
         ),
         [
             pltpu.VMEM((2, 4, BRICKS, COL), bf16),
@@ -629,7 +707,9 @@
     return call(
         second_kernel,
         whole,
-        (xs0, xs1, r0, r1, ids, band_two, rows[2], rows[3], cover, masked, acc),
+        (
+            edges, r0, r1, ids, slots, band_two, rows[2], rows[3], cover, masked, acc,
+        ),
         [outer],
         flops=2 * 256 * 1152 * 256,
         bytes_accessed=3 << 20,

time: 30.4 us -> 28.9 us (0.951)
  waiting for transfers between devices: 2.65 us -> 1.72 us
  Pallas kernels: 8.47 us -> 7.85 us
    ppermute x6, waiting for transfers between devices: 1.37 us -> 0.73 us  [pair_exchange(): return lax.ppermute(value, ('sx', 'sy'), pairs)]
    pallas_call x7 -> x6, Pallas kernels: 8.47 us -> 7.85 us  [call(): pl.pallas_call(kernel, out_shape=out_shape, in_specs=[vmem] * len(args),...]
  transfers between devices with their start and end apart: 7 -> 7, of which waited for: 2 -> 2; matrix products, arithmetic and copies ran while one was open for 0% -> 0% of each run, Pallas kernels for 14% -> 12%
where the time goes in v3:
time: 28.9 us; the launch traced here: 28.6 us
  starting transfers between devices  17 us (59%)
  Pallas kernels  7.85 us (27%)
  waiting for transfers between devices  1.72 us (6%)
  local copies, waits for them, and re-layouts  1 us (3%)
  other arithmetic  0.81 us (3%)
    ppermute x6, starting transfers between devices, pair_exchange(): return lax.ppermute(value, ('sx', 'sy'), pairs)  10.6 us
    pallas_call x6, Pallas kernels, call(): pl.pallas_call(kernel, out_shape=out_shape, in_specs=[vmem] * len(args),...  7.85 us
    all_to_all x1, starting transfers between devices, local(): group = lax.all_to_all(tokens, 'sy', 0, 0)  6.45 us
    unnamed x22, local copies, waits for them, and re-layouts  1 us
    all_to_all x1, waiting for transfers between devices, local(): group = lax.all_to_all(tokens, 'sy', 0, 0)  0.99 us
    concatenate x1, other arithmetic, local(): marks = jnp.concatenate([occupancy, adjacency], axis=1)  0.81 us
    ppermute x6, waiting for transfers between devices, pair_exchange(): return lax.ppermute(value, ('sx', 'sy'), pairs)  0.73 us
  transfers between devices with their start and end apart: 7, of which 2 were waited for; matrix products, arithmetic and copies ran while one was open for 0% of the time, Pallas kernels for 12%

profile of v3, /device:TPU:1, one launch (start us, length us, event | category | flops | bytes accessed | tf_op | source)
XLA Modules:
  0.0 28.6 jit_solution(3575621607401142099)
XLA Ops:
  0.0 0.8 %pad_add_fusion.marks = s32[32,91]{1,0:T(8,128)S(1)} fusion(s32[32,27]{1,0:T(8,128)} %param.15, s32[32,64]{1,0:T(8,128)} %param.14), kind=kLoop, calls=%fused_computation | loop fusion | flops 2912 | bytes 23296 | tf_op jit(solution)/shard_map/concatenate | solution.py:645
  0.8 0.0 copy-start
  0.8 0.9 %copy-done = bf16[32,4096]{1,0:T(8,128)(2,1)S(1)} copy-done((bf16[32,4096]{1,0:T(8,128)(2,1)S(1)}, bf16[32,4096]{1,0:T(8,128)(2,1)}, u32[]{:S(2)}) %copy-start) | copy-done | bytes 262168
  1.8 1.0 %shard_map.127 = (bf16[32,4096]{1,0:T(8,128)(2,1)S(1)}, bf16[32,4096]{1,0:T(8,128)(2,1)S(1)}, bf16[16,16,128]{2,1,0:T(8,128)(2,1)}, bf16[32,256]{1,0:T(8,128)(2,...) custom-call(bf16[32,4096]{1,0:T(8,128)(2,1)S(1)} %copy-done, ...), custom_call_target="tpu_custom_call" | custom-call | bytes 2097152 | tf_op jit(solution)/shard_map/pallas_call | solution.py:22
  2.8 2.1 %collective-permute-start = (bf16[32,2304]{1,0:T(8,128)(2,1)S(1)}, bf16[32,2304]{1,0:T(8,128)(2,1)S(1)}, u32[]{:S(2)}, u32[]{:S(2)}) collective-permute-start(bf16[32,2304]{1,0:T(8,128)(2,1)S(1)} %get-tuple-element.27), channel_id=1, source_target_pairs={{0,1},{1,0},{2,3},{3,2},{4,5},{5,4},{6,7},{7,6},{8,9},{9,8},{10,11... | collective-permute-start | bytes 442376 | tf_op jit(solution)/shard_map/ppermute | solution.py:72
  4.8 1.0 %collective-permute-start.1 = (bf16[32,2304]{1,0:T(8,128)(2,1)S(1)}, bf16[32,2304]{1,0:T(8,128)(2,1)S(1)}, u32[]{:S(2)}, u32[]{:S(2)}) collective-permute-start(bf16[32,2304]{1,0:T(8,128)(2,1)S(1)} %get-tuple-element.28), channel_id=1, source_target_pairs={{0,16},{1,2},{2,1},{3,4},{4,3},{5,6},{6,5},{7,8},{8,7},{9,10},{10,... | collective-permute-start | bytes 442376 | tf_op jit(solution)/shard_map/ppermute | solution.py:72
  5.8 6.5 %all-to-all-start = ((bf16[16,16,128]{2,1,0:T(8,128)(2,1)}), bf16[16,16,128]{2,1,0:T(8,128)(2,1)S(1)}, u32[]{:S(2)}, u32[]{:S(2)}) async-start(bf16[16,16,128]{2,1,0:T(8,128)(2,1)} %get-tuple-element.34), calls=%async_computation | async-start | bytes 131072 | tf_op jit(solution)/shard_map/all_to_all | solution.py:658
  12.2 0.0 collective-permute-done.t0
  12.2 0.0 collective-permute-done.1.t1
  12.3 0.0 copy-start.9
  12.3 1.6 %collective-permute-start.2 = (bf16[32,2048]{1,0:T(8,128)(2,1)S(1)}, bf16[32,2048]{1,0:T(8,128)(2,1)S(1)}, u32[]{:S(2)}, u32[]{:S(2)}) collective-permute-start(bf16[32,2048]{1,0:T(8,128)(2,1)S(1)} %get-tuple-element.29), channel_id=1, source_target_pairs={{0,16},{1,17},{2,18},{3,19},{4,20},{5,21},{6,22},{7,23},{8,24},{9,... | collective-permute-start | bytes 393224 | tf_op jit(solution)/shard_map/ppermute | solution.py:72
  13.9 1.6 %collective-permute-start.3 = (bf16[32,2048]{1,0:T(8,128)(2,1)S(1)}, bf16[32,2048]{1,0:T(8,128)(2,1)S(1)}, u32[]{:S(2)}, u32[]{:S(2)}) collective-permute-start(bf16[32,2048]{1,0:T(8,128)(2,1)S(1)} %get-tuple-element.30), channel_id=1, source_target_pairs={{0,1},{1,0},{2,3},{3,2},{4,5},{5,4},{6,7},{7,6},{8,9},{9,8},{10,11... | collective-permute-start | bytes 393224 | tf_op jit(solution)/shard_map/ppermute | solution.py:72
  15.5 0.0 copy-done.9
  15.5 0.0 copy-start.1
  15.5 0.0 copy-start.2
  15.5 0.0 copy-start.3
  15.5 0.0 copy-start.4
  15.5 0.0 copy-start.5
  15.6 0.0 copy-start.6
  15.6 2.2 %shard_map.129 = (f32[4,128,256]{2,1,0:T(8,128)S(1)}, f32[4,64,256]{2,1,0:T(8,128)S(1)}, bf16[6,384,256]{2,1,0:T(8,128)(2,1)S(1)}, bf16[4,16,128]{2,1,0:T(8,128)(2,1)S(1)}, s32[2,8,128]{2,1,0:T(8,128)S(1)}) custom-call(bf16[32,4096]{1,0:T(8,128)(2,1)S(1)} %get-tuple-element.26.masked, bf16[32,2304]{1,0:T(8,128)(2,1)S(1)} %collective-permute-done.t0, ...), custom_call_target="tpu_custom_call" | custom-call | flops 8589934592 | bytes 2097152 | tf_op jit(solution)/shard_map/pallas_call | solution.py:22
  17.8 1.0 %all-to-all-done.group = bf16[16,16,128]{2,1,0:T(8,128)(2,1)S(1)} async-done(((bf16[16,16,128]{2,1,0:T(8,128)(2,1)}), bf16[16,16,128]{2,1,0:T(8,128)(2,1)S(1)}, u32[]{:S(2)}, u32[]{:S(2)}) %all-to-all-start) | async-done | bytes 65568 | tf_op jit(solution)/shard_map/all_to_all | solution.py:658
  18.7 0.0 collective-permute-done.2.r0
  18.8 0.0 collective-permute-done.3.r1
  18.8 0.0 copy-done.1
  18.8 0.0 copy-done.2
  18.8 0.0 copy-done.3
  18.8 0.0 copy-done.4
  18.8 0.0 copy-done.5
  18.8 0.0 copy-done.6
  18.8 0.0 copy-start.10
  18.8 1.9 %shard_map.130 = (bf16[2,32,1536]{2,1,0:T(8,128)(2,1)S(1)}, bf16[16,1280]{1,0:T(8,128)(2,1)S(1)}, bf16[16,1280]{1,0:T(8,128)(2,1)S(1)}, f32[96,256]{1,0:T(8,128)S(1)}) custom-call(bf16[32,4096]{1,0:T(8,128)(2,1)S(1)} %get-tuple-element.26.masked, bf16[32,2048]{1,0:T(8,128)(2,1)S(1)} %collective-permute-done.2.r0, ...), custom_call_target="tpu_custom_call" | custom-call | flops 679477248 | bytes 4194304 | tf_op jit(solution)/shard_map/pallas_call | solution.py:22
  20.8 2.7 %collective-permute-start.4 = (bf16[16,1280]{1,0:T(8,128)(2,1)S(1)}, bf16[16,1280]{1,0:T(8,128)(2,1)S(1)}, u32[]{:S(2)}, u32[]{:S(2)}) collective-permute-start(bf16[16,1280]{1,0:T(8,128)(2,1)S(1)} %get-tuple-element.41), channel_id=1, source_target_pairs={{0,16},{1,17},{2,18},{3,19},{4,20},{5,21},{6,22},{7,23},{8,24},{9,... | collective-permute-start | bytes 122888 | tf_op jit(solution)/shard_map/ppermute | solution.py:72
  23.5 1.6 %collective-permute-start.5 = (bf16[16,1280]{1,0:T(8,128)(2,1)S(1)}, bf16[16,1280]{1,0:T(8,128)(2,1)S(1)}, u32[]{:S(2)}, u32[]{:S(2)}) collective-permute-start(bf16[16,1280]{1,0:T(8,128)(2,1)S(1)} %get-tuple-element.42), channel_id=1, source_target_pairs={{0,1},{1,0},{2,3},{3,2},{4,5},{5,4},{6,7},{7,6},{8,9},{9,8},{10,11... | collective-permute-start | bytes 122888 | tf_op jit(solution)/shard_map/ppermute | solution.py:72
  25.1 0.0 copy-done.10
  25.1 0.0 copy-start.7
  25.1 0.0 copy-start.8
  25.1 1.3 %shard_map.131 = (f32[4,128,256]{2,1,0:T(8,128)S(1)}, bf16[6,384,256]{2,1,0:T(8,128)(2,1)S(1)}) custom-call(f32[4,128,256]{2,1,0:T(8,128)S(1)} %get-tuple-element.36.acc, f32[4,64,256]{2,1,0:T(8,128)S(1)} %get-tuple-element.37.acc_side, f32[1,64]{1,0:T(1,128)S(1)} %bitcast.5, f32[1,64]{1,0:T(1,128)S(1)} %bitcast.7, ...), custom_call_target="tpu_custom_call" | custom-call | flops 8589934592 | bytes 4194304 | tf_op jit(solution)/shard_map/pallas_call | solution.py:22
  26.5 0.0 collective-permute-done.4.r0
  26.5 0.7 %collective-permute-done.5.r1 = bf16[16,1280]{1,0:T(8,128)(2,1)S(1)} collective-permute-done((bf16[16,1280]{1,0:T(8,128)(2,1)S(1)}, bf16[16,1280]{1,0:T(8,128)(2,1)S(1)}, u32[]{:S(2)}, u32[]{:S(2)}) %collective-permute-start.5) | collective-permute-done | bytes 40992 | tf_op jit(solution)/shard_map/ppermute | solution.py:72
  27.2 0.0 copy-done.7
  27.2 0.0 copy-done.8
  27.2 1.4 %shard_map.132 = bf16[32,4096]{1,0:T(8,128)(2,1)} custom-call(bf16[2,32,1536]{2,1,0:T(8,128)(2,1)S(1)} %get-tuple-element.40.edges, bf16[16,1280]{1,0:T(8,128)(2,1)S(1)} %collective-permute-done.4.r0, bf16[16,1280]{1,0:T(8,128)(2,1)S(1)} %collective-permute-done.5.r1, s32[32,27]{1,0:T(8,128)S(1)} %get-tuple-element.31.ids_ref, ...), custom_call_target="tpu_custom_call" | custom-call | flops 150994944 | bytes 3145728 | tf_op jit(solution)/shard_map/pallas_call | solution.py:22
  (1 shorter events, 0.0 us)
Async XLA Ops:
  0.8 1.0 %copy-start = (bf16[32,4096]{1,0:T(8,128)(2,1)S(1)}, bf16[32,4096]{1,0:T(8,128)(2,1)}, u32[]{:S(2)}) copy-start(bf16[32,4096]{1,0:T(8,128)(2,1)} %feat.1) | copy-start | bytes 786436
  2.8 9.5 %collective-permute-start = (bf16[32,2304]{1,0:T(8,128)(2,1)S(1)}, bf16[32,2304]{1,0:T(8,128)(2,1)S(1)}, u32[]{:S(2)}, u32[]{:S(2)}) collective-permute-start(bf16[32,2304]{1,0:T(8,128)(2,1)S(1)} %get-tuple-element.27), channel_id=1, source_target_pairs={{0,1},{1,0},{2,3},{3,2},{4,5},{5,4},{6,7},{7,6},{8,9},{9,8},{10,11... | collective-permute-start | bytes 442376 | tf_op jit(solution)/shard_map/ppermute | solution.py:72
  4.8 7.4 %collective-permute-start.1 = (bf16[32,2304]{1,0:T(8,128)(2,1)S(1)}, bf16[32,2304]{1,0:T(8,128)(2,1)S(1)}, u32[]{:S(2)}, u32[]{:S(2)}) collective-permute-start(bf16[32,2304]{1,0:T(8,128)(2,1)S(1)} %get-tuple-element.28), channel_id=1, source_target_pairs={{0,16},{1,2},{2,1},{3,4},{4,3},{5,6},{6,5},{7,8},{8,7},{9,10},{10,... | collective-permute-start | bytes 442376 | tf_op jit(solution)/shard_map/ppermute | solution.py:72
  5.8 13.0 %all-to-all-start = ((bf16[16,16,128]{2,1,0:T(8,128)(2,1)}), bf16[16,16,128]{2,1,0:T(8,128)(2,1)S(1)}, u32[]{:S(2)}, u32[]{:S(2)}) async-start(bf16[16,16,128]{2,1,0:T(8,128)(2,1)} %get-tuple-element.34), calls=%async_computation | async-start | bytes 131072 | tf_op jit(solution)/shard_map/all_to_all | solution.py:658
  12.3 3.3 %copy-start.9 = (bf16[27,64,64]{2,1,0:T(8,128)(2,1)S(1)}, bf16[27,64,64]{2,1,0:T(8,128)(2,1)}, u32[]{:S(2)}) copy-start(bf16[27,64,64]{2,1,0:T(8,128)(2,1)} %weight.2) | copy-start | bytes 663556
  12.3 6.4 %collective-permute-start.2 = (bf16[32,2048]{1,0:T(8,128)(2,1)S(1)}, bf16[32,2048]{1,0:T(8,128)(2,1)S(1)}, u32[]{:S(2)}, u32[]{:S(2)}) collective-permute-start(bf16[32,2048]{1,0:T(8,128)(2,1)S(1)} %get-tuple-element.29), channel_id=1, source_target_pairs={{0,16},{1,17},{2,18},{3,19},{4,20},{5,21},{6,22},{7,23},{8,24},{9,... | collective-permute-start | bytes 393224 | tf_op jit(solution)/shard_map/ppermute | solution.py:72
  13.9 4.8 %collective-permute-start.3 = (bf16[32,2048]{1,0:T(8,128)(2,1)S(1)}, bf16[32,2048]{1,0:T(8,128)(2,1)S(1)}, u32[]{:S(2)}, u32[]{:S(2)}) collective-permute-start(bf16[32,2048]{1,0:T(8,128)(2,1)S(1)} %get-tuple-element.30), channel_id=1, source_target_pairs={{0,1},{1,0},{2,3},{3,2},{4,5},{5,4},{6,7},{7,6},{8,9},{9,8},{10,11... | collective-permute-start | bytes 393224 | tf_op jit(solution)/shard_map/ppermute | solution.py:72
  15.5 3.2 %copy-start.1 = (bf16[64,64]{1,0:T(8,128)(2,1)S(1)}, bf16[64,64]{1,0:T(8,128)(2,1)}, u32[]{:S(2)}) copy-start(bf16[64,64]{1,0:T(8,128)(2,1)} %w_key.1) | copy-start | bytes 24580
  15.5 3.2 %copy-start.2 = (bf16[64,64]{1,0:T(8,128)(2,1)S(1)}, bf16[64,64]{1,0:T(8,128)(2,1)}, u32[]{:S(2)}) copy-start(bf16[64,64]{1,0:T(8,128)(2,1)} %w_value.1) | copy-start | bytes 24580
  15.5 3.2 %copy-start.3 = (bf16[64,64]{1,0:T(8,128)(2,1)S(1)}, bf16[64,64]{1,0:T(8,128)(2,1)}, u32[]{:S(2)}) copy-start(bf16[64,64]{1,0:T(8,128)(2,1)} %w_query.1) | copy-start | bytes 24580
  15.5 3.2 %copy-start.4 = (bf16[64,64]{1,0:T(8,128)(2,1)S(1)}, bf16[64,64]{1,0:T(8,128)(2,1)}, u32[]{:S(2)}) copy-start(bf16[64,64]{1,0:T(8,128)(2,1)} %w_out.1) | copy-start | bytes 24580
  15.5 3.2 %copy-start.5 = (f32[64]{0:T(128)S(1)}, f32[64]{0:T(128)}, u32[]{:S(2)}) copy-start(f32[64]{0:T(128)} %param.18) | copy-start | bytes 772
  15.6 3.2 %copy-start.6 = (f32[64]{0:T(128)S(1)}, f32[64]{0:T(128)}, u32[]{:S(2)}) copy-start(f32[64]{0:T(128)} %param.19) | copy-start | bytes 772
  18.8 6.3 %copy-start.10 = (bf16[27,64,64]{2,1,0:T(8,128)(2,1)S(1)}, bf16[27,64,64]{2,1,0:T(8,128)(2,1)}, u32[]{:S(2)}) copy-start(bf16[27,64,64]{2,1,0:T(8,128)(2,1)} %weight.3) | copy-start | bytes 663556
  20.8 5.7 %collective-permute-start.4 = (bf16[16,1280]{1,0:T(8,128)(2,1)S(1)}, bf16[16,1280]{1,0:T(8,128)(2,1)S(1)}, u32[]{:S(2)}, u32[]{:S(2)}) collective-permute-start(bf16[16,1280]{1,0:T(8,128)(2,1)S(1)} %get-tuple-element.41), channel_id=1, source_target_pairs={{0,16},{1,17},{2,18},{3,19},{4,20},{5,21},{6,22},{7,23},{8,24},{9,... | collective-permute-start | bytes 122888 | tf_op jit(solution)/shard_map/ppermute | solution.py:72
  23.5 3.7 %collective-permute-start.5 = (bf16[16,1280]{1,0:T(8,128)(2,1)S(1)}, bf16[16,1280]{1,0:T(8,128)(2,1)S(1)}, u32[]{:S(2)}, u32[]{:S(2)}) collective-permute-start(bf16[16,1280]{1,0:T(8,128)(2,1)S(1)} %get-tuple-element.42), channel_id=1, source_target_pairs={{0,1},{1,0},{2,3},{3,2},{4,5},{5,4},{6,7},{7,6},{8,9},{9,8},{10,11... | collective-permute-start | bytes 122888 | tf_op jit(solution)/shard_map/ppermute | solution.py:72
  25.1 2.1 %copy-start.7 = (f32[64]{0:T(128)S(1)}, f32[64]{0:T(128)}, u32[]{:S(2)}) copy-start(f32[64]{0:T(128)} %param.20) | copy-start | bytes 772
  25.1 2.1 %copy-start.8 = (f32[64]{0:T(128)S(1)}, f32[64]{0:T(128)}, u32[]{:S(2)}) copy-start(f32[64]{0:T(128)} %param.21) | copy-start | bytes 772

commit v4 on v3

--- a/solution.py
+++ b/solution.py
@@ -17,13 +17,13 @@
 f32, bf16 = jnp.float32, jnp.bfloat16
 
 
-def call(kernel, out_shape, args, scratch=(), flops=0, bytes_accessed=0):
-    vmem = pl.BlockSpec(memory_space=pltpu.VMEM)
+def call(kernel, out_shape, args, scratch=(), flops=0, bytes_accessed=0, hbm_out=False):
+    vmem, hbm = pl.BlockSpec(memory_space=pltpu.VMEM), pl.BlockSpec(memory_space=pl.ANY)
     return pl.pallas_call(
         kernel,
         out_shape=out_shape,
         in_specs=[vmem] * len(args),
-        out_specs=jax.tree.map(lambda _: vmem, out_shape),
+        out_specs=jax.tree.map(lambda _: hbm if hbm_out else vmem, out_shape),
         scratch_shapes=list(scratch),
         compiler_params=pltpu.CompilerParams(vmem_limit_bytes=VMEM_LIMIT),
         cost_estimate=pl.CostEstimate(
@@ -49,9 +49,9 @@
 
 
 def parities():
-    even_x = lax.rem(lax.axis_index("sx"), 2) == 0
-    even_y = lax.rem(lax.axis_index("sy"), 2) == 0
-    return even_x, even_y
+    odd_x = lax.rem(lax.axis_index("sx"), 2) == 1
+    odd_y = lax.rem(lax.axis_index("sy"), 2) == 1
+    return odd_x, odd_y
 
 
 def pair_exchange(value, axis, phase):
@@ -168,7 +168,7 @@
     gap = jnp.zeros((BRICKS, C - 27), bf16)
     about = jnp.concatenate([high, gap, low, gap, occupied, tokens], axis=1)
     meta[...] = about
-    _, even_y = parities()
+    _, odd_y = parities()
 
     def write(out, near, behind):
         for place, y in ((NEAR, near), (BEHIND, behind)):
@@ -176,12 +176,12 @@
                 out[:, place + x * COL : place + (x + 1) * COL] = masked[:, column(x, y)]
         out[:, META:] = about
 
-    @pl.when(even_y)
+    @pl.when(odd_y)
     def _():
         write(s0, 3, 2)
         write(s1, 0, 1)
 
-    @pl.when(jnp.logical_not(even_y))
+    @pl.when(jnp.logical_not(odd_y))
     def _():
         write(s0, 0, 1)
         write(s1, 3, 2)
@@ -199,7 +199,7 @@
 
 
 def message_kernel(masked, t0, t1, x0, x1):
-    even_x, even_y = parities()
+    odd_x, odd_y = parities()
 
     def write(out, x):
         out[:, : 4 * COL] = face_x(masked, x)
@@ -207,15 +207,15 @@
         for a, b in ((t1, t0), (t0, t1)):
             for plane in (NEAR, BEHIND):
                 lanes = slice(plane + x * COL, plane + (x + 1) * COL)
-                out[:, place : place + COL] = pick(even_y, a[:, lanes], b[:, lanes])
+                out[:, place : place + COL] = pick(odd_y, a[:, lanes], b[:, lanes])
                 place += COL
 
-    @pl.when(even_x)
+    @pl.when(odd_x)
     def _():
         write(x0, 3)
         write(x1, 0)
 
-    @pl.when(jnp.logical_not(even_x))
+    @pl.when(jnp.logical_not(odd_x))
     def _():
         write(x0, 0)
         write(x1, 3)
@@ -374,23 +374,23 @@
 
 
 def y_reader(t0, t1):
-    _, even_y = parities()
+    _, odd_y = parities()
 
     def from_y(oy, place, width=COL):
         lanes = slice(place, place + width)
         a, b = (t1, t0) if oy < 0 else (t0, t1)
-        return pick(even_y, a[:, lanes], b[:, lanes])
+        return pick(odd_y, a[:, lanes], b[:, lanes])
 
     return from_y
 
 
 def x_reader(r0, r1):
-    even_x, _ = parities()
+    odd_x, _ = parities()
 
     def from_x(ox, k):
         lanes = slice(k * COL, (k + 1) * COL)
         a, b = (r1, r0) if ox < 0 else (r0, r1)
-        return pick(even_x, a[:, lanes], b[:, lanes])
+        return pick(odd_x, a[:, lanes], b[:, lanes])
 
     return from_x
 
@@ -486,15 +486,12 @@
         store_side(x, side, one(acc_side[k * BRICKS : (k + 1) * BRICKS], 1 + k, cov))
 
 
-def first_edge_kernel(
-    masked, r0, r1, t0, t1, ids_ref, band_edge, scale, shift, cover, acc, acc_side,
-    group, w_key, w_value, w_query, w_out, pack, edges, m0, m1, term_out, outer, side_outer,
+def edge_conv_kernel(
+    masked, r0, r1, t0, t1, ids_ref, band_edge, acc, acc_side, total, total_side,
+    outer, side_outer,
 ):
-    even_x, _ = parities()
     from_message, from_x = y_reader(t0, t1), x_reader(r0, r1)
     ids = ids_ref[...]
-    term = global_term(group, w_key, w_value, w_query, w_out)
-    term_out[...] = term
 
     def own(x, y):
         return masked[:, column(x, y)]
@@ -514,15 +511,27 @@
             own, from_x, from_message, side,
             lambda side, ox, number=number: side_select(number, side, ox), side_outer, (-1, 1),
         )
+    for n, x in enumerate((0, 3)):
+        more = convolve_edge(outer, side_outer, band_edge, x)
+        total[n] = acc[x] + more[: 4 * BRICKS]
+        total_side[n] = acc_side[x] + more[4 * BRICKS :]
+
+
+def edge_finish_kernel(
+    group, w_key, w_value, w_query, w_out, t0, t1, scale, shift, cover, total, total_side, pack,
+    edges, m0, m1, term_out,
+):
+    odd_x, _ = parities()
+    from_message = y_reader(t0, t1)
+    term = global_term(group, w_key, w_value, w_query, w_out)
+    term_out[...] = term
 
     def put(x, k, value):
         edges[0 if x == 0 else 1, :, k * COL : (k + 1) * COL] = value
 
-    for x in (0, 3):
-        more = convolve_edge(outer, side_outer, band_edge, x)
+    for n, x in enumerate((0, 3)):
         finish(
-            acc[x] + more[: 4 * BRICKS], acc_side[x] + more[4 * BRICKS :], x, four(scale),
-            four(shift), cover, from_message, term,
+            total[n], total_side[n], x, four(scale), four(shift), cover, from_message, term,
             put, lambda x, side, value: put(x, 4 if side < 0 else 5, value),
         )
     messages = []
@@ -535,8 +544,8 @@
         )
         side = jnp.dot(pack[2 * n + 1, :, : 2 * BRICKS], sides, preferred_element_type=f32)
         messages.append(jnp.concatenate([face, side], axis=1).astype(bf16))
-    m0[...] = pick(even_x, messages[1], messages[0])
-    m1[...] = pick(even_x, messages[0], messages[1])
+    m0[...] = pick(odd_x, messages[1], messages[0])
+    m1[...] = pick(odd_x, messages[0], messages[1])
 
 
 def edge_reader(edges):
@@ -545,7 +554,7 @@
 
 def middle_kernel(
     acc, acc_side, scale, shift, cover, t0, t1, term, edges, ids_ref, weight,
-    acc_out, band_edge, mid, mid_side, padded, band,
+    scale_two, shift_two, masked, acc_out, band_edge, result, mid, mid_side, padded, band,
 ):
     edge = edge_reader(edges)
     from_message = y_reader(t0, t1)
@@ -577,22 +586,46 @@
 
     def store(x_range, value):
         for n, x in enumerate(x_range):
-            acc_out[x] = value[n * 4 * BRICKS : (n + 1) * 4 * BRICKS]
+            part = value[n * 4 * BRICKS : (n + 1) * 4 * BRICKS]
+            if x in (0, 3):
+                acc_out[0 if x == 0 else 1] = part
+            else:
+                gain, offset = four(scale_two), four(shift_two)
+                put_result(part, x, gain, offset, cover, masked, result.at[x - 1])
 
     convolve_inner(padded, None, band, store)
 
 
+def put_result(total, x, gain, offset, cover, masked, out):
+    for y in range(4):
+        lanes = column(x, y)
+        value = total[y * BRICKS : (y + 1) * BRICKS] * gain + offset
+        value = jnp.maximum(value + masked[:, lanes].astype(f32), 0.0)
+        value = (value * cover[:, lanes].astype(f32)).astype(bf16)
+        out[:, y * COL : (y + 1) * COL] = value
+
+
 def second_kernel(
-    edges, r0, r1, ids_ref, slots, band_edge, scale, shift, cover, masked, acc, refined, outer
+    edges, r0, r1, ids_ref, slots, band_edge, scale, shift, cover, masked, acc, middle, refined,
+    outer, result, sem,
 ):
-    even_x, _ = parities()
+    copies = []
+
+    def send(part, x):
+        there = refined.at[:, x * 4 * COL : (x + 1) * 4 * COL]
+        copies.append(pltpu.make_async_copy(part, there, sem.at[x]))
+        copies[-1].start()
+
+    send(middle.at[0], 1)
+    send(middle.at[1], 2)
+    odd_x, _ = parities()
     edge, ids = edge_reader(edges), ids_ref[...]
     base = device_base()
 
     def received(ox, rows, k):
         lanes = slice(k * COL, (k + 1) * COL)
         a, b = (r1, r0) if ox < 0 else (r0, r1)
-        return pick(even_x, a[rows, lanes], b[rows, lanes])
+        return pick(odd_x, a[rows, lanes], b[rows, lanes])
 
     def from_corner(ox, oy):
         return received(ox, slice(None), 4)
@@ -614,19 +647,16 @@
         (-1, 1),
     )
     gain, offset = four(scale), four(shift)
-    for x in (1, 2, 0, 3):
-        total = acc[x]
-        if x in (0, 3):
-            total = total + convolve_edge(outer, None, band_edge, x)
-        for y in range(4):
-            lanes = column(x, y)
-            value = total[y * BRICKS : (y + 1) * BRICKS] * gain + offset
-            value = jnp.maximum(value + masked[:, lanes].astype(f32), 0.0)
-            refined[:, lanes] = (value * cover[:, lanes].astype(f32)).astype(bf16)
+    for n, x in enumerate((0, 3)):
+        total = acc[n] + convolve_edge(outer, None, band_edge, x)
+        put_result(total, x, gain, offset, cover, masked, result.at[n])
+        send(result.at[n], x)
+    for copy in copies:
+        copy.wait()
 
 
 def exchange(first, second, axis):
-    return pair_exchange(first, axis, 0), pair_exchange(second, axis, 1)
+    return pair_exchange(first, axis, 1), pair_exchange(second, axis, 0)
 
 
 def local(
@@ -672,28 +702,39 @@
         flops=1 << 33,
         bytes_accessed=2 << 20,
     )
-    group, acc = lax.optimization_barrier((group, acc))
+    total, total_side = call(
+        edge_conv_kernel,
+        [
+            shape(2, 4 * BRICKS, COL, dtype=f32),
+            shape(2, 2 * BRICKS, COL, dtype=f32),
+        ],
+        (masked, r0, r1, t0, t1, ids, band_one, acc, acc_side),
+        [outer, side_outer],
+        flops=2 * 384 * 1152 * 256,
+        bytes_accessed=4 << 20,
+    )
+    group, total = lax.optimization_barrier((group, total))
     out_message = shape(FACE_SLOTS, 5 * COL)
     edges, m0, m1, term = call(
-        first_edge_kernel,
+        edge_finish_kernel,
         [
             shape(2, BRICKS, 6 * COL), out_message, out_message,
             shape(3 * BRICKS, COL, dtype=f32),
         ],
         (
-            masked, r0, r1, t0, t1, ids, band_one, rows[0], rows[1], cover, acc, acc_side,
-            group, w_key, w_value, w_query, w_out, pack,
+            group, w_key, w_value, w_query, w_out, t0, t1, rows[0], rows[1], cover, total,
+            total_side, pack,
         ),
-        [outer, side_outer],
-        flops=2 * 384 * 3456 * 256,
-        bytes_accessed=4 << 20,
+        flops=1 << 26,
+        bytes_accessed=2 << 20,
     )
     r0, r1 = exchange(m0, m1, "sx")
-    acc, band_two = call(
+    acc, band_two, half = call(
         middle_kernel,
-        [own_acc, band_edge],
+        [shape(2, 4 * BRICKS, COL, dtype=f32), band_edge, shape(2, BRICKS, 4 * COL)],
         (
             acc, acc_side, rows[0], rows[1], cover, t0, t1, term, edges, ids, conv_two,
+            rows[2], rows[3], masked,
         ),
         [
             pltpu.VMEM((2, 4, BRICKS, COL), bf16),
@@ -708,11 +749,12 @@
         second_kernel,
         whole,
         (
-            edges, r0, r1, ids, slots, band_two, rows[2], rows[3], cover, masked, acc,
+            edges, r0, r1, ids, slots, band_two, rows[2], rows[3], cover, masked, acc, half,
         ),
-        [outer],
+        [outer, pltpu.VMEM((2, BRICKS, 4 * COL), bf16), pltpu.SemaphoreType.DMA((4,))],
         flops=2 * 256 * 1152 * 256,
         bytes_accessed=3 << 20,
+        hbm_out=True,
     )
 
 

time: 28.9 us -> 27.9 us (0.965)
  waiting for transfers between devices: 1.72 us -> 1 us
  starting transfers between devices: 17 us -> 16.5 us
    all_to_all x1, waiting for transfers between devices: 0.99 us -> 0.01 us  [local(): group = lax.all_to_all(tokens, 'sy', 0, 0)]
    pallas_call x6 -> x7, Pallas kernels: 7.85 us -> 7.98 us  [call(): pl.pallas_call(kernel, out_shape=out_shape, in_specs=[vmem] * len(args),...]
  transfers between devices with their start and end apart: 7 -> 7, of which waited for: 2 -> 2; matrix products, arithmetic and copies ran while one was open for 0% -> 0% of each run, Pallas kernels for 12% -> 16%
where the time goes in v4:
time: 27.9 us; the launch traced here: 27.5 us
  starting transfers between devices  16.5 us (59%)
  Pallas kernels  7.98 us (29%)
  local copies, waits for them, and re-layouts  1.01 us (4%)
  waiting for transfers between devices  1 us (4%)
  other arithmetic  0.81 us (3%)
    ppermute x6, starting transfers between devices, pair_exchange(): return lax.ppermute(value, ('sx', 'sy'), pairs)  10.4 us
    pallas_call x7, Pallas kernels, call(): pl.pallas_call(kernel, out_shape=out_shape, in_specs=[vmem] * len(args),...  7.98 us
    all_to_all x1, starting transfers between devices, local(): group = lax.all_to_all(tokens, 'sy', 0, 0)  6.17 us
    unnamed x22, local copies, waits for them, and re-layouts  1.01 us
    ppermute x6, waiting for transfers between devices, pair_exchange(): return lax.ppermute(value, ('sx', 'sy'), pairs)  0.99 us
    concatenate x1, other arithmetic, local(): marks = jnp.concatenate([occupancy, adjacency], axis=1)  0.81 us
  transfers between devices with their start and end apart: 7, of which 2 were waited for; matrix products, arithmetic and copies ran while one was open for 0% of the time, Pallas kernels for 16%

profile of v4, /device:TPU:1, one launch (start us, length us, event | category | flops | bytes accessed | tf_op | source)
XLA Modules:
  0.0 27.5 jit_solution(11787510849275167960)
XLA Ops:
  0.0 0.8 %pad_add_fusion.marks = s32[32,91]{1,0:T(8,128)S(1)} fusion(s32[32,27]{1,0:T(8,128)} %param.15, s32[32,64]{1,0:T(8,128)} %param.14), kind=kLoop, calls=%fused_computation | loop fusion | flops 2912 | bytes 23296 | tf_op jit(solution)/shard_map/concatenate | solution.py:675
  0.8 0.0 copy-start
  0.8 0.9 %copy-done = bf16[32,4096]{1,0:T(8,128)(2,1)S(1)} copy-done((bf16[32,4096]{1,0:T(8,128)(2,1)S(1)}, bf16[32,4096]{1,0:T(8,128)(2,1)}, u32[]{:S(2)}) %copy-start) | copy-done | bytes 262168
  1.8 1.0 %shard_map.127 = (bf16[32,4096]{1,0:T(8,128)(2,1)S(1)}, bf16[32,4096]{1,0:T(8,128)(2,1)S(1)}, bf16[16,16,128]{2,1,0:T(8,128)(2,1)}, bf16[32,256]{1,0:T(8,128)(2,...) custom-call(bf16[32,4096]{1,0:T(8,128)(2,1)S(1)} %copy-done, ...), custom_call_target="tpu_custom_call" | custom-call | bytes 2097152 | tf_op jit(solution)/shard_map/pallas_call | solution.py:22
  2.8 1.4 %collective-permute-start = (bf16[32,2304]{1,0:T(8,128)(2,1)S(1)}, bf16[32,2304]{1,0:T(8,128)(2,1)S(1)}, u32[]{:S(2)}, u32[]{:S(2)}) collective-permute-start(bf16[32,2304]{1,0:T(8,128)(2,1)S(1)} %get-tuple-element.31), channel_id=1, source_target_pairs={{0,16},{1,2},{2,1},{3,4},{4,3},{5,6},{6,5},{7,8},{8,7},{9,10},{10,... | collective-permute-start | bytes 442376 | tf_op jit(solution)/shard_map/ppermute | solution.py:72
  4.2 1.8 %collective-permute-start.1 = (bf16[32,2304]{1,0:T(8,128)(2,1)S(1)}, bf16[32,2304]{1,0:T(8,128)(2,1)S(1)}, u32[]{:S(2)}, u32[]{:S(2)}) collective-permute-start(bf16[32,2304]{1,0:T(8,128)(2,1)S(1)} %get-tuple-element.32), channel_id=1, source_target_pairs={{0,1},{1,0},{2,3},{3,2},{4,5},{5,4},{6,7},{7,6},{8,9},{9,8},{10,11... | collective-permute-start | bytes 442376 | tf_op jit(solution)/shard_map/ppermute | solution.py:72
  6.0 6.2 %all-to-all-start = ((bf16[16,16,128]{2,1,0:T(8,128)(2,1)}), bf16[16,16,128]{2,1,0:T(8,128)(2,1)S(1)}, u32[]{:S(2)}, u32[]{:S(2)}) async-start(bf16[16,16,128]{2,1,0:T(8,128)(2,1)} %get-tuple-element.29), calls=%async_computation | async-start | bytes 131072 | tf_op jit(solution)/shard_map/all_to_all | solution.py:688
  12.2 0.0 collective-permute-done.t0
  12.2 0.0 collective-permute-done.1.t1
  12.2 0.0 copy-start.9
  12.3 3.1 %collective-permute-start.2 = (bf16[32,2048]{1,0:T(8,128)(2,1)S(1)}, bf16[32,2048]{1,0:T(8,128)(2,1)S(1)}, u32[]{:S(2)}, u32[]{:S(2)}) collective-permute-start(bf16[32,2048]{1,0:T(8,128)(2,1)S(1)} %get-tuple-element.33), channel_id=1, source_target_pairs={{0,1},{1,0},{2,3},{3,2},{4,5},{5,4},{6,7},{7,6},{8,9},{9,8},{10,11... | collective-permute-start | bytes 393224 | tf_op jit(solution)/shard_map/ppermute | solution.py:72
  15.4 0.4 %collective-permute-start.3 = (bf16[32,2048]{1,0:T(8,128)(2,1)S(1)}, bf16[32,2048]{1,0:T(8,128)(2,1)S(1)}, u32[]{:S(2)}, u32[]{:S(2)}) collective-permute-start(bf16[32,2048]{1,0:T(8,128)(2,1)S(1)} %get-tuple-element.34), channel_id=1, source_target_pairs={{0,16},{1,17},{2,18},{3,19},{4,20},{5,21},{6,22},{7,23},{8,24},{9,... | collective-permute-start | bytes 393224 | tf_op jit(solution)/shard_map/ppermute | solution.py:72
  15.8 0.0 copy-done.9
  15.8 2.2 %shard_map.129 = (f32[4,128,256]{2,1,0:T(8,128)S(1)}, f32[4,64,256]{2,1,0:T(8,128)S(1)}, bf16[6,384,256]{2,1,0:T(8,128)(2,1)S(1)}, bf16[4,16,128]{2,1,0:T(8,128)(2,1)S(1)}, s32[2,8,128]{2,1,0:T(8,128)S(1)}) custom-call(bf16[32,4096]{1,0:T(8,128)(2,1)S(1)} %get-tuple-element.30.masked, bf16[32,2304]{1,0:T(8,128)(2,1)S(1)} %collective-permute-done.t0, ...), custom_call_target="tpu_custom_call" | custom-call | flops 8589934592 | bytes 2097152 | tf_op jit(solution)/shard_map/pallas_call | solution.py:22
  18.0 0.4 %collective-permute-done.2.r0 = bf16[32,2048]{1,0:T(8,128)(2,1)S(1)} collective-permute-done((bf16[32,2048]{1,0:T(8,128)(2,1)S(1)}, bf16[32,2048]{1,0:T(8,128)(2,1)S(1)}, u32[]{:S(2)}, u32[]{:S(2)}) %collective-permute-start.2) | collective-permute-done | bytes 131104 | tf_op jit(solution)/shard_map/ppermute | solution.py:72
  18.4 0.0 collective-permute-done.3.r1
  18.4 0.0 copy-start.1
  18.4 0.0 copy-start.2
  18.4 0.0 copy-start.3
  18.4 0.0 copy-start.4
  18.4 0.0 copy-start.5
  18.4 0.0 copy-start.6
  18.4 0.0 copy-start.7
  18.4 0.0 copy-start.8
  18.4 0.0 copy-start.10
  18.4 0.9 %shard_map.130 = (f32[2,128,256]{2,1,0:T(8,128)S(1)}, f32[2,64,256]{2,1,0:T(8,128)S(1)}) custom-call(bf16[32,4096]{1,0:T(8,128)(2,1)S(1)} %get-tuple-element.30.masked, bf16[32,2048]{1,0:T(8,128)(2,1)S(1)} %collective-permute-done.2.r0, bf16[32,2048]{1,0:T(8,128)(2,1)S(1)} %collective-permute-done.3.r1, bf16[32,2304]{1,0:T(8,128)(2,1)S(1)} %collective-permute-done.t0, ...), custom_call_target="tpu_custom_call" | custom-call | flops 226492416 | bytes 4194304 | tf_op jit(solution)/shard_map/pallas_call | solution.py:22
  19.4 0.0 all-to-all-done.group
  19.4 0.0 copy-done.1
  19.4 0.0 copy-done.2
  19.4 0.0 copy-done.3
  19.4 0.0 copy-done.4
  19.4 0.0 copy-done.5
  19.4 0.0 copy-done.6
  19.4 1.2 %shard_map.131 = (bf16[2,32,1536]{2,1,0:T(8,128)(2,1)S(1)}, bf16[16,1280]{1,0:T(8,128)(2,1)S(1)}, bf16[16,1280]{1,0:T(8,128)(2,1)S(1)}, f32[96,256]{1,0:T(8,128)S(1)}) custom-call(bf16[16,16,128]{2,1,0:T(8,128)(2,1)S(1)} %all-to-all-done.group, bf16[64,64]{1,0:T(8,128)(2,1)S(1)} %copy-done.1, bf16[64,64]{1,0:T(8,128)(2,1)S(1)} %copy-done.2, ...), custom_call_target="tpu_custom_call" | custom-call | flops 67108864 | bytes 2097152 | tf_op jit(solution)/shard_map/pallas_call | solution.py:22
  20.7 3.6 %collective-permute-start.4 = (bf16[16,1280]{1,0:T(8,128)(2,1)S(1)}, bf16[16,1280]{1,0:T(8,128)(2,1)S(1)}, u32[]{:S(2)}, u32[]{:S(2)}) collective-permute-start(bf16[16,1280]{1,0:T(8,128)(2,1)S(1)} %get-tuple-element.46), channel_id=1, source_target_pairs={{0,1},{1,0},{2,3},{3,2},{4,5},{5,4},{6,7},{7,6},{8,9},{9,8},{10,11... | collective-permute-start | bytes 122888 | tf_op jit(solution)/shard_map/ppermute | solution.py:72
  24.3 0.0 collective-permute-start.5
  24.3 0.0 copy-done.7
  24.3 0.0 copy-done.8
  24.3 0.0 copy-done.10
  24.3 1.3 %shard_map.132 = (f32[2,128,256]{2,1,0:T(8,128)S(1)}, bf16[6,384,256]{2,1,0:T(8,128)(2,1)S(1)}, bf16[2,32,1024]{2,1,0:T(8,128)(2,1)S(1)}) custom-call(f32[4,128,256]{2,1,0:T(8,128)S(1)} %get-tuple-element.37.acc, f32[4,64,256]{2,1,0:T(8,128)S(1)} %get-tuple-element.38.acc_side, f32[1,64]{1,0:T(1,128)S(1)} %bitcast.5, f32[1,64]{1,0:T(1,128)S(1)} %bitcast.7, ...), custom_call_target="tpu_custom_call" | custom-call | flops 8589934592 | bytes 4194304 | tf_op jit(solution)/shard_map/pallas_call | solution.py:22
  25.6 0.6 %collective-permute-done.4.r0 = bf16[16,1280]{1,0:T(8,128)(2,1)S(1)} collective-permute-done((bf16[16,1280]{1,0:T(8,128)(2,1)S(1)}, bf16[16,1280]{1,0:T(8,128)(2,1)S(1)}, u32[]{:S(2)}, u32[]{:S(2)}) %collective-permute-start.4) | collective-permute-done | bytes 40992 | tf_op jit(solution)/shard_map/ppermute | solution.py:72
  26.2 0.0 collective-permute-done.5.r1
  26.2 1.3 %shard_map.133 = bf16[32,4096]{1,0:T(8,128)(2,1)} custom-call(bf16[2,32,1536]{2,1,0:T(8,128)(2,1)S(1)} %get-tuple-element.45.edges, bf16[16,1280]{1,0:T(8,128)(2,1)S(1)} %collective-permute-done.4.r0, bf16[16,1280]{1,0:T(8,128)(2,1)S(1)} %collective-permute-done.5.r1, s32[32,27]{1,0:T(8,128)S(1)} %get-tuple-element.35.ids_ref, ...), custom_call_target="tpu_custom_call" | custom-call | flops 150994944 | bytes 3145728 | tf_op jit(solution)/shard_map/pallas_call | solution.py:22
  (1 shorter events, 0.0 us)
Async XLA Ops:
  0.8 1.0 %copy-start = (bf16[32,4096]{1,0:T(8,128)(2,1)S(1)}, bf16[32,4096]{1,0:T(8,128)(2,1)}, u32[]{:S(2)}) copy-start(bf16[32,4096]{1,0:T(8,128)(2,1)} %feat.1) | copy-start | bytes 786436
  2.8 9.4 %collective-permute-start = (bf16[32,2304]{1,0:T(8,128)(2,1)S(1)}, bf16[32,2304]{1,0:T(8,128)(2,1)S(1)}, u32[]{:S(2)}, u32[]{:S(2)}) collective-permute-start(bf16[32,2304]{1,0:T(8,128)(2,1)S(1)} %get-tuple-element.31), channel_id=1, source_target_pairs={{0,16},{1,2},{2,1},{3,4},{4,3},{5,6},{6,5},{7,8},{8,7},{9,10},{10,... | collective-permute-start | bytes 442376 | tf_op jit(solution)/shard_map/ppermute | solution.py:72
  4.2 8.0 %collective-permute-start.1 = (bf16[32,2304]{1,0:T(8,128)(2,1)S(1)}, bf16[32,2304]{1,0:T(8,128)(2,1)S(1)}, u32[]{:S(2)}, u32[]{:S(2)}) collective-permute-start(bf16[32,2304]{1,0:T(8,128)(2,1)S(1)} %get-tuple-element.32), channel_id=1, source_target_pairs={{0,1},{1,0},{2,3},{3,2},{4,5},{5,4},{6,7},{7,6},{8,9},{9,8},{10,11... | collective-permute-start | bytes 442376 | tf_op jit(solution)/shard_map/ppermute | solution.py:72
  6.0 13.3 %all-to-all-start = ((bf16[16,16,128]{2,1,0:T(8,128)(2,1)}), bf16[16,16,128]{2,1,0:T(8,128)(2,1)S(1)}, u32[]{:S(2)}, u32[]{:S(2)}) async-start(bf16[16,16,128]{2,1,0:T(8,128)(2,1)} %get-tuple-element.29), calls=%async_computation | async-start | bytes 131072 | tf_op jit(solution)/shard_map/all_to_all | solution.py:688
  12.2 3.6 %copy-start.9 = (bf16[27,64,64]{2,1,0:T(8,128)(2,1)S(1)}, bf16[27,64,64]{2,1,0:T(8,128)(2,1)}, u32[]{:S(2)}) copy-start(bf16[27,64,64]{2,1,0:T(8,128)(2,1)} %weight.2) | copy-start | bytes 663556
  12.3 6.1 %collective-permute-start.2 = (bf16[32,2048]{1,0:T(8,128)(2,1)S(1)}, bf16[32,2048]{1,0:T(8,128)(2,1)S(1)}, u32[]{:S(2)}, u32[]{:S(2)}) collective-permute-start(bf16[32,2048]{1,0:T(8,128)(2,1)S(1)} %get-tuple-element.33), channel_id=1, source_target_pairs={{0,1},{1,0},{2,3},{3,2},{4,5},{5,4},{6,7},{7,6},{8,9},{9,8},{10,11... | collective-permute-start | bytes 393224 | tf_op jit(solution)/shard_map/ppermute | solution.py:72
  15.4 3.0 %collective-permute-start.3 = (bf16[32,2048]{1,0:T(8,128)(2,1)S(1)}, bf16[32,2048]{1,0:T(8,128)(2,1)S(1)}, u32[]{:S(2)}, u32[]{:S(2)}) collective-permute-start(bf16[32,2048]{1,0:T(8,128)(2,1)S(1)} %get-tuple-element.34), channel_id=1, source_target_pairs={{0,16},{1,17},{2,18},{3,19},{4,20},{5,21},{6,22},{7,23},{8,24},{9,... | collective-permute-start | bytes 393224 | tf_op jit(solution)/shard_map/ppermute | solution.py:72
  18.4 1.0 %copy-start.1 = (bf16[64,64]{1,0:T(8,128)(2,1)S(1)}, bf16[64,64]{1,0:T(8,128)(2,1)}, u32[]{:S(2)}) copy-start(bf16[64,64]{1,0:T(8,128)(2,1)} %w_key.1) | copy-start | bytes 24580
  18.4 1.0 %copy-start.2 = (bf16[64,64]{1,0:T(8,128)(2,1)S(1)}, bf16[64,64]{1,0:T(8,128)(2,1)}, u32[]{:S(2)}) copy-start(bf16[64,64]{1,0:T(8,128)(2,1)} %w_value.1) | copy-start | bytes 24580
  18.4 1.0 %copy-start.3 = (bf16[64,64]{1,0:T(8,128)(2,1)S(1)}, bf16[64,64]{1,0:T(8,128)(2,1)}, u32[]{:S(2)}) copy-start(bf16[64,64]{1,0:T(8,128)(2,1)} %w_query.1) | copy-start | bytes 24580
  18.4 1.0 %copy-start.4 = (bf16[64,64]{1,0:T(8,128)(2,1)S(1)}, bf16[64,64]{1,0:T(8,128)(2,1)}, u32[]{:S(2)}) copy-start(bf16[64,64]{1,0:T(8,128)(2,1)} %w_out.1) | copy-start | bytes 24580
  18.4 1.0 %copy-start.5 = (f32[64]{0:T(128)S(1)}, f32[64]{0:T(128)}, u32[]{:S(2)}) copy-start(f32[64]{0:T(128)} %param.18) | copy-start | bytes 772
  18.4 1.0 %copy-start.6 = (f32[64]{0:T(128)S(1)}, f32[64]{0:T(128)}, u32[]{:S(2)}) copy-start(f32[64]{0:T(128)} %param.19) | copy-start | bytes 772
  18.4 5.9 %copy-start.7 = (f32[64]{0:T(128)S(1)}, f32[64]{0:T(128)}, u32[]{:S(2)}) copy-start(f32[64]{0:T(128)} %param.20) | copy-start | bytes 772
  18.4 5.8 %copy-start.8 = (f32[64]{0:T(128)S(1)}, f32[64]{0:T(128)}, u32[]{:S(2)}) copy-start(f32[64]{0:T(128)} %param.21) | copy-start | bytes 772
  18.4 5.8 %copy-start.10 = (bf16[27,64,64]{2,1,0:T(8,128)(2,1)S(1)}, bf16[27,64,64]{2,1,0:T(8,128)(2,1)}, u32[]{:S(2)}) copy-start(bf16[27,64,64]{2,1,0:T(8,128)(2,1)} %weight.3) | copy-start | bytes 663556
  20.7 5.6 %collective-permute-start.4 = (bf16[16,1280]{1,0:T(8,128)(2,1)S(1)}, bf16[16,1280]{1,0:T(8,128)(2,1)S(1)}, u32[]{:S(2)}, u32[]{:S(2)}) collective-permute-start(bf16[16,1280]{1,0:T(8,128)(2,1)S(1)} %get-tuple-element.46), channel_id=1, source_target_pairs={{0,1},{1,0},{2,3},{3,2},{4,5},{5,4},{6,7},{7,6},{8,9},{9,8},{10,11... | collective-permute-start | bytes 122888 | tf_op jit(solution)/shard_map/ppermute | solution.py:72
  24.3 2.0 %collective-permute-start.5 = (bf16[16,1280]{1,0:T(8,128)(2,1)S(1)}, bf16[16,1280]{1,0:T(8,128)(2,1)S(1)}, u32[]{:S(2)}, u32[]{:S(2)}) collective-permute-start(bf16[16,1280]{1,0:T(8,128)(2,1)S(1)} %get-tuple-element.47), channel_id=1, source_target_pairs={{0,16},{1,17},{2,18},{3,19},{4,20},{5,21},{6,22},{7,23},{8,24},{9,... | collective-permute-start | bytes 122888 | tf_op jit(solution)/shard_map/ppermute | solution.py:72

commit v5 on v4

--- a/solution.py
+++ b/solution.py
@@ -14,18 +14,23 @@
 EPSILON = 1e-05
 FAR = -(1 << 20)
 VMEM_LIMIT = 16 * 1024 * 1024
+WHOLE_VMEM = 60 * 1024 * 1024
 f32, bf16 = jnp.float32, jnp.bfloat16
 
 
-def call(kernel, out_shape, args, scratch=(), flops=0, bytes_accessed=0, hbm_out=False):
+def call(
+    kernel, out_shape, args, scratch=(), flops=0, bytes_accessed=0, hbm_in=False, hbm_out=False
+):
     vmem, hbm = pl.BlockSpec(memory_space=pltpu.VMEM), pl.BlockSpec(memory_space=pl.ANY)
     return pl.pallas_call(
         kernel,
         out_shape=out_shape,
-        in_specs=[vmem] * len(args),
+        in_specs=[hbm if hbm_in else vmem] * len(args),
         out_specs=jax.tree.map(lambda _: hbm if hbm_out else vmem, out_shape),
         scratch_shapes=list(scratch),
-        compiler_params=pltpu.CompilerParams(vmem_limit_bytes=VMEM_LIMIT),
+        compiler_params=pltpu.CompilerParams(
+            vmem_limit_bytes=WHOLE_VMEM if hbm_in else VMEM_LIMIT
+        ),
         cost_estimate=pl.CostEstimate(
             flops=flops, bytes_accessed=bytes_accessed, transcendentals=0
         ),
@@ -141,10 +146,18 @@
 NEAR, BEHIND, META, Y_LANES = 0, 4 * COL, 8 * COL, 9 * COL
 
 
-def prepare_kernel(feat, marks, masked, cover, tokens_all, meta, ids, s0, s1):
-    occupied = marks[:, :C].astype(f32).astype(bf16)
+def prepare_kernel(
+    feat_hbm, occ_hbm, adj_hbm, masked, cover, tokens_all, meta, ids, s0, s1, feat, occ, adj, sems
+):
+    pairs = ((occ_hbm, occ), (feat_hbm, feat), (adj_hbm, adj))
+    copies = [pltpu.make_async_copy(a, b, sems.at[k]) for k, (a, b) in enumerate(pairs)]
+    for copy in copies:
+        copy.start()
+    copies[0].wait()
+    occupied = occ[...].astype(f32).astype(bf16)
     row = lax.broadcasted_iota(jnp.int32, (64, COL), 0)
     voxel = lax.shift_right_logical(lax.broadcasted_iota(jnp.int32, (64, COL), 1), 6)
+    copies[1].wait()
     total = jnp.zeros((BRICKS, 128), f32)
     for k in range(16):
         lanes = slice(k * COL, (k + 1) * COL)
@@ -160,7 +173,8 @@
     half = BRICKS // 2
     packed = jnp.concatenate([tokens[:half], tokens[half:]], axis=1)
     tokens_all[...] = jnp.broadcast_to(packed[None], tokens_all.shape)
-    number = marks[:, C : C + 27]
+    copies[2].wait()
+    number = adj[...]
     ids[...] = jnp.where(number < 0, FAR, number)
     number = number + 1
     high = lax.shift_right_logical(number, 6).astype(f32).astype(bf16)
@@ -672,7 +686,7 @@
     outer = pltpu.VMEM((2, 6, BRICKS, TAP), bf16)
     side_inner = pltpu.VMEM((4, 3, 2 * BRICKS, TAP), bf16)
     side_outer = pltpu.VMEM((2, 3, 2 * BRICKS, TAP), bf16)
-    marks = jnp.concatenate([occupancy, adjacency], axis=1)
+    inputs = (features, occupancy, adjacency)
     message = shape(BRICKS, Y_LANES)
     masked, cover, tokens, meta, ids, s0, s1 = call(
         prepare_kernel,
@@ -680,8 +694,10 @@
             whole, whole, shape(n_sy, BRICKS // 2, 2 * C), shape(BRICKS, 4 * C),
             shape(BRICKS, 27, dtype=jnp.int32), message, message,
         ],
-        (features, marks),
+        inputs,
+        [pltpu.VMEM(v.shape, v.dtype) for v in inputs] + [pltpu.SemaphoreType.DMA((3,))],
         bytes_accessed=2 << 20,
+        hbm_in=True,
     )
     rows = [v.reshape(1, C) for v in (scale_one, shift_one, scale_two, shift_two)]
     t0, t1 = exchange(s0, s1, "sy")

time: 27.9 us -> 27.6 us (0.989)
  Pallas kernels: 7.98 us -> 9.33 us
  other arithmetic: 0.81 us -> 0 us
  starting transfers between devices: 16.5 us -> 15.7 us
    pallas_call x7, Pallas kernels: 7.98 us -> 9.33 us  [call(): pl.pallas_call(kernel, out_shape=out_shape, in_specs=[hbm if hbm_in else...]
    ppermute x6, starting transfers between devices: 10.4 us -> 9.51 us  [pair_exchange(): return lax.ppermute(value, ('sx', 'sy'), pairs)]
    concatenate x1 -> x0, other arithmetic: 0.81 us -> none  [local(): marks = jnp.concatenate([occupancy, adjacency], axis=1)]
    unnamed x22 -> x28, local copies, waits for them, and re-layouts: 1.01 us -> 1.01 us
where the time goes in v5:
time: 27.6 us; the launch traced here: 27.2 us
  starting transfers between devices  15.7 us (57%)
  Pallas kernels  9.33 us (34%)
  local copies, waits for them, and re-layouts  1.01 us (4%)
  waiting for transfers between devices  0.96 us (3%)
    ppermute x6, starting transfers between devices, pair_exchange(): return lax.ppermute(value, ('sx', 'sy'), pairs)  9.51 us
    pallas_call x7, Pallas kernels, call(): pl.pallas_call(kernel, out_shape=out_shape, in_specs=[hbm if hbm_in else...  9.33 us
    all_to_all x1, starting transfers between devices, local(): group = lax.all_to_all(tokens, 'sy', 0, 0)  6.17 us
    unnamed x28, local copies, waits for them, and re-layouts  1.01 us
    ppermute x6, waiting for transfers between devices, pair_exchange(): return lax.ppermute(value, ('sx', 'sy'), pairs)  0.96 us
  transfers between devices with their start and end apart: 7, of which 2 were waited for; matrix products, arithmetic and copies ran while one was open for 0% of the time, Pallas kernels for 16%

profile of v5, /device:TPU:1, one launch (start us, length us, event | category | flops | bytes accessed | tf_op | source)
XLA Modules:
  0.0 27.2 jit_solution(10345311518217151714)
XLA Ops:
  0.0 2.4 %shard_map.127 = (bf16[32,4096]{1,0:T(8,128)(2,1)}, bf16[32,4096]{1,0:T(8,128)(2,1)}, bf16[16,16,128]{2,1,0:T(8,128)(2,1)}, bf16[32,256]{1,0:T(8,128)(2,1)}, s32...) custom-call(bf16[32,4096]{1,0:T(8,128)(2,1)} %feat_hbm.1, s32[32,64]{1,0:T(8,128)} %occ_hbm.1, ...), custom_call_target="tpu_custom_call" | custom-call | bytes 2097152 | tf_op jit(solution)/shard_map/pallas_call | solution.py:25
  2.4 1.5 %collective-permute-start = (bf16[32,2304]{1,0:T(8,128)(2,1)}, bf16[32,2304]{1,0:T(8,128)(2,1)S(1)}, u32[]{:S(2)}, u32[]{:S(2)}) collective-permute-start(bf16[32,2304]{1,0:T(8,128)(2,1)} %get-tuple-element.31), channel_id=1, source_target_pairs={{0,16},{1,2},{2,1},{3,4},{4,3},{5,6},{6,5},{7,8},{8,7},{9,10},{10,... | collective-permute-start | bytes 442376 | tf_op jit(solution)/shard_map/ppermute | solution.py:77
  3.9 1.8 %collective-permute-start.1 = (bf16[32,2304]{1,0:T(8,128)(2,1)}, bf16[32,2304]{1,0:T(8,128)(2,1)S(1)}, u32[]{:S(2)}, u32[]{:S(2)}) collective-permute-start(bf16[32,2304]{1,0:T(8,128)(2,1)} %get-tuple-element.32), channel_id=1, source_target_pairs={{0,1},{1,0},{2,3},{3,2},{4,5},{5,4},{6,7},{7,6},{8,9},{9,8},{10,11... | collective-permute-start | bytes 442376 | tf_op jit(solution)/shard_map/ppermute | solution.py:77
  5.7 6.2 %all-to-all-start = ((bf16[16,16,128]{2,1,0:T(8,128)(2,1)}), bf16[16,16,128]{2,1,0:T(8,128)(2,1)S(1)}, u32[]{:S(2)}, u32[]{:S(2)}) async-start(bf16[16,16,128]{2,1,0:T(8,128)(2,1)} %get-tuple-element.29), calls=%async_computation | async-start | bytes 131072 | tf_op jit(solution)/shard_map/all_to_all | solution.py:704
  11.9 0.0 collective-permute-done.t0
  11.9 0.0 collective-permute-done.1.t1
  11.9 0.0 copy-start.1
  11.9 0.9 %copy-done.1 = bf16[32,4096]{1,0:T(8,128)(2,1)S(1)} copy-done((bf16[32,4096]{1,0:T(8,128)(2,1)S(1)}, bf16[32,4096]{1,0:T(8,128)(2,1)}, u32[]{:S(2)}) %copy-start.1) | copy-done | bytes 262168
  12.9 0.0 copy-start.3
  12.9 0.0 copy-start.12
  12.9 3.1 %collective-permute-start.2 = (bf16[32,2048]{1,0:T(8,128)(2,1)S(1)}, bf16[32,2048]{1,0:T(8,128)(2,1)S(1)}, u32[]{:S(2)}, u32[]{:S(2)}) collective-permute-start(bf16[32,2048]{1,0:T(8,128)(2,1)S(1)} %get-tuple-element.33), channel_id=1, source_target_pairs={{0,1},{1,0},{2,3},{3,2},{4,5},{5,4},{6,7},{7,6},{8,9},{9,8},{10,11... | collective-permute-start | bytes 393224 | tf_op jit(solution)/shard_map/ppermute | solution.py:77
  16.0 0.4 %collective-permute-start.3 = (bf16[32,2048]{1,0:T(8,128)(2,1)S(1)}, bf16[32,2048]{1,0:T(8,128)(2,1)S(1)}, u32[]{:S(2)}, u32[]{:S(2)}) collective-permute-start(bf16[32,2048]{1,0:T(8,128)(2,1)S(1)} %get-tuple-element.34), channel_id=1, source_target_pairs={{0,16},{1,17},{2,18},{3,19},{4,20},{5,21},{6,22},{7,23},{8,24},{9,... | collective-permute-start | bytes 393224 | tf_op jit(solution)/shard_map/ppermute | solution.py:77
  16.4 0.0 copy-done.3
  16.4 0.0 copy-done.12
  16.4 2.2 %shard_map.129 = (f32[4,128,256]{2,1,0:T(8,128)S(1)}, f32[4,64,256]{2,1,0:T(8,128)S(1)}, bf16[6,384,256]{2,1,0:T(8,128)(2,1)S(1)}, bf16[4,16,128]{2,1,0:T(8,128)(2,1)S(1)}, s32[2,8,128]{2,1,0:T(8,128)S(1)}) custom-call(bf16[32,4096]{1,0:T(8,128)(2,1)S(1)} %copy-done.1, bf16[32,2304]{1,0:T(8,128)(2,1)S(1)} %collective-permute-done.t0, ...), custom_call_target="tpu_custom_call" | custom-call | flops 8589934592 | bytes 2097152 | tf_op jit(solution)/shard_map/pallas_call | solution.py:25
  18.6 0.3 %collective-permute-done.2.r0 = bf16[32,2048]{1,0:T(8,128)(2,1)S(1)} collective-permute-done((bf16[32,2048]{1,0:T(8,128)(2,1)S(1)}, bf16[32,2048]{1,0:T(8,128)(2,1)S(1)}, u32[]{:S(2)}, u32[]{:S(2)}) %collective-permute-start.2) | collective-permute-done | bytes 131104 | tf_op jit(solution)/shard_map/ppermute | solution.py:77
  18.9 0.0 collective-permute-done.3.r1
  18.9 0.0 copy-start
  19.0 0.0 copy-start.4
  19.0 0.0 copy-start.5
  19.0 0.0 copy-start.6
  19.0 0.0 copy-start.7
  19.0 0.0 copy-start.8
  19.0 0.0 copy-start.9
  19.0 0.0 copy-start.2
  19.0 0.0 copy-start.10
  19.0 0.0 copy-start.11
  19.0 0.0 copy-start.13
  19.1 0.9 %shard_map.130 = (f32[2,128,256]{2,1,0:T(8,128)S(1)}, f32[2,64,256]{2,1,0:T(8,128)S(1)}) custom-call(bf16[32,4096]{1,0:T(8,128)(2,1)S(1)} %copy-done.1, bf16[32,2048]{1,0:T(8,128)(2,1)S(1)} %collective-permute-done.2.r0, bf16[32,2048]{1,0:T(8,128)(2,1)S(1)} %collective-permute-done.3.r1, bf16[32,2304]{1,0:T(8,128)(2,1)S(1)} %collective-permute-done.t0, ...), custom_call_target="tpu_custom_call" | custom-call | flops 226492416 | bytes 4194304 | tf_op jit(solution)/shard_map/pallas_call | solution.py:25
  20.0 0.0 all-to-all-done.group
  20.0 0.0 copy-done
  20.0 0.0 copy-done.4
  20.0 0.0 copy-done.5
  20.0 0.0 copy-done.6
  20.0 0.0 copy-done.7
  20.0 0.0 copy-done.8
  20.0 0.0 copy-done.9
  20.1 1.2 %shard_map.131 = (bf16[2,32,1536]{2,1,0:T(8,128)(2,1)S(1)}, bf16[16,1280]{1,0:T(8,128)(2,1)S(1)}, bf16[16,1280]{1,0:T(8,128)(2,1)S(1)}, f32[96,256]{1,0:T(8,128)S(1)}) custom-call(bf16[16,16,128]{2,1,0:T(8,128)(2,1)S(1)} %all-to-all-done.group, bf16[64,64]{1,0:T(8,128)(2,1)S(1)} %copy-done.4, bf16[64,64]{1,0:T(8,128)(2,1)S(1)} %copy-done.5, ...), custom_call_target="tpu_custom_call" | custom-call | flops 67108864 | bytes 2097152 | tf_op jit(solution)/shard_map/pallas_call | solution.py:25
  21.3 2.7 %collective-permute-start.4 = (bf16[16,1280]{1,0:T(8,128)(2,1)S(1)}, bf16[16,1280]{1,0:T(8,128)(2,1)S(1)}, u32[]{:S(2)}, u32[]{:S(2)}) collective-permute-start(bf16[16,1280]{1,0:T(8,128)(2,1)S(1)} %get-tuple-element.46), channel_id=1, source_target_pairs={{0,1},{1,0},{2,3},{3,2},{4,5},{5,4},{6,7},{7,6},{8,9},{9,8},{10,11... | collective-permute-start | bytes 122888 | tf_op jit(solution)/shard_map/ppermute | solution.py:77
  23.9 0.0 collective-permute-start.5
  23.9 0.0 copy-done.2
  24.0 0.0 copy-done.10
  24.0 0.0 copy-done.11
  24.0 0.0 copy-done.13
  24.0 1.3 %shard_map.132 = (f32[2,128,256]{2,1,0:T(8,128)S(1)}, bf16[6,384,256]{2,1,0:T(8,128)(2,1)S(1)}, bf16[2,32,1024]{2,1,0:T(8,128)(2,1)S(1)}) custom-call(f32[4,128,256]{2,1,0:T(8,128)S(1)} %get-tuple-element.37.acc, f32[4,64,256]{2,1,0:T(8,128)S(1)} %get-tuple-element.38.acc_side, f32[1,64]{1,0:T(1,128)S(1)} %bitcast.5, f32[1,64]{1,0:T(1,128)S(1)} %bitcast.7, ...), custom_call_target="tpu_custom_call" | custom-call | flops 8589934592 | bytes 4194304 | tf_op jit(solution)/shard_map/pallas_call | solution.py:25
  25.3 0.6 %collective-permute-done.4.r0 = bf16[16,1280]{1,0:T(8,128)(2,1)S(1)} collective-permute-done((bf16[16,1280]{1,0:T(8,128)(2,1)S(1)}, bf16[16,1280]{1,0:T(8,128)(2,1)S(1)}, u32[]{:S(2)}, u32[]{:S(2)}) %collective-permute-start.4) | collective-permute-done | bytes 40992 | tf_op jit(solution)/shard_map/ppermute | solution.py:77
  25.9 0.0 collective-permute-done.5.r1
  25.9 1.3 %shard_map.133 = bf16[32,4096]{1,0:T(8,128)(2,1)} custom-call(bf16[2,32,1536]{2,1,0:T(8,128)(2,1)S(1)} %get-tuple-element.45.edges, bf16[16,1280]{1,0:T(8,128)(2,1)S(1)} %collective-permute-done.4.r0, bf16[16,1280]{1,0:T(8,128)(2,1)S(1)} %collective-permute-done.5.r1, s32[32,27]{1,0:T(8,128)S(1)} %copy-done.3, s32[2,8,128]{2,1,0:T(8,128)S(1)} %get-tuple-element.48.slots, ...), custom_call_target="tpu_custom_call" | custom-call | flops 150994944 | bytes 3145728 | tf_op jit(solution)/shard_map/pallas_call | solution.py:25
  (1 shorter events, 0.0 us)
Async XLA Ops:
  2.4 9.5 %collective-permute-start = (bf16[32,2304]{1,0:T(8,128)(2,1)}, bf16[32,2304]{1,0:T(8,128)(2,1)S(1)}, u32[]{:S(2)}, u32[]{:S(2)}) collective-permute-start(bf16[32,2304]{1,0:T(8,128)(2,1)} %get-tuple-element.31), channel_id=1, source_target_pairs={{0,16},{1,2},{2,1},{3,4},{4,3},{5,6},{6,5},{7,8},{8,7},{9,10},{10,... | collective-permute-start | bytes 442376 | tf_op jit(solution)/shard_map/ppermute | solution.py:77
  3.9 8.0 %collective-permute-start.1 = (bf16[32,2304]{1,0:T(8,128)(2,1)}, bf16[32,2304]{1,0:T(8,128)(2,1)S(1)}, u32[]{:S(2)}, u32[]{:S(2)}) collective-permute-start(bf16[32,2304]{1,0:T(8,128)(2,1)} %get-tuple-element.32), channel_id=1, source_target_pairs={{0,1},{1,0},{2,3},{3,2},{4,5},{5,4},{6,7},{7,6},{8,9},{9,8},{10,11... | collective-permute-start | bytes 442376 | tf_op jit(solution)/shard_map/ppermute | solution.py:77
  5.7 14.3 %all-to-all-start = ((bf16[16,16,128]{2,1,0:T(8,128)(2,1)}), bf16[16,16,128]{2,1,0:T(8,128)(2,1)S(1)}, u32[]{:S(2)}, u32[]{:S(2)}) async-start(bf16[16,16,128]{2,1,0:T(8,128)(2,1)} %get-tuple-element.29), calls=%async_computation | async-start | bytes 131072 | tf_op jit(solution)/shard_map/all_to_all | solution.py:704
  11.9 1.0 %copy-start.1 = (bf16[32,4096]{1,0:T(8,128)(2,1)S(1)}, bf16[32,4096]{1,0:T(8,128)(2,1)}, u32[]{:S(2)}) copy-start(bf16[32,4096]{1,0:T(8,128)(2,1)} %get-tuple-element.30.masked) | copy-start | bytes 786436
  12.9 3.5 %copy-start.3 = (s32[32,27]{1,0:T(8,128)S(1)}, s32[32,27]{1,0:T(8,128)}, u32[]{:S(2)}) copy-start(s32[32,27]{1,0:T(8,128)} %get-tuple-element.35.ids_ref) | copy-start | bytes 10372
  12.9 3.5 %copy-start.12 = (bf16[27,64,64]{2,1,0:T(8,128)(2,1)S(1)}, bf16[27,64,64]{2,1,0:T(8,128)(2,1)}, u32[]{:S(2)}) copy-start(bf16[27,64,64]{2,1,0:T(8,128)(2,1)} %weight.2) | copy-start | bytes 663556
  12.9 6.1 %collective-permute-start.2 = (bf16[32,2048]{1,0:T(8,128)(2,1)S(1)}, bf16[32,2048]{1,0:T(8,128)(2,1)S(1)}, u32[]{:S(2)}, u32[]{:S(2)}) collective-permute-start(bf16[32,2048]{1,0:T(8,128)(2,1)S(1)} %get-tuple-element.33), channel_id=1, source_target_pairs={{0,1},{1,0},{2,3},{3,2},{4,5},{5,4},{6,7},{7,6},{8,9},{9,8},{10,11... | collective-permute-start | bytes 393224 | tf_op jit(solution)/shard_map/ppermute | solution.py:77
  16.0 3.0 %collective-permute-start.3 = (bf16[32,2048]{1,0:T(8,128)(2,1)S(1)}, bf16[32,2048]{1,0:T(8,128)(2,1)S(1)}, u32[]{:S(2)}, u32[]{:S(2)}) collective-permute-start(bf16[32,2048]{1,0:T(8,128)(2,1)S(1)} %get-tuple-element.34), channel_id=1, source_target_pairs={{0,16},{1,17},{2,18},{3,19},{4,20},{5,21},{6,22},{7,23},{8,24},{9,... | collective-permute-start | bytes 393224 | tf_op jit(solution)/shard_map/ppermute | solution.py:77
  18.9 1.0 %copy-start = (bf16[32,4096]{1,0:T(8,128)(2,1)S(1)}, bf16[32,4096]{1,0:T(8,128)(2,1)}, u32[]{:S(2)}) copy-start(bf16[32,4096]{1,0:T(8,128)(2,1)} %get-tuple-element.41.cover) | copy-start | bytes 786436
  19.0 1.0 %copy-start.4 = (bf16[64,64]{1,0:T(8,128)(2,1)S(1)}, bf16[64,64]{1,0:T(8,128)(2,1)}, u32[]{:S(2)}) copy-start(bf16[64,64]{1,0:T(8,128)(2,1)} %w_key.1) | copy-start | bytes 24580
  19.0 1.1 %copy-start.5 = (bf16[64,64]{1,0:T(8,128)(2,1)S(1)}, bf16[64,64]{1,0:T(8,128)(2,1)}, u32[]{:S(2)}) copy-start(bf16[64,64]{1,0:T(8,128)(2,1)} %w_value.1) | copy-start | bytes 24580
  19.0 1.1 %copy-start.6 = (bf16[64,64]{1,0:T(8,128)(2,1)S(1)}, bf16[64,64]{1,0:T(8,128)(2,1)}, u32[]{:S(2)}) copy-start(bf16[64,64]{1,0:T(8,128)(2,1)} %w_query.1) | copy-start | bytes 24580
  19.0 1.1 %copy-start.7 = (bf16[64,64]{1,0:T(8,128)(2,1)S(1)}, bf16[64,64]{1,0:T(8,128)(2,1)}, u32[]{:S(2)}) copy-start(bf16[64,64]{1,0:T(8,128)(2,1)} %w_out.1) | copy-start | bytes 24580
  19.0 1.1 %copy-start.8 = (f32[64]{0:T(128)S(1)}, f32[64]{0:T(128)}, u32[]{:S(2)}) copy-start(f32[64]{0:T(128)} %param.18) | copy-start | bytes 772
  19.0 1.1 %copy-start.9 = (f32[64]{0:T(128)S(1)}, f32[64]{0:T(128)}, u32[]{:S(2)}) copy-start(f32[64]{0:T(128)} %param.19) | copy-start | bytes 772
  19.0 4.9 %copy-start.2 = (bf16[32,4096]{1,0:T(8,128)(2,1)S(1)}, bf16[32,4096]{1,0:T(8,128)(2,1)}, u32[]{:S(2)}) copy-start(bf16[32,4096]{1,0:T(8,128)(2,1)} %get-tuple-element.30.masked) | copy-start | bytes 786436
  19.0 4.9 %copy-start.10 = (f32[64]{0:T(128)S(1)}, f32[64]{0:T(128)}, u32[]{:S(2)}) copy-start(f32[64]{0:T(128)} %param.20) | copy-start | bytes 772
  19.0 4.9 %copy-start.11 = (f32[64]{0:T(128)S(1)}, f32[64]{0:T(128)}, u32[]{:S(2)}) copy-start(f32[64]{0:T(128)} %param.21) | copy-start | bytes 772
  19.0 4.9 %copy-start.13 = (bf16[27,64,64]{2,1,0:T(8,128)(2,1)S(1)}, bf16[27,64,64]{2,1,0:T(8,128)(2,1)}, u32[]{:S(2)}) copy-start(bf16[27,64,64]{2,1,0:T(8,128)(2,1)} %weight.3) | copy-start | bytes 663556
  21.3 4.6 %collective-permute-start.4 = (bf16[16,1280]{1,0:T(8,128)(2,1)S(1)}, bf16[16,1280]{1,0:T(8,128)(2,1)S(1)}, u32[]{:S(2)}, u32[]{:S(2)}) collective-permute-start(bf16[16,1280]{1,0:T(8,128)(2,1)S(1)} %get-tuple-element.46), channel_id=1, source_target_pairs={{0,1},{1,0},{2,3},{3,2},{4,5},{5,4},{6,7},{7,6},{8,9},{9,8},{10,11... | collective-permute-start | bytes 122888 | tf_op jit(solution)/shard_map/ppermute | solution.py:77
  23.9 2.0 %collective-permute-start.5 = (bf16[16,1280]{1,0:T(8,128)(2,1)S(1)}, bf16[16,1280]{1,0:T(8,128)(2,1)S(1)}, u32[]{:S(2)}, u32[]{:S(2)}) collective-permute-start(bf16[16,1280]{1,0:T(8,128)(2,1)S(1)} %get-tuple-element.47), channel_id=1, source_target_pairs={{0,16},{1,17},{2,18},{3,19},{4,20},{5,21},{6,22},{7,23},{8,24},{9,... | collective-permute-start | bytes 122888 | tf_op jit(solution)/shard_map/ppermute | solution.py:77

commit v6 on v5

--- a/solution.py
+++ b/solution.py
@@ -147,41 +147,58 @@
 
 
 def prepare_kernel(
-    feat_hbm, occ_hbm, adj_hbm, masked, cover, tokens_all, meta, ids, s0, s1, feat, occ, adj, sems
+    feat_hbm, occ_hbm, adj_hbm,
+    masked_hbm, cover_hbm, tokens_hbm, meta_hbm, ids_hbm, s0_hbm, s1_hbm,
+    masked, cover, tokens_all, meta, ids, s0, s1, feat, occ, adj, in_sems, out_sems,
 ):
-    pairs = ((occ_hbm, occ), (feat_hbm, feat), (adj_hbm, adj))
-    copies = [pltpu.make_async_copy(a, b, sems.at[k]) for k, (a, b) in enumerate(pairs)]
+    planes = [slice(x * 4 * COL, (x + 1) * 4 * COL) for x in range(4)]
+    pairs = [(occ_hbm, occ), (adj_hbm, adj)]
+    pairs += [(feat_hbm.at[:, lanes], feat.at[:, lanes]) for lanes in planes]
+    copies = [pltpu.make_async_copy(a, b, in_sems.at[k]) for k, (a, b) in enumerate(pairs)]
     for copy in copies:
         copy.start()
+    sent = []
+
+    def send(source, target):
+        sent.append(pltpu.make_async_copy(source, target, out_sems.at[len(sent)]))
+        sent[-1].start()
+
     copies[0].wait()
     occupied = occ[...].astype(f32).astype(bf16)
     row = lax.broadcasted_iota(jnp.int32, (64, COL), 0)
     voxel = lax.shift_right_logical(lax.broadcasted_iota(jnp.int32, (64, COL), 1), 6)
-    copies[1].wait()
-    total = jnp.zeros((BRICKS, 128), f32)
     for k in range(16):
-        lanes = slice(k * COL, (k + 1) * COL)
         spread = (row == voxel + 4 * k).astype(f32).astype(bf16)
         cov = jnp.dot(occupied, spread, preferred_element_type=f32).astype(bf16)
-        part = feat[:, lanes] * cov
-        cover[:, lanes] = cov
-        masked[:, lanes] = part
-        wide = part.astype(f32)
-        total = total + wide[:, :128] + wide[:, 128:]
+        cover[:, k * COL : (k + 1) * COL] = cov
+    send(cover, cover_hbm)
+    copies[1].wait()
+    number = adj[...]
+    ids[...] = jnp.where(number < 0, FAR, number)
+    send(ids, ids_hbm)
+    total = jnp.zeros((BRICKS, 128), f32)
+    for x in range(4):
+        copies[2 + x].wait()
+        for y in range(4):
+            lanes = column(x, y)
+            part = feat[:, lanes] * cover[:, lanes]
+            masked[:, lanes] = part
+            wide = part.astype(f32)
+            total = total + wide[:, :128] + wide[:, 128:]
+        send(masked.at[:, planes[x]], masked_hbm.at[:, planes[x]])
     summed = total[:, :C] + total[:, C:]
     tokens = (summed / 8.0).astype(bf16)
     half = BRICKS // 2
     packed = jnp.concatenate([tokens[:half], tokens[half:]], axis=1)
     tokens_all[...] = jnp.broadcast_to(packed[None], tokens_all.shape)
-    copies[2].wait()
-    number = adj[...]
-    ids[...] = jnp.where(number < 0, FAR, number)
+    send(tokens_all, tokens_hbm)
     number = number + 1
     high = lax.shift_right_logical(number, 6).astype(f32).astype(bf16)
     low = jnp.bitwise_and(number, 63).astype(f32).astype(bf16)
     gap = jnp.zeros((BRICKS, C - 27), bf16)
     about = jnp.concatenate([high, gap, low, gap, occupied, tokens], axis=1)
     meta[...] = about
+    send(meta, meta_hbm)
     _, odd_y = parities()
 
     def write(out, near, behind):
@@ -199,6 +216,11 @@
     def _():
         write(s0, 0, 1)
         write(s1, 3, 2)
+
+    send(s0, s0_hbm)
+    send(s1, s1_hbm)
+    for copy in sent:
+        copy.wait()
 
 
 def fill_band(weight, band):
@@ -688,16 +710,19 @@
     side_outer = pltpu.VMEM((2, 3, 2 * BRICKS, TAP), bf16)
     inputs = (features, occupancy, adjacency)
     message = shape(BRICKS, Y_LANES)
+    prepared = [
+        whole, whole, shape(n_sy, BRICKS // 2, 2 * C), shape(BRICKS, 4 * C),
+        shape(BRICKS, 27, dtype=jnp.int32), message, message,
+    ]
     masked, cover, tokens, meta, ids, s0, s1 = call(
         prepare_kernel,
-        [
-            whole, whole, shape(n_sy, BRICKS // 2, 2 * C), shape(BRICKS, 4 * C),
-            shape(BRICKS, 27, dtype=jnp.int32), message, message,
-        ],
+        prepared,
         inputs,
-        [pltpu.VMEM(v.shape, v.dtype) for v in inputs] + [pltpu.SemaphoreType.DMA((3,))],
+        [pltpu.VMEM(v.shape, v.dtype) for v in (*prepared, *inputs)]
+        + [pltpu.SemaphoreType.DMA((6,)), pltpu.SemaphoreType.DMA((10,))],
         bytes_accessed=2 << 20,
         hbm_in=True,
+        hbm_out=True,
     )
     rows = [v.reshape(1, C) for v in (scale_one, shift_one, scale_two, shift_two)]
     t0, t1 = exchange(s0, s1, "sy")

time: 27.6 us -> 27.2 us (0.986)
  Pallas kernels: 9.33 us -> 8.98 us
    pallas_call x7, Pallas kernels: 9.33 us -> 8.98 us  [call(): pl.pallas_call(kernel, out_shape=out_shape, in_specs=[hbm if hbm_in else...]
  transfers between devices with their start and end apart: 7 -> 7, of which waited for: 2 -> 2; matrix products, arithmetic and copies ran while one was open for 0% -> 0% of each run, Pallas kernels for 16% -> 17%
where the time goes in v6:
time: 27.2 us; the launch traced here: 26.9 us
  starting transfers between devices  15.7 us (58%)
  Pallas kernels  8.98 us (33%)
  local copies, waits for them, and re-layouts  1.01 us (4%)
  waiting for transfers between devices  0.96 us (4%)
    ppermute x6, starting transfers between devices, pair_exchange(): return lax.ppermute(value, ('sx', 'sy'), pairs)  9.5 us
    pallas_call x7, Pallas kernels, call(): pl.pallas_call(kernel, out_shape=out_shape, in_specs=[hbm if hbm_in else...  8.98 us
    all_to_all x1, starting transfers between devices, local(): group = lax.all_to_all(tokens, 'sy', 0, 0)  6.17 us
    unnamed x28, local copies, waits for them, and re-layouts  1.01 us
    ppermute x6, waiting for transfers between devices, pair_exchange(): return lax.ppermute(value, ('sx', 'sy'), pairs)  0.95 us
  transfers between devices with their start and end apart: 7, of which 2 were waited for; matrix products, arithmetic and copies ran while one was open for 0% of the time, Pallas kernels for 17%

profile of v6, /device:TPU:1, one launch (start us, length us, event | category | flops | bytes accessed | tf_op | source)
XLA Modules:
  0.0 26.9 jit_solution(8335377881092355822)
XLA Ops:
  0.0 2.0 %shard_map.127 = (bf16[32,4096]{1,0:T(8,128)(2,1)}, bf16[32,4096]{1,0:T(8,128)(2,1)}, bf16[16,16,128]{2,1,0:T(8,128)(2,1)}, bf16[32,256]{1,0:T(8,128)(2,1)}, s32...) custom-call(bf16[32,4096]{1,0:T(8,128)(2,1)} %feat_hbm.1, s32[32,64]{1,0:T(8,128)} %occ_hbm.1, ...), custom_call_target="tpu_custom_call" | custom-call | bytes 2097152 | tf_op jit(solution)/shard_map/pallas_call | solution.py:25
  2.0 1.5 %collective-permute-start = (bf16[32,2304]{1,0:T(8,128)(2,1)}, bf16[32,2304]{1,0:T(8,128)(2,1)S(1)}, u32[]{:S(2)}, u32[]{:S(2)}) collective-permute-start(bf16[32,2304]{1,0:T(8,128)(2,1)} %get-tuple-element.31), channel_id=1, source_target_pairs={{0,16},{1,2},{2,1},{3,4},{4,3},{5,6},{6,5},{7,8},{8,7},{9,10},{10,... | collective-permute-start | bytes 442376 | tf_op jit(solution)/shard_map/ppermute | solution.py:77
  3.5 1.8 %collective-permute-start.1 = (bf16[32,2304]{1,0:T(8,128)(2,1)}, bf16[32,2304]{1,0:T(8,128)(2,1)S(1)}, u32[]{:S(2)}, u32[]{:S(2)}) collective-permute-start(bf16[32,2304]{1,0:T(8,128)(2,1)} %get-tuple-element.32), channel_id=1, source_target_pairs={{0,1},{1,0},{2,3},{3,2},{4,5},{5,4},{6,7},{7,6},{8,9},{9,8},{10,11... | collective-permute-start | bytes 442376 | tf_op jit(solution)/shard_map/ppermute | solution.py:77
  5.4 6.2 %all-to-all-start = ((bf16[16,16,128]{2,1,0:T(8,128)(2,1)}), bf16[16,16,128]{2,1,0:T(8,128)(2,1)S(1)}, u32[]{:S(2)}, u32[]{:S(2)}) async-start(bf16[16,16,128]{2,1,0:T(8,128)(2,1)} %get-tuple-element.29), calls=%async_computation | async-start | bytes 131072 | tf_op jit(solution)/shard_map/all_to_all | solution.py:729
  11.5 0.0 collective-permute-done.t0
  11.5 0.0 collective-permute-done.1.t1
  11.6 0.0 copy-start.1
  11.6 0.9 %copy-done.1 = bf16[32,4096]{1,0:T(8,128)(2,1)S(1)} copy-done((bf16[32,4096]{1,0:T(8,128)(2,1)S(1)}, bf16[32,4096]{1,0:T(8,128)(2,1)}, u32[]{:S(2)}) %copy-start.1) | copy-done | bytes 262168
  12.5 0.0 copy-start.3
  12.5 0.0 copy-start.12
  12.5 3.1 %collective-permute-start.2 = (bf16[32,2048]{1,0:T(8,128)(2,1)S(1)}, bf16[32,2048]{1,0:T(8,128)(2,1)S(1)}, u32[]{:S(2)}, u32[]{:S(2)}) collective-permute-start(bf16[32,2048]{1,0:T(8,128)(2,1)S(1)} %get-tuple-element.33), channel_id=1, source_target_pairs={{0,1},{1,0},{2,3},{3,2},{4,5},{5,4},{6,7},{7,6},{8,9},{9,8},{10,11... | collective-permute-start | bytes 393224 | tf_op jit(solution)/shard_map/ppermute | solution.py:77
  15.6 0.4 %collective-permute-start.3 = (bf16[32,2048]{1,0:T(8,128)(2,1)S(1)}, bf16[32,2048]{1,0:T(8,128)(2,1)S(1)}, u32[]{:S(2)}, u32[]{:S(2)}) collective-permute-start(bf16[32,2048]{1,0:T(8,128)(2,1)S(1)} %get-tuple-element.34), channel_id=1, source_target_pairs={{0,16},{1,17},{2,18},{3,19},{4,20},{5,21},{6,22},{7,23},{8,24},{9,... | collective-permute-start | bytes 393224 | tf_op jit(solution)/shard_map/ppermute | solution.py:77
  16.0 0.0 copy-done.3
  16.1 0.0 copy-done.12
  16.1 2.2 %shard_map.129 = (f32[4,128,256]{2,1,0:T(8,128)S(1)}, f32[4,64,256]{2,1,0:T(8,128)S(1)}, bf16[6,384,256]{2,1,0:T(8,128)(2,1)S(1)}, bf16[4,16,128]{2,1,0:T(8,128)(2,1)S(1)}, s32[2,8,128]{2,1,0:T(8,128)S(1)}) custom-call(bf16[32,4096]{1,0:T(8,128)(2,1)S(1)} %copy-done.1, bf16[32,2304]{1,0:T(8,128)(2,1)S(1)} %collective-permute-done.t0, ...), custom_call_target="tpu_custom_call" | custom-call | flops 8589934592 | bytes 2097152 | tf_op jit(solution)/shard_map/pallas_call | solution.py:25
  18.3 0.3 %collective-permute-done.2.r0 = bf16[32,2048]{1,0:T(8,128)(2,1)S(1)} collective-permute-done((bf16[32,2048]{1,0:T(8,128)(2,1)S(1)}, bf16[32,2048]{1,0:T(8,128)(2,1)S(1)}, u32[]{:S(2)}, u32[]{:S(2)}) %collective-permute-start.2) | collective-permute-done | bytes 131104 | tf_op jit(solution)/shard_map/ppermute | solution.py:77
  18.6 0.0 collective-permute-done.3.r1
  18.6 0.0 copy-start
  18.6 0.0 copy-start.4
  18.6 0.0 copy-start.5
  18.6 0.0 copy-start.6
  18.6 0.0 copy-start.7
  18.6 0.0 copy-start.8
  18.6 0.0 copy-start.9
  18.7 0.0 copy-start.2
  18.7 0.0 copy-start.10
  18.7 0.0 copy-start.11
  18.7 0.0 copy-start.13
  18.7 0.9 %shard_map.130 = (f32[2,128,256]{2,1,0:T(8,128)S(1)}, f32[2,64,256]{2,1,0:T(8,128)S(1)}) custom-call(bf16[32,4096]{1,0:T(8,128)(2,1)S(1)} %copy-done.1, bf16[32,2048]{1,0:T(8,128)(2,1)S(1)} %collective-permute-done.2.r0, bf16[32,2048]{1,0:T(8,128)(2,1)S(1)} %collective-permute-done.3.r1, bf16[32,2304]{1,0:T(8,128)(2,1)S(1)} %collective-permute-done.t0, ...), custom_call_target="tpu_custom_call" | custom-call | flops 226492416 | bytes 4194304 | tf_op jit(solution)/shard_map/pallas_call | solution.py:25
  19.6 0.0 all-to-all-done.group
  19.6 0.0 copy-done
  19.6 0.0 copy-done.4
  19.7 0.0 copy-done.5
  19.7 0.0 copy-done.6
  19.7 0.0 copy-done.7
  19.7 0.0 copy-done.8
  19.7 0.0 copy-done.9
  19.7 1.2 %shard_map.131 = (bf16[2,32,1536]{2,1,0:T(8,128)(2,1)S(1)}, bf16[16,1280]{1,0:T(8,128)(2,1)S(1)}, bf16[16,1280]{1,0:T(8,128)(2,1)S(1)}, f32[96,256]{1,0:T(8,128)S(1)}) custom-call(bf16[16,16,128]{2,1,0:T(8,128)(2,1)S(1)} %all-to-all-done.group, bf16[64,64]{1,0:T(8,128)(2,1)S(1)} %copy-done.4, bf16[64,64]{1,0:T(8,128)(2,1)S(1)} %copy-done.5, ...), custom_call_target="tpu_custom_call" | custom-call | flops 67108864 | bytes 2097152 | tf_op jit(solution)/shard_map/pallas_call | solution.py:25
  20.9 2.7 %collective-permute-start.4 = (bf16[16,1280]{1,0:T(8,128)(2,1)S(1)}, bf16[16,1280]{1,0:T(8,128)(2,1)S(1)}, u32[]{:S(2)}, u32[]{:S(2)}) collective-permute-start(bf16[16,1280]{1,0:T(8,128)(2,1)S(1)} %get-tuple-element.46), channel_id=1, source_target_pairs={{0,1},{1,0},{2,3},{3,2},{4,5},{5,4},{6,7},{7,6},{8,9},{9,8},{10,11... | collective-permute-start | bytes 122888 | tf_op jit(solution)/shard_map/ppermute | solution.py:77
  23.6 0.0 collective-permute-start.5
  23.6 0.0 copy-done.2
  23.6 0.0 copy-done.10
  23.6 0.0 copy-done.11
  23.6 0.0 copy-done.13
  23.6 1.3 %shard_map.132 = (f32[2,128,256]{2,1,0:T(8,128)S(1)}, bf16[6,384,256]{2,1,0:T(8,128)(2,1)S(1)}, bf16[2,32,1024]{2,1,0:T(8,128)(2,1)S(1)}) custom-call(f32[4,128,256]{2,1,0:T(8,128)S(1)} %get-tuple-element.37.acc, f32[4,64,256]{2,1,0:T(8,128)S(1)} %get-tuple-element.38.acc_side, f32[1,64]{1,0:T(1,128)S(1)} %bitcast.5, f32[1,64]{1,0:T(1,128)S(1)} %bitcast.7, ...), custom_call_target="tpu_custom_call" | custom-call | flops 8589934592 | bytes 4194304 | tf_op jit(solution)/shard_map/pallas_call | solution.py:25
  25.0 0.6 %collective-permute-done.4.r0 = bf16[16,1280]{1,0:T(8,128)(2,1)S(1)} collective-permute-done((bf16[16,1280]{1,0:T(8,128)(2,1)S(1)}, bf16[16,1280]{1,0:T(8,128)(2,1)S(1)}, u32[]{:S(2)}, u32[]{:S(2)}) %collective-permute-start.4) | collective-permute-done | bytes 40992 | tf_op jit(solution)/shard_map/ppermute | solution.py:77
  25.6 0.0 collective-permute-done.5.r1
  25.6 1.3 %shard_map.133 = bf16[32,4096]{1,0:T(8,128)(2,1)} custom-call(bf16[2,32,1536]{2,1,0:T(8,128)(2,1)S(1)} %get-tuple-element.45.edges, bf16[16,1280]{1,0:T(8,128)(2,1)S(1)} %collective-permute-done.4.r0, bf16[16,1280]{1,0:T(8,128)(2,1)S(1)} %collective-permute-done.5.r1, s32[32,27]{1,0:T(8,128)S(1)} %copy-done.3, s32[2,8,128]{2,1,0:T(8,128)S(1)} %get-tuple-element.48.slots, ...), custom_call_target="tpu_custom_call" | custom-call | flops 150994944 | bytes 3145728 | tf_op jit(solution)/shard_map/pallas_call | solution.py:25
  (1 shorter events, 0.0 us)
Async XLA Ops:
  2.0 9.5 %collective-permute-start = (bf16[32,2304]{1,0:T(8,128)(2,1)}, bf16[32,2304]{1,0:T(8,128)(2,1)S(1)}, u32[]{:S(2)}, u32[]{:S(2)}) collective-permute-start(bf16[32,2304]{1,0:T(8,128)(2,1)} %get-tuple-element.31), channel_id=1, source_target_pairs={{0,16},{1,2},{2,1},{3,4},{4,3},{5,6},{6,5},{7,8},{8,7},{9,10},{10,... | collective-permute-start | bytes 442376 | tf_op jit(solution)/shard_map/ppermute | solution.py:77
  3.5 8.0 %collective-permute-start.1 = (bf16[32,2304]{1,0:T(8,128)(2,1)}, bf16[32,2304]{1,0:T(8,128)(2,1)S(1)}, u32[]{:S(2)}, u32[]{:S(2)}) collective-permute-start(bf16[32,2304]{1,0:T(8,128)(2,1)} %get-tuple-element.32), channel_id=1, source_target_pairs={{0,1},{1,0},{2,3},{3,2},{4,5},{5,4},{6,7},{7,6},{8,9},{9,8},{10,11... | collective-permute-start | bytes 442376 | tf_op jit(solution)/shard_map/ppermute | solution.py:77
  5.4 14.3 %all-to-all-start = ((bf16[16,16,128]{2,1,0:T(8,128)(2,1)}), bf16[16,16,128]{2,1,0:T(8,128)(2,1)S(1)}, u32[]{:S(2)}, u32[]{:S(2)}) async-start(bf16[16,16,128]{2,1,0:T(8,128)(2,1)} %get-tuple-element.29), calls=%async_computation | async-start | bytes 131072 | tf_op jit(solution)/shard_map/all_to_all | solution.py:729
  11.6 1.0 %copy-start.1 = (bf16[32,4096]{1,0:T(8,128)(2,1)S(1)}, bf16[32,4096]{1,0:T(8,128)(2,1)}, u32[]{:S(2)}) copy-start(bf16[32,4096]{1,0:T(8,128)(2,1)} %get-tuple-element.30.masked) | copy-start | bytes 786436
  12.5 3.5 %copy-start.3 = (s32[32,27]{1,0:T(8,128)S(1)}, s32[32,27]{1,0:T(8,128)}, u32[]{:S(2)}) copy-start(s32[32,27]{1,0:T(8,128)} %get-tuple-element.35.ids_ref) | copy-start | bytes 10372
  12.5 3.5 %copy-start.12 = (bf16[27,64,64]{2,1,0:T(8,128)(2,1)S(1)}, bf16[27,64,64]{2,1,0:T(8,128)(2,1)}, u32[]{:S(2)}) copy-start(bf16[27,64,64]{2,1,0:T(8,128)(2,1)} %weight.2) | copy-start | bytes 663556
  12.5 6.1 %collective-permute-start.2 = (bf16[32,2048]{1,0:T(8,128)(2,1)S(1)}, bf16[32,2048]{1,0:T(8,128)(2,1)S(1)}, u32[]{:S(2)}, u32[]{:S(2)}) collective-permute-start(bf16[32,2048]{1,0:T(8,128)(2,1)S(1)} %get-tuple-element.33), channel_id=1, source_target_pairs={{0,1},{1,0},{2,3},{3,2},{4,5},{5,4},{6,7},{7,6},{8,9},{9,8},{10,11... | collective-permute-start | bytes 393224 | tf_op jit(solution)/shard_map/ppermute | solution.py:77
  15.6 3.0 %collective-permute-start.3 = (bf16[32,2048]{1,0:T(8,128)(2,1)S(1)}, bf16[32,2048]{1,0:T(8,128)(2,1)S(1)}, u32[]{:S(2)}, u32[]{:S(2)}) collective-permute-start(bf16[32,2048]{1,0:T(8,128)(2,1)S(1)} %get-tuple-element.34), channel_id=1, source_target_pairs={{0,16},{1,17},{2,18},{3,19},{4,20},{5,21},{6,22},{7,23},{8,24},{9,... | collective-permute-start | bytes 393224 | tf_op jit(solution)/shard_map/ppermute | solution.py:77
  18.6 1.0 %copy-start = (bf16[32,4096]{1,0:T(8,128)(2,1)S(1)}, bf16[32,4096]{1,0:T(8,128)(2,1)}, u32[]{:S(2)}) copy-start(bf16[32,4096]{1,0:T(8,128)(2,1)} %get-tuple-element.41.cover) | copy-start | bytes 786436
  18.6 1.0 %copy-start.4 = (bf16[64,64]{1,0:T(8,128)(2,1)S(1)}, bf16[64,64]{1,0:T(8,128)(2,1)}, u32[]{:S(2)}) copy-start(bf16[64,64]{1,0:T(8,128)(2,1)} %w_key.1) | copy-start | bytes 24580
  18.6 1.1 %copy-start.5 = (bf16[64,64]{1,0:T(8,128)(2,1)S(1)}, bf16[64,64]{1,0:T(8,128)(2,1)}, u32[]{:S(2)}) copy-start(bf16[64,64]{1,0:T(8,128)(2,1)} %w_value.1) | copy-start | bytes 24580
  18.6 1.1 %copy-start.6 = (bf16[64,64]{1,0:T(8,128)(2,1)S(1)}, bf16[64,64]{1,0:T(8,128)(2,1)}, u32[]{:S(2)}) copy-start(bf16[64,64]{1,0:T(8,128)(2,1)} %w_query.1) | copy-start | bytes 24580
  18.6 1.1 %copy-start.7 = (bf16[64,64]{1,0:T(8,128)(2,1)S(1)}, bf16[64,64]{1,0:T(8,128)(2,1)}, u32[]{:S(2)}) copy-start(bf16[64,64]{1,0:T(8,128)(2,1)} %w_out.1) | copy-start | bytes 24580
  18.6 1.1 %copy-start.8 = (f32[64]{0:T(128)S(1)}, f32[64]{0:T(128)}, u32[]{:S(2)}) copy-start(f32[64]{0:T(128)} %param.18) | copy-start | bytes 772
  18.6 1.0 %copy-start.9 = (f32[64]{0:T(128)S(1)}, f32[64]{0:T(128)}, u32[]{:S(2)}) copy-start(f32[64]{0:T(128)} %param.19) | copy-start | bytes 772
  18.7 4.9 %copy-start.2 = (bf16[32,4096]{1,0:T(8,128)(2,1)S(1)}, bf16[32,4096]{1,0:T(8,128)(2,1)}, u32[]{:S(2)}) copy-start(bf16[32,4096]{1,0:T(8,128)(2,1)} %get-tuple-element.30.masked) | copy-start | bytes 786436
  18.7 4.9 %copy-start.10 = (f32[64]{0:T(128)S(1)}, f32[64]{0:T(128)}, u32[]{:S(2)}) copy-start(f32[64]{0:T(128)} %param.20) | copy-start | bytes 772
  18.7 4.9 %copy-start.11 = (f32[64]{0:T(128)S(1)}, f32[64]{0:T(128)}, u32[]{:S(2)}) copy-start(f32[64]{0:T(128)} %param.21) | copy-start | bytes 772
  18.7 4.9 %copy-start.13 = (bf16[27,64,64]{2,1,0:T(8,128)(2,1)S(1)}, bf16[27,64,64]{2,1,0:T(8,128)(2,1)}, u32[]{:S(2)}) copy-start(bf16[27,64,64]{2,1,0:T(8,128)(2,1)} %weight.3) | copy-start | bytes 663556
  20.9 4.6 %collective-permute-start.4 = (bf16[16,1280]{1,0:T(8,128)(2,1)S(1)}, bf16[16,1280]{1,0:T(8,128)(2,1)S(1)}, u32[]{:S(2)}, u32[]{:S(2)}) collective-permute-start(bf16[16,1280]{1,0:T(8,128)(2,1)S(1)} %get-tuple-element.46), channel_id=1, source_target_pairs={{0,1},{1,0},{2,3},{3,2},{4,5},{5,4},{6,7},{7,6},{8,9},{9,8},{10,11... | collective-permute-start | bytes 122888 | tf_op jit(solution)/shard_map/ppermute | solution.py:77
  23.6 2.0 %collective-permute-start.5 = (bf16[16,1280]{1,0:T(8,128)(2,1)S(1)}, bf16[16,1280]{1,0:T(8,128)(2,1)S(1)}, u32[]{:S(2)}, u32[]{:S(2)}) collective-permute-start(bf16[16,1280]{1,0:T(8,128)(2,1)S(1)} %get-tuple-element.47), channel_id=1, source_target_pairs={{0,16},{1,17},{2,18},{3,19},{4,20},{5,21},{6,22},{7,23},{8,24},{9,... | collective-permute-start | bytes 122888 | tf_op jit(solution)/shard_map/ppermute | solution.py:77

commit v7 on v6

--- a/solution.py
+++ b/solution.py
@@ -453,7 +453,7 @@
 
 
 def near_kernel(
-    masked, t0, t1, ids_ref, weight, acc, acc_side, band_edge, pack, slots, inner, side_inner,
+    masked, t0, t1, ids_ref, weight, acc, acc_side, band_edge, pack, selects, inner, side_inner,
     band,
 ):
     from_message = y_reader(t0, t1)
@@ -482,7 +482,13 @@
         for oy in (-1, 1):
             corner = [(ox, oy, oz) for oz in (-1, 0, 1)]
             parts.append(slot_ids(ids, base + id_step(ox, oy), corner, SIDE_SLOTS))
-        slots[k, :, : FACE_SLOTS + 2 * SIDE_SLOTS] = jnp.concatenate(parts, axis=1)
+        known = jnp.concatenate(parts, axis=1)[:1]
+        for n, oy in enumerate((-1, 0, 1)):
+            candidates = [device_row(base), known[:, :FACE_SLOTS]]
+            if oy:
+                candidates += [device_row(base + id_step(0, oy)), known[:, FACE_SLOTS:]]
+            value = one_hot(ids, [(ox, oy, oz) for oz in (1, -1, 0)], candidates)
+            selects[3 * k + n, :, : value.shape[1]] = value
 
     def store(x_range, value):
         count = len(x_range)
@@ -642,7 +648,7 @@
 
 
 def second_kernel(
-    edges, r0, r1, ids_ref, slots, band_edge, scale, shift, cover, masked, acc, middle, refined,
+    edges, r0, r1, selects, band_edge, scale, shift, cover, masked, acc, middle, refined,
     outer, result, sem,
 ):
     copies = []
@@ -655,8 +661,7 @@
     send(middle.at[0], 1)
     send(middle.at[1], 2)
     odd_x, _ = parities()
-    edge, ids = edge_reader(edges), ids_ref[...]
-    base = device_base()
+    edge = edge_reader(edges)
 
     def received(ox, rows, k):
         lanes = slice(k * COL, (k + 1) * COL)
@@ -667,11 +672,8 @@
         return received(ox, slice(None), 4)
 
     def select_of(ox, oy):
-        known = slots[0 if ox < 0 else 1, :1, : FACE_SLOTS + 2 * SIDE_SLOTS]
-        candidates = [device_row(base), known[:, :FACE_SLOTS]]
-        if oy:
-            candidates += [device_row(base + id_step(0, oy)), known[:, FACE_SLOTS:]]
-        return one_hot(ids, [(ox, oy, oz) for oz in (1, -1, 0)], candidates)
+        width = BRICKS + FACE_SLOTS + (BRICKS + 2 * SIDE_SLOTS if oy else 0)
+        return selects[(0 if ox < 0 else 3) + oy + 1, :, :width]
 
     gather_own(
         edge,
@@ -732,11 +734,11 @@
         message_kernel, [x_message] * 2, (masked, t0, t1), flops=1 << 35, bytes_accessed=1 << 20
     )
     r0, r1 = exchange(x0, x1, "sx")
-    acc, acc_side, band_one, pack, slots = call(
+    acc, acc_side, band_one, pack, selects = call(
         near_kernel,
         [
             own_acc, side_acc, band_edge, shape(4, FACE_SLOTS, 128),
-            shape(2, 8, 128, dtype=jnp.int32),
+            shape(6, 3 * BRICKS, 128),
         ],
         (masked, t0, t1, ids, conv_one),
         [inner, side_inner, band],
@@ -790,7 +792,7 @@
         second_kernel,
         whole,
         (
-            edges, r0, r1, ids, slots, band_two, rows[2], rows[3], cover, masked, acc, half,
+            edges, r0, r1, selects, band_two, rows[2], rows[3], cover, masked, acc, half,
         ),
         [outer, pltpu.VMEM((2, BRICKS, 4 * COL), bf16), pltpu.SemaphoreType.DMA((4,))],
         flops=2 * 256 * 1152 * 256,

time: 27.2 us -> 27.1 us (level)
  no operation moved by 1% of the time
where the time goes in v7:
time: 27.1 us; the launch traced here: 26.8 us
  starting transfers between devices  15.7 us (58%)
  Pallas kernels  8.9 us (33%)
  local copies, waits for them, and re-layouts  1.01 us (4%)
  waiting for transfers between devices  0.97 us (4%)
    ppermute x6, starting transfers between devices, pair_exchange(): return lax.ppermute(value, ('sx', 'sy'), pairs)  9.5 us
    pallas_call x7, Pallas kernels, call(): pl.pallas_call(kernel, out_shape=out_shape, in_specs=[hbm if hbm_in else...  8.9 us
    all_to_all x1, starting transfers between devices, local(): group = lax.all_to_all(tokens, 'sy', 0, 0)  6.17 us
    unnamed x28, local copies, waits for them, and re-layouts  1.01 us
    ppermute x6, waiting for transfers between devices, pair_exchange(): return lax.ppermute(value, ('sx', 'sy'), pairs)  0.97 us
  transfers between devices with their start and end apart: 7, of which 2 were waited for; matrix products, arithmetic and copies ran while one was open for 0% of the time, Pallas kernels for 17%

profile of v7, /device:TPU:1, one launch (start us, length us, event | category | flops | bytes accessed | tf_op | source)
XLA Modules:
  0.0 26.8 jit_solution(12902214114152170904)
XLA Ops:
  0.0 2.0 %shard_map.127 = (bf16[32,4096]{1,0:T(8,128)(2,1)}, bf16[32,4096]{1,0:T(8,128)(2,1)}, bf16[16,16,128]{2,1,0:T(8,128)(2,1)}, bf16[32,256]{1,0:T(8,128)(2,1)}, s32...) custom-call(bf16[32,4096]{1,0:T(8,128)(2,1)} %feat_hbm.1, s32[32,64]{1,0:T(8,128)} %occ_hbm.1, ...), custom_call_target="tpu_custom_call" | custom-call | bytes 2097152 | tf_op jit(solution)/shard_map/pallas_call | solution.py:25
  2.0 1.5 %collective-permute-start = (bf16[32,2304]{1,0:T(8,128)(2,1)}, bf16[32,2304]{1,0:T(8,128)(2,1)S(1)}, u32[]{:S(2)}, u32[]{:S(2)}) collective-permute-start(bf16[32,2304]{1,0:T(8,128)(2,1)} %get-tuple-element.31), channel_id=1, source_target_pairs={{0,16},{1,2},{2,1},{3,4},{4,3},{5,6},{6,5},{7,8},{8,7},{9,10},{10,... | collective-permute-start | bytes 442376 | tf_op jit(solution)/shard_map/ppermute | solution.py:77
  3.5 1.8 %collective-permute-start.1 = (bf16[32,2304]{1,0:T(8,128)(2,1)}, bf16[32,2304]{1,0:T(8,128)(2,1)S(1)}, u32[]{:S(2)}, u32[]{:S(2)}) collective-permute-start(bf16[32,2304]{1,0:T(8,128)(2,1)} %get-tuple-element.32), channel_id=1, source_target_pairs={{0,1},{1,0},{2,3},{3,2},{4,5},{5,4},{6,7},{7,6},{8,9},{9,8},{10,11... | collective-permute-start | bytes 442376 | tf_op jit(solution)/shard_map/ppermute | solution.py:77
  5.4 6.2 %all-to-all-start = ((bf16[16,16,128]{2,1,0:T(8,128)(2,1)}), bf16[16,16,128]{2,1,0:T(8,128)(2,1)S(1)}, u32[]{:S(2)}, u32[]{:S(2)}) async-start(bf16[16,16,128]{2,1,0:T(8,128)(2,1)} %get-tuple-element.29), calls=%async_computation | async-start | bytes 131072 | tf_op jit(solution)/shard_map/all_to_all | solution.py:731
  11.5 0.0 collective-permute-done.t0
  11.5 0.0 collective-permute-done.1.t1
  11.6 0.0 copy-start.1
  11.6 0.9 %copy-done.1 = bf16[32,4096]{1,0:T(8,128)(2,1)S(1)} copy-done((bf16[32,4096]{1,0:T(8,128)(2,1)S(1)}, bf16[32,4096]{1,0:T(8,128)(2,1)}, u32[]{:S(2)}) %copy-start.1) | copy-done | bytes 262168
  12.5 0.0 copy-start.7
  12.5 0.0 copy-start.12
  12.5 3.1 %collective-permute-start.2 = (bf16[32,2048]{1,0:T(8,128)(2,1)S(1)}, bf16[32,2048]{1,0:T(8,128)(2,1)S(1)}, u32[]{:S(2)}, u32[]{:S(2)}) collective-permute-start(bf16[32,2048]{1,0:T(8,128)(2,1)S(1)} %get-tuple-element.33), channel_id=1, source_target_pairs={{0,1},{1,0},{2,3},{3,2},{4,5},{5,4},{6,7},{7,6},{8,9},{9,8},{10,11... | collective-permute-start | bytes 393224 | tf_op jit(solution)/shard_map/ppermute | solution.py:77
  15.6 0.4 %collective-permute-start.3 = (bf16[32,2048]{1,0:T(8,128)(2,1)S(1)}, bf16[32,2048]{1,0:T(8,128)(2,1)S(1)}, u32[]{:S(2)}, u32[]{:S(2)}) collective-permute-start(bf16[32,2048]{1,0:T(8,128)(2,1)S(1)} %get-tuple-element.34), channel_id=1, source_target_pairs={{0,16},{1,17},{2,18},{3,19},{4,20},{5,21},{6,22},{7,23},{8,24},{9,... | collective-permute-start | bytes 393224 | tf_op jit(solution)/shard_map/ppermute | solution.py:77
  16.0 0.0 copy-done.7
  16.1 0.0 copy-done.12
  16.1 2.2 %shard_map.129 = (f32[4,128,256]{2,1,0:T(8,128)S(1)}, f32[4,64,256]{2,1,0:T(8,128)S(1)}, bf16[6,384,256]{2,1,0:T(8,128)(2,1)S(1)}, bf16[4,16,128]{2,1,0:T(8,128)(2,1)S(1)}, bf16[6,96,128]{2,1,0:T(8,128)(2,1)S(1)}) custom-call(bf16[32,4096]{1,0:T(8,128)(2,1)S(1)} %copy-done.1, bf16[32,2304]{1,0:T(8,128)(2,1)S(1)} %collective-permute-done.t0, ...), custom_call_target="tpu_custom_call" | custom-call | flops 8589934592 | bytes 2097152 | tf_op jit(solution)/shard_map/pallas_call | solution.py:25
  18.2 0.4 %collective-permute-done.2.r0 = bf16[32,2048]{1,0:T(8,128)(2,1)S(1)} collective-permute-done((bf16[32,2048]{1,0:T(8,128)(2,1)S(1)}, bf16[32,2048]{1,0:T(8,128)(2,1)S(1)}, u32[]{:S(2)}, u32[]{:S(2)}) %collective-permute-start.2) | collective-permute-done | bytes 131104 | tf_op jit(solution)/shard_map/ppermute | solution.py:77
  18.6 0.0 collective-permute-done.3.r1
  18.6 0.0 copy-start
  18.6 0.0 copy-start.3
  18.6 0.0 copy-start.4
  18.6 0.0 copy-start.5
  18.6 0.0 copy-start.6
  18.6 0.0 copy-start.8
  18.6 0.0 copy-start.9
  18.7 0.0 copy-start.2
  18.7 0.0 copy-start.10
  18.7 0.0 copy-start.11
  18.7 0.0 copy-start.13
  18.7 0.9 %shard_map.130 = (f32[2,128,256]{2,1,0:T(8,128)S(1)}, f32[2,64,256]{2,1,0:T(8,128)S(1)}) custom-call(bf16[32,4096]{1,0:T(8,128)(2,1)S(1)} %copy-done.1, bf16[32,2048]{1,0:T(8,128)(2,1)S(1)} %collective-permute-done.2.r0, bf16[32,2048]{1,0:T(8,128)(2,1)S(1)} %collective-permute-done.3.r1, bf16[32,2304]{1,0:T(8,128)(2,1)S(1)} %collective-permute-done.t0, ...), custom_call_target="tpu_custom_call" | custom-call | flops 226492416 | bytes 4194304 | tf_op jit(solution)/shard_map/pallas_call | solution.py:25
  19.6 0.0 all-to-all-done.group
  19.6 0.0 copy-done
  19.6 0.0 copy-done.3
  19.7 0.0 copy-done.4
  19.7 0.0 copy-done.5
  19.7 0.0 copy-done.6
  19.7 0.0 copy-done.8
  19.7 0.0 copy-done.9
  19.7 1.2 %shard_map.131 = (bf16[2,32,1536]{2,1,0:T(8,128)(2,1)S(1)}, bf16[16,1280]{1,0:T(8,128)(2,1)S(1)}, bf16[16,1280]{1,0:T(8,128)(2,1)S(1)}, f32[96,256]{1,0:T(8,128)S(1)}) custom-call(bf16[16,16,128]{2,1,0:T(8,128)(2,1)S(1)} %all-to-all-done.group, bf16[64,64]{1,0:T(8,128)(2,1)S(1)} %copy-done.3, bf16[64,64]{1,0:T(8,128)(2,1)S(1)} %copy-done.4, ...), custom_call_target="tpu_custom_call" | custom-call | flops 67108864 | bytes 2097152 | tf_op jit(solution)/shard_map/pallas_call | solution.py:25
  20.9 2.7 %collective-permute-start.4 = (bf16[16,1280]{1,0:T(8,128)(2,1)S(1)}, bf16[16,1280]{1,0:T(8,128)(2,1)S(1)}, u32[]{:S(2)}, u32[]{:S(2)}) collective-permute-start(bf16[16,1280]{1,0:T(8,128)(2,1)S(1)} %get-tuple-element.46), channel_id=1, source_target_pairs={{0,1},{1,0},{2,3},{3,2},{4,5},{5,4},{6,7},{7,6},{8,9},{9,8},{10,11... | collective-permute-start | bytes 122888 | tf_op jit(solution)/shard_map/ppermute | solution.py:77
  23.6 0.0 collective-permute-start.5
  23.6 0.0 copy-done.2
  23.6 0.0 copy-done.10
  23.6 0.0 copy-done.11
  23.6 0.0 copy-done.13
  23.6 1.3 %shard_map.132 = (f32[2,128,256]{2,1,0:T(8,128)S(1)}, bf16[6,384,256]{2,1,0:T(8,128)(2,1)S(1)}, bf16[2,32,1024]{2,1,0:T(8,128)(2,1)S(1)}) custom-call(f32[4,128,256]{2,1,0:T(8,128)S(1)} %get-tuple-element.37.acc, f32[4,64,256]{2,1,0:T(8,128)S(1)} %get-tuple-element.38.acc_side, f32[1,64]{1,0:T(1,128)S(1)} %bitcast.5, f32[1,64]{1,0:T(1,128)S(1)} %bitcast.7, ...), custom_call_target="tpu_custom_call" | custom-call | flops 8589934592 | bytes 4194304 | tf_op jit(solution)/shard_map/pallas_call | solution.py:25
  25.0 0.6 %collective-permute-done.4.r0 = bf16[16,1280]{1,0:T(8,128)(2,1)S(1)} collective-permute-done((bf16[16,1280]{1,0:T(8,128)(2,1)S(1)}, bf16[16,1280]{1,0:T(8,128)(2,1)S(1)}, u32[]{:S(2)}, u32[]{:S(2)}) %collective-permute-start.4) | collective-permute-done | bytes 40992 | tf_op jit(solution)/shard_map/ppermute | solution.py:77
  25.6 0.0 collective-permute-done.5.r1
  25.6 1.2 %shard_map.133 = bf16[32,4096]{1,0:T(8,128)(2,1)} custom-call(bf16[2,32,1536]{2,1,0:T(8,128)(2,1)S(1)} %get-tuple-element.45.edges, bf16[16,1280]{1,0:T(8,128)(2,1)S(1)} %collective-permute-done.4.r0, bf16[16,1280]{1,0:T(8,128)(2,1)S(1)} %collective-permute-done.5.r1, bf16[6,96,128]{2,1,0:T(8,128)(2,1)S(1)} %get-tuple-element.48.selects, ...), custom_call_target="tpu_custom_call" | custom-call | flops 150994944 | bytes 3145728 | tf_op jit(solution)/shard_map/pallas_call | solution.py:25
  (1 shorter events, 0.0 us)
Async XLA Ops:
  2.0 9.5 %collective-permute-start = (bf16[32,2304]{1,0:T(8,128)(2,1)}, bf16[32,2304]{1,0:T(8,128)(2,1)S(1)}, u32[]{:S(2)}, u32[]{:S(2)}) collective-permute-start(bf16[32,2304]{1,0:T(8,128)(2,1)} %get-tuple-element.31), channel_id=1, source_target_pairs={{0,16},{1,2},{2,1},{3,4},{4,3},{5,6},{6,5},{7,8},{8,7},{9,10},{10,... | collective-permute-start | bytes 442376 | tf_op jit(solution)/shard_map/ppermute | solution.py:77
  3.5 8.0 %collective-permute-start.1 = (bf16[32,2304]{1,0:T(8,128)(2,1)}, bf16[32,2304]{1,0:T(8,128)(2,1)S(1)}, u32[]{:S(2)}, u32[]{:S(2)}) collective-permute-start(bf16[32,2304]{1,0:T(8,128)(2,1)} %get-tuple-element.32), channel_id=1, source_target_pairs={{0,1},{1,0},{2,3},{3,2},{4,5},{5,4},{6,7},{7,6},{8,9},{9,8},{10,11... | collective-permute-start | bytes 442376 | tf_op jit(solution)/shard_map/ppermute | solution.py:77
  5.4 14.3 %all-to-all-start = ((bf16[16,16,128]{2,1,0:T(8,128)(2,1)}), bf16[16,16,128]{2,1,0:T(8,128)(2,1)S(1)}, u32[]{:S(2)}, u32[]{:S(2)}) async-start(bf16[16,16,128]{2,1,0:T(8,128)(2,1)} %get-tuple-element.29), calls=%async_computation | async-start | bytes 131072 | tf_op jit(solution)/shard_map/all_to_all | solution.py:731
  11.6 1.0 %copy-start.1 = (bf16[32,4096]{1,0:T(8,128)(2,1)S(1)}, bf16[32,4096]{1,0:T(8,128)(2,1)}, u32[]{:S(2)}) copy-start(bf16[32,4096]{1,0:T(8,128)(2,1)} %get-tuple-element.30.masked) | copy-start | bytes 786436
  12.5 3.5 %copy-start.7 = (s32[32,27]{1,0:T(8,128)S(1)}, s32[32,27]{1,0:T(8,128)}, u32[]{:S(2)}) copy-start(s32[32,27]{1,0:T(8,128)} %get-tuple-element.35.ids_ref) | copy-start | bytes 10372
  12.5 3.5 %copy-start.12 = (bf16[27,64,64]{2,1,0:T(8,128)(2,1)S(1)}, bf16[27,64,64]{2,1,0:T(8,128)(2,1)}, u32[]{:S(2)}) copy-start(bf16[27,64,64]{2,1,0:T(8,128)(2,1)} %weight.2) | copy-start | bytes 663556
  12.5 6.1 %collective-permute-start.2 = (bf16[32,2048]{1,0:T(8,128)(2,1)S(1)}, bf16[32,2048]{1,0:T(8,128)(2,1)S(1)}, u32[]{:S(2)}, u32[]{:S(2)}) collective-permute-start(bf16[32,2048]{1,0:T(8,128)(2,1)S(1)} %get-tuple-element.33), channel_id=1, source_target_pairs={{0,1},{1,0},{2,3},{3,2},{4,5},{5,4},{6,7},{7,6},{8,9},{9,8},{10,11... | collective-permute-start | bytes 393224 | tf_op jit(solution)/shard_map/ppermute | solution.py:77
  15.6 3.0 %collective-permute-start.3 = (bf16[32,2048]{1,0:T(8,128)(2,1)S(1)}, bf16[32,2048]{1,0:T(8,128)(2,1)S(1)}, u32[]{:S(2)}, u32[]{:S(2)}) collective-permute-start(bf16[32,2048]{1,0:T(8,128)(2,1)S(1)} %get-tuple-element.34), channel_id=1, source_target_pairs={{0,16},{1,17},{2,18},{3,19},{4,20},{5,21},{6,22},{7,23},{8,24},{9,... | collective-permute-start | bytes 393224 | tf_op jit(solution)/shard_map/ppermute | solution.py:77
  18.6 1.0 %copy-start = (bf16[32,4096]{1,0:T(8,128)(2,1)S(1)}, bf16[32,4096]{1,0:T(8,128)(2,1)}, u32[]{:S(2)}) copy-start(bf16[32,4096]{1,0:T(8,128)(2,1)} %get-tuple-element.41.cover) | copy-start | bytes 786436
  18.6 1.0 %copy-start.3 = (bf16[64,64]{1,0:T(8,128)(2,1)S(1)}, bf16[64,64]{1,0:T(8,128)(2,1)}, u32[]{:S(2)}) copy-start(bf16[64,64]{1,0:T(8,128)(2,1)} %w_key.1) | copy-start | bytes 24580
  18.6 1.1 %copy-start.4 = (bf16[64,64]{1,0:T(8,128)(2,1)S(1)}, bf16[64,64]{1,0:T(8,128)(2,1)}, u32[]{:S(2)}) copy-start(bf16[64,64]{1,0:T(8,128)(2,1)} %w_value.1) | copy-start | bytes 24580
  18.6 1.1 %copy-start.5 = (bf16[64,64]{1,0:T(8,128)(2,1)S(1)}, bf16[64,64]{1,0:T(8,128)(2,1)}, u32[]{:S(2)}) copy-start(bf16[64,64]{1,0:T(8,128)(2,1)} %w_query.1) | copy-start | bytes 24580
  18.6 1.1 %copy-start.6 = (bf16[64,64]{1,0:T(8,128)(2,1)S(1)}, bf16[64,64]{1,0:T(8,128)(2,1)}, u32[]{:S(2)}) copy-start(bf16[64,64]{1,0:T(8,128)(2,1)} %w_out.1) | copy-start | bytes 24580
  18.6 1.1 %copy-start.8 = (f32[64]{0:T(128)S(1)}, f32[64]{0:T(128)}, u32[]{:S(2)}) copy-start(f32[64]{0:T(128)} %param.18) | copy-start | bytes 772
  18.6 1.0 %copy-start.9 = (f32[64]{0:T(128)S(1)}, f32[64]{0:T(128)}, u32[]{:S(2)}) copy-start(f32[64]{0:T(128)} %param.19) | copy-start | bytes 772
  18.7 4.9 %copy-start.2 = (bf16[32,4096]{1,0:T(8,128)(2,1)S(1)}, bf16[32,4096]{1,0:T(8,128)(2,1)}, u32[]{:S(2)}) copy-start(bf16[32,4096]{1,0:T(8,128)(2,1)} %get-tuple-element.30.masked) | copy-start | bytes 786436
  18.7 4.9 %copy-start.10 = (f32[64]{0:T(128)S(1)}, f32[64]{0:T(128)}, u32[]{:S(2)}) copy-start(f32[64]{0:T(128)} %param.20) | copy-start | bytes 772
  18.7 4.9 %copy-start.11 = (f32[64]{0:T(128)S(1)}, f32[64]{0:T(128)}, u32[]{:S(2)}) copy-start(f32[64]{0:T(128)} %param.21) | copy-start | bytes 772
  18.7 4.9 %copy-start.13 = (bf16[27,64,64]{2,1,0:T(8,128)(2,1)S(1)}, bf16[27,64,64]{2,1,0:T(8,128)(2,1)}, u32[]{:S(2)}) copy-start(bf16[27,64,64]{2,1,0:T(8,128)(2,1)} %weight.3) | copy-start | bytes 663556
  20.9 4.6 %collective-permute-start.4 = (bf16[16,1280]{1,0:T(8,128)(2,1)S(1)}, bf16[16,1280]{1,0:T(8,128)(2,1)S(1)}, u32[]{:S(2)}, u32[]{:S(2)}) collective-permute-start(bf16[16,1280]{1,0:T(8,128)(2,1)S(1)} %get-tuple-element.46), channel_id=1, source_target_pairs={{0,1},{1,0},{2,3},{3,2},{4,5},{5,4},{6,7},{7,6},{8,9},{9,8},{10,11... | collective-permute-start | bytes 122888 | tf_op jit(solution)/shard_map/ppermute | solution.py:77
  23.6 2.0 %collective-permute-start.5 = (bf16[16,1280]{1,0:T(8,128)(2,1)S(1)}, bf16[16,1280]{1,0:T(8,128)(2,1)S(1)}, u32[]{:S(2)}, u32[]{:S(2)}) collective-permute-start(bf16[16,1280]{1,0:T(8,128)(2,1)S(1)} %get-tuple-element.47), channel_id=1, source_target_pairs={{0,16},{1,17},{2,18},{3,19},{4,20},{5,21},{6,22},{7,23},{8,24},{9,... | collective-permute-start | bytes 122888 | tf_op jit(solution)/shard_map/ppermute | solution.py:77
